TPU v7x, 32 devices: a whole 2x2x4 slice. The times are simulated.
32 devices in a mesh: expert: 16 (over z, y, x), tensor: 2 (over core).
Axes of the slice: x: 2, y: 2, z: 4, core: 2. Of those that a mesh axis runs over, the one named last changes fastest.
Arguments:
- hidden_in: bfloat16 [8192, 1536], P('expert'), may hold values from -6 to 6
- attn_gain: float32 [1536], replicated, may hold values from 0.5 to 1.5
- w_query: bfloat16 [1536, 1536], P(None, 'tensor'), may hold values from -0.15625 to 0.15625
- w_key: bfloat16 [1536, 256], P(None, 'tensor'), may hold values from -0.15625 to 0.15625
- w_value: bfloat16 [1536, 256], P(None, 'tensor'), may hold values from -0.15625 to 0.15625
- w_output: bfloat16 [1536, 1536], P('tensor'), may hold values from -0.625 to 0.625
- moe_gain: float32 [1536], replicated, may hold values from 0.5 to 1.5
- w_gate: bfloat16 [16, 1536, 768], P('expert', None, 'tensor'), may hold values from -0.15625 to 0.15625
- w_up: bfloat16 [16, 1536, 768], P('expert', None, 'tensor'), may hold values from -0.15625 to 0.15625
- w_down: bfloat16 [16, 768, 1536], P('expert', 'tensor'), may hold values from -0.4375 to 0.4375
- gate_logits: float32 [8192, 4], P('expert'), may hold values from -3 to 3
- routes: int32 [8192, 4], P('expert'), may hold values from 0 to 15, all different within a row; in each aligned block of 512 rows (0 to 511, 512 to 1023, ...) at most 256 rows name the same one
- out_grad: bfloat16 [8192, 1536], P('expert'), may hold values from -6 to 6
Outputs:
- block_out: bfloat16 [8192, 1536], P('expert')
- grad_in: float32 [8192, 1536], P('expert')
- grad_attn_gain: float32 [1536], replicated
- grad_query: float32 [1536, 1536], P(None, 'tensor')
- grad_key: float32 [1536, 256], P(None, 'tensor')
- grad_value: float32 [1536, 256], P(None, 'tensor')
- grad_output: float32 [1536, 1536], P('tensor')
- grad_moe_gain: float32 [1536], replicated
- grad_gate: float32 [16, 1536, 768], P('expert', None, 'tensor')
- grad_up: float32 [16, 1536, 768], P('expert', None, 'tensor')
- grad_down: float32 [16, 768, 1536], P('expert', 'tensor')
Inputs may be any that keep to these rules, and one draw needn't show every extreme that they name: `routes`: A row names 4 different experts. Among the 512 rows of one sequence, no expert is named by more than 256 rows, a bound that some block reaches.
All inputs are finite; a program needn't handle non-finite values.
Results may differ from a plain program's by a relative error of at most 0.018.
Values may be sent and summed in bfloat16 or wider, within the bound.
No kernel may reach another device: no remote copies, remote signals or barrier semaphores. Data moves between devices by JAX's collectives and lax.ppermute only.
A program may use at most 256 MiB of HBM per device.

v0:
```python
import math

import jax
import jax.numpy as jnp
from jax import lax
from jax.sharding import PartitionSpec as P

HD = 128


epsilon = 1e-06
rope_base = 10000.0
masked_score = -1e30


def rotate(values, places, sign):
    halfway = values.shape[-1] // 2
    frequency = rope_base ** (-jnp.arange(halfway, dtype=jnp.float32) / halfway)
    angles = places.astype(jnp.float32)[:, None] * frequency[None, :]
    cosine = jnp.cos(angles)[:, None, :]
    sine = sign * jnp.sin(angles)[:, None, :]
    first = values[..., :halfway]
    second = values[..., halfway:]
    return jnp.concatenate(
        [first * cosine - second * sine, second * cosine + first * sine], axis=-1
    )


def contract_rows(left, right):
    return lax.dot_general(
        left, right, (((0,), (0,)), ((), ())), preferred_element_type=jnp.float32
    )


def contract_cols(left, right):
    return lax.dot_general(
        left, right, (((1,), (1,)), ((), ())), preferred_element_type=jnp.float32
    )


def block_scores(query_block, keys_used, row_start, scale_factor):
    query_rows = query_block.shape[0]
    key_rows = keys_used.shape[0]
    raw_scores = (
        jnp.einsum("qcgd,kcd->cgqk", query_block, keys_used, preferred_element_type=jnp.float32)
        * scale_factor
    )
    row_ids = row_start + jnp.arange(query_rows)
    causal = jnp.arange(key_rows)[None, :] <= row_ids[:, None]
    return jnp.where(causal, raw_scores, masked_score)


def on_device(
    hidden_in,
    attn_gain,
    w_query,
    w_key,
    w_value,
    w_output,
    moe_gain,
    w_gate,
    w_up,
    w_down,
    gate_logits,
    routes,
    out_grad,
):
    tokens, model_width = hidden_in.shape
    experts = lax.axis_size("expert")
    tensor_ranks = lax.axis_size("tensor")
    tensor_rank = lax.axis_index("tensor")
    route_width = routes.shape[1]
    route_count = tokens * route_width
    capacity = 2 * route_count // experts
    half_slots = capacity // tensor_ranks
    heads_local = w_query.shape[1] // HD
    kv_local = w_key.shape[1] // HD
    groups = heads_local // kv_local
    scale_factor = 1.0 / math.sqrt(HD)
    block_rows = min(512, tokens)
    places = jnp.arange(tokens, dtype=jnp.int32)
    flat_routes = routes.reshape(-1)
    route_hits = (flat_routes[:, None] == jnp.arange(experts, dtype=jnp.int32)[None, :]).astype(
        jnp.int32
    )
    slot_index = jnp.sum(jnp.cumsum(route_hits, axis=0) * route_hits, axis=1) - 1
    which_route = (
        jnp.full((experts * capacity,), route_count, jnp.int32)
        .at[flat_routes * capacity + slot_index]
        .set(jnp.arange(route_count, dtype=jnp.int32))
    )
    which_token = which_route // route_width
    own_half = slot_index // half_slots == tensor_rank
    back_index = jnp.where(
        own_half, flat_routes * half_slots + slot_index % half_slots, experts * half_slots
    )
    gate_weights = jax.nn.softmax(gate_logits, axis=-1)
    full_gate, full_up, full_down = (w_gate[0], w_up[0], w_down[0])

    def deliver(buffer):
        arrived_all = lax.all_to_all(buffer, "expert", split_axis=0, concat_axis=0, tiled=True)
        return arrived_all.reshape(experts * capacity, model_width)

    def give_back(partial_value):
        summed_rows = lax.psum_scatter(
            partial_value.reshape(experts, capacity, model_width).astype(jnp.bfloat16),
            "tensor",
            scatter_dimension=1,
            tiled=True,
        )
        returned = lax.all_to_all(summed_rows, "expert", split_axis=0, concat_axis=0, tiled=True)
        return jnp.concatenate(
            [
                returned.reshape(experts * half_slots, model_width),
                jnp.zeros((1, model_width), jnp.bfloat16),
            ],
            axis=0,
        )

    def collect(returned, weights):
        picked = returned[back_index].astype(jnp.float32).reshape(tokens, route_width, model_width)
        return lax.psum(
            jnp.sum(picked * weights[:, :, None], axis=1).astype(jnp.bfloat16), "tensor"
        ).astype(jnp.float32)

    source = hidden_in.astype(jnp.float32)
    scale_one = lax.rsqrt(jnp.mean(source * source, axis=-1, keepdims=True) + epsilon)
    unit_one = source * scale_one
    normed = (unit_one * attn_gain).astype(jnp.bfloat16)
    query_pre = jnp.dot(normed, w_query, preferred_element_type=jnp.float32).reshape(
        tokens, heads_local, HD
    )
    queries = (
        rotate(query_pre, places, 1.0).astype(jnp.bfloat16).reshape(tokens, kv_local, groups, HD)
    )
    key_pre = jnp.dot(normed, w_key, preferred_element_type=jnp.float32).reshape(
        tokens, kv_local, HD
    )
    keys_used = rotate(key_pre, places, 1.0).astype(jnp.bfloat16)
    values_used = (
        jnp.dot(normed, w_value, preferred_element_type=jnp.float32)
        .astype(jnp.bfloat16)
        .reshape(tokens, kv_local, HD)
    )
    row_start = 0
    query_block = queries
    raw_scores = block_scores(query_block, keys_used, row_start, scale_factor)
    biggest = jnp.max(raw_scores, axis=-1, keepdims=True)
    exponent = jnp.exp(raw_scores - biggest)
    row_total = jnp.sum(exponent, axis=-1, keepdims=True)
    weights_low = (exponent / row_total).astype(jnp.bfloat16)
    logsums = [biggest + jnp.log(row_total)]
    attended = jnp.einsum(
        "cgqk,kcd->qcgd", weights_low, values_used, preferred_element_type=jnp.float32
    )
    mixed_blocks = attended.reshape(block_rows, heads_local * HD).astype(jnp.bfloat16)
    attn_part = jnp.dot(mixed_blocks, w_output, preferred_element_type=jnp.float32)
    middle = source + lax.psum(attn_part.astype(jnp.bfloat16), "tensor").astype(jnp.float32)
    scale_two = lax.rsqrt(jnp.mean(middle * middle, axis=-1, keepdims=True) + epsilon)
    unit_two = middle * scale_two
    rows_in = (unit_two * moe_gain).astype(jnp.bfloat16)
    padded_rows = jnp.concatenate([rows_in, jnp.zeros((1, model_width), jnp.bfloat16)], axis=0)
    arrived = deliver(padded_rows[which_token].reshape(experts, capacity, model_width))
    gate_pre = jnp.dot(arrived, full_gate, preferred_element_type=jnp.float32)
    up_pre = jnp.dot(arrived, full_up, preferred_element_type=jnp.float32)
    sigmoid = jax.nn.sigmoid(gate_pre)
    activated = gate_pre * sigmoid
    hidden_units = (activated * up_pre).astype(jnp.bfloat16)
    produced = jnp.dot(hidden_units, full_down, preferred_element_type=jnp.float32)
    moe_result = collect(give_back(produced), gate_weights)
    block_out = (middle + moe_result).astype(jnp.bfloat16)
    grad_out = out_grad.astype(jnp.float32)
    route_grads = (
        (gate_weights[:, :, None] * grad_out[:, None, :])
        .astype(jnp.bfloat16)
        .reshape(route_count, model_width)
    )
    padded_grads = jnp.concatenate([route_grads, jnp.zeros((1, model_width), jnp.bfloat16)], axis=0)
    grad_arrived = deliver(padded_grads[which_route].reshape(experts, capacity, model_width))
    grad_down = contract_rows(hidden_units, grad_arrived)
    grad_inner = contract_cols(grad_arrived, full_down)
    grad_gate_pre = (grad_inner * up_pre * sigmoid * (1.0 + gate_pre * (1.0 - sigmoid))).astype(
        jnp.bfloat16
    )
    grad_up_pre = (grad_inner * activated).astype(jnp.bfloat16)
    grad_gate = contract_rows(arrived, grad_gate_pre)
    grad_up = contract_rows(arrived, grad_up_pre)
    grad_arrived_rows = contract_cols(grad_gate_pre, full_gate) + contract_cols(
        grad_up_pre, full_up
    )
    grad_rows = collect(give_back(grad_arrived_rows), jnp.ones_like(gate_weights))
    grad_unit_two = grad_rows * moe_gain
    grad_moe_gain = jnp.sum(grad_rows * unit_two, axis=0)
    grad_middle = grad_out + scale_two * (
        grad_unit_two - unit_two * jnp.mean(grad_unit_two * unit_two, axis=-1, keepdims=True)
    )
    grad_attn = grad_middle.astype(jnp.bfloat16)
    grad_output = contract_rows(mixed_blocks, grad_attn)
    grad_mixed = (
        contract_cols(grad_attn, w_output)
        .astype(jnp.bfloat16)
        .reshape(tokens, kv_local, groups, HD)
    )
    grad_query_blocks = []
    grad_keys = jnp.zeros((tokens, kv_local, HD), jnp.float32)
    grad_values = jnp.zeros((tokens, kv_local, HD), jnp.float32)
    for block_number, row_start in enumerate(range(0, tokens, block_rows)):
        query_block = queries
        raw_scores = block_scores(query_block, keys_used, row_start, scale_factor)
        probs = jnp.exp(raw_scores - logsums[block_number])
        probs_low = probs.astype(jnp.bfloat16)
        grad_probs = jnp.einsum(
            "qcgd,kcd->cgqk", grad_mixed, values_used, preferred_element_type=jnp.float32
        )
        delta = jnp.sum(probs * grad_probs, axis=-1, keepdims=True)
        grad_scores = (probs * (grad_probs - delta)).astype(jnp.bfloat16)
        grad_query_blocks.append(
            jnp.einsum("cgqk,kcd->qcgd", grad_scores, keys_used, preferred_element_type=jnp.float32)
            * scale_factor
        )
        grad_keys = (
            jnp.einsum(
                "cgqk,qcgd->kcd", grad_scores, query_block, preferred_element_type=jnp.float32
            )
            * scale_factor
        )
        grad_values = jnp.einsum(
            "cgqk,qcgd->kcd", probs_low, grad_mixed, preferred_element_type=jnp.float32
        )
    grad_queries = grad_query_blocks[0].reshape(tokens, heads_local, HD)
    grad_query_pre = (
        rotate(grad_queries, places, -1.0).astype(jnp.bfloat16).reshape(tokens, heads_local * HD)
    )
    grad_key_pre = (
        rotate(grad_keys, places, -1.0).astype(jnp.bfloat16).reshape(tokens, kv_local * HD)
    )
    grad_value_pre = grad_values.astype(jnp.bfloat16).reshape(tokens, kv_local * HD)
    grad_query = contract_rows(normed, grad_query_pre)
    grad_key = contract_rows(normed, grad_key_pre)
    grad_value = contract_rows(normed, grad_value_pre)
    grad_normed_part = (
        contract_cols(grad_query_pre, w_query)
        + contract_cols(grad_key_pre, w_key)
        + contract_cols(grad_value_pre, w_value)
    )
    grad_normed = lax.psum(grad_normed_part.astype(jnp.bfloat16), "tensor").astype(jnp.float32)
    grad_unit_one = grad_normed * attn_gain
    grad_attn_gain = jnp.sum(grad_normed * unit_one, axis=0)
    grad_in = grad_middle + scale_one * (
        grad_unit_one - unit_one * jnp.mean(grad_unit_one * unit_one, axis=-1, keepdims=True)
    )
    summed = lax.psum(
        (grad_query, grad_key, grad_value, grad_output, grad_attn_gain, grad_moe_gain), "expert"
    )
    return (
        block_out,
        grad_in,
        summed[4],
        summed[0],
        summed[1],
        summed[2],
        summed[3],
        summed[5],
        grad_gate[None],
        grad_up[None],
        grad_down[None],
    )


def solution(mesh):
    return jax.shard_map(
        on_device,
        mesh=mesh,
        in_specs=(
            P("expert", None),
            P(),
            P(None, "tensor"),
            P(None, "tensor"),
            P(None, "tensor"),
            P("tensor", None),
            P(),
            P("expert", None, "tensor"),
            P("expert", None, "tensor"),
            P("expert", "tensor", None),
            P("expert", None),
            P("expert", None),
            P("expert", None),
        ),
        out_specs=(
            P("expert", None),
            P("expert", None),
            P(),
            P(None, "tensor"),
            P(None, "tensor"),
            P(None, "tensor"),
            P("tensor", None),
            P(),
            P("expert", None, "tensor"),
            P("expert", None, "tensor"),
            P("expert", "tensor", None),
        ),
        check_vma=False,
    )
```

profile of v0, /device:TPU:0, one launch (start us, length us, event | category | flops | bytes accessed | tf_op | source)
XLA Modules:
  0.0 1492.9 jit_solution(14141813546785277838)
XLA Ops:
  41.9 8.3 scatter_custom_fusion
  50.3 7.7 all-reduce.12.cloned.1.call-done
  62.6 27.0 %gather_fusion = bf16[4096,1536]{1,0:T(8,128)(2,1)} fusion(bf16[513,1536]{1,0:T(8,128)(2,1)} %concatenate.50, s32[4096]{0:T(1024)S(1)} %get-tuple-element.39), kind=kCustom, calls=%fused_computation | custom fusion | bytes 25182208 | tf_op jit(solution)/shard_map/gather | solution.py:163
  97.0 7.2 mul.500
  104.2 15.0 %mul.501 = f32[2048,1536]{1,0:T(8,128)} reshape(f32[512,4,1536]{2,1,0:T(4,128)} %mul.500) | data formatting | bytes 25165824 | tf_op jit(solution)/shard_map/mul | solution.py:174
  119.2 7.9 multiply_convert_fusion
  132.9 28.9 %gather_fusion.2 = bf16[4096,1536]{1,0:T(8,128)(2,1)} fusion(bf16[2049,1536]{1,0:T(8,128)(2,1)} %concatenate.52, s32[4096]{0:T(1024)S(1)} %get-tuple-element.38), kind=kCustom, calls=%fused_computation.2 | custom fusion | bytes 25182208 | tf_op jit(solution)/shard_map/gather | solution.py:179
  161.8 172.6 %all-to-all-done = bf16[16,256,1536]{2,1,0:T(8,128)(2,1)} async-done(((bf16[16,256,1536]{2,1,0:T(8,128)(2,1)}), bf16[16,256,1536]{2,1,0:T(8,128)(2,1)}, u32[]{:S(2)}, u32[]{:S(2)}) %all-to-all-start) | async-done | bytes 12582944 | tf_op jit(solution)/shard_map/all_to_all | solution.py:101
  334.5 55.2 %all-to-all-start.2 = ((bf16[16,256,1536]{2,1,0:T(8,128)(2,1)}), bf16[16,256,1536]{2,1,0:T(8,128)(2,1)}, u32[]{:S(2)}, u32[]{:S(2)}) async-start(bf16[16,256,1536]{2,1,0:T(8,128)(2,1)} %bitcast.181), calls=%async_computation.3 | async-start | bytes 25165824 | tf_op jit(solution)/shard_map/all_to_all | solution.py:101
  390.1 11.8 fusion.39
  401.9 11.4 fusion.43
  413.3 211.3 %all-to-all-done.2 = bf16[16,256,1536]{2,1,0:T(8,128)(2,1)} async-done(((bf16[16,256,1536]{2,1,0:T(8,128)(2,1)}), bf16[16,256,1536]{2,1,0:T(8,128)(2,1)}, u32[]{:S(2)}, u32[]{:S(2)}) %all-to-all-start.2) | async-done | bytes 12582944 | tf_op jit(solution)/shard_map/all_to_all | solution.py:101
  624.6 16.8 %multiply_convert_fusion.1 = (bf16[4096,384]{1,0:T(8,128)(2,1)}, bf16[4096,384]{1,0:T(8,128)(2,1)S(1)}, bf16[4096,384]{1,0:T(8,128)(2,1)}) fusion(f32[4096,384]{1,0:T(8,128)} %fusion.43, f32[4096,384]{1,0:T(8,128)} %fusion.39, bf16[4096,1536]{1,0:T(8,128)(2,1)} %bitcast.25, bf16[1,384,1536]{2,1,0:T(8,128)(2,1)} %param.22), kind=kOutput, calls=%fused_computation.16 | convolution fusion | flops 4855431168 | bytes 35782656 | tf_op jit(solution)/shard_map/dot_general | solution.py:36
  641.4 12.0 fusion.41
  653.3 15.5 %add_convert_fusion = bf16[4096,1536]{1,0:T(8,128)(2,1)} fusion(f32[4096,1536]{1,0:T(8,128)} %fusion.41, bf16[4096,384]{1,0:T(8,128)(2,1)} %get-tuple-element.23, bf16[1,1536,384]{2,1,0:T(8,128)(2,1)} %param.21), kind=kOutput, calls=%fused_computation.5 | convolution fusion | flops 4844421120 | bytes 42074112 | tf_op jit(solution)/shard_map/dot_general | solution.py:36
  670.1 11.7 convolution_convert_fusion
  681.8 58.6 %reduce-scatter.5.cloned.1.call-done = bf16[16,128,1536]{2,1,0:T(8,128)(2,1)} async-done(((bf16[16,256,1536]{2,1,0:T(8,128)(2,1)}), bf16[16,128,1536]{2,1,0:T(8,128)(2,1)}) %reduce-scatter.5.cloned.1.call-update) | async-done | bytes 6291472 | tf_op jit(solution)/shard_map/reduce_scatter | solution.py:105
  747.3 18.3 %reduce-scatter.3.cloned.1.call-done = bf16[16,128,1536]{2,1,0:T(8,128)(2,1)} async-done(((bf16[16,256,1536]{2,1,0:T(8,128)(2,1)}), bf16[16,128,1536]{2,1,0:T(8,128)(2,1)}) %reduce-scatter.3.cloned.1.call-update) | async-done | bytes 6291472 | tf_op jit(solution)/shard_map/reduce_scatter | solution.py:105
  765.5 101.9 %all-to-all-done.3 = bf16[16,128,1536]{2,1,0:T(8,128)(2,1)} async-done(((bf16[16,128,1536]{2,1,0:T(8,128)(2,1)}), bf16[16,128,1536]{2,1,0:T(8,128)(2,1)}, u32[]{:S(2)}, u32[]{:S(2)}) %all-to-all-start.3) | async-done | bytes 6291488 | tf_op jit(solution)/shard_map/all_to_all | solution.py:111
  867.4 29.3 %all-to-all-start.1 = ((bf16[16,128,1536]{2,1,0:T(8,128)(2,1)}), bf16[16,128,1536]{2,1,0:T(8,128)(2,1)}, u32[]{:S(2)}, u32[]{:S(2)}) async-start(bf16[16,128,1536]{2,1,0:T(8,128)(2,1)} %reduce-scatter.3.cloned.1.call-done), calls=%async_computation.2 | async-start | bytes 12582912 | tf_op jit(solution)/shard_map/all_to_all | solution.py:111
  902.7 17.3 %gather_fusion.3 = bf16[2048,1536]{1,0:T(8,128)(2,1)} fusion(bf16[2049,1536]{1,0:T(8,128)(2,1)} %concatenate.53, s32[2048]{0:T(1024)S(1)} %broadcast_clamp_fusion), kind=kCustom, calls=%fused_computation.3 | custom fusion | bytes 12591104 | tf_op jit(solution)/shard_map/gather | solution.py:121
  920.0 11.1 gather.18
  931.1 11.6 reduce_sum.117
  942.7 70.7 %all-to-all-done.1 = bf16[16,128,1536]{2,1,0:T(8,128)(2,1)} async-done(((bf16[16,128,1536]{2,1,0:T(8,128)(2,1)}), bf16[16,128,1536]{2,1,0:T(8,128)(2,1)}, u32[]{:S(2)}, u32[]{:S(2)}) %all-to-all-start.1) | async-done | bytes 6291488 | tf_op jit(solution)/shard_map/all_to_all | solution.py:111
  1019.3 16.9 %gather_fusion.1 = bf16[2048,1536]{1,0:T(8,128)(2,1)} fusion(bf16[2049,1536]{1,0:T(8,128)(2,1)} %concatenate.51, s32[2048]{0:T(1024)S(1)} %broadcast_clamp_fusion), kind=kCustom, calls=%fused_computation.1 | custom fusion | bytes 12591104 | tf_op jit(solution)/shard_map/gather | solution.py:121
  1036.1 12.3 reshape.522
  1048.4 12.6 multiply_reduce_fusion
  1108.5 12.0 convolution_bitcast_fusion.1
  1120.5 10.8 convolution_bitcast_fusion.2
  1131.3 9.5 convolution_bitcast_fusion
  1144.9 100.5 %all-reduce.4 = (f32[1536]{0:T(1024)}, f32[1536]{0:T(1024)}) all-reduce(f32[1536]{0:T(1024)S(1)} %get-tuple-element.13, f32[1536]{0:T(1024)S(1)} %get-tuple-element.11), channel_id=1, replica_groups=mesh['expert'=16,'tensor'=2] {'expert'}, use_global_device_ids=true, to_apply=%region_22.23 | all-reduce | flops 3072 | bytes 24576 | tf_op jit(solution)/shard_map/psum | solution.py:252
  1251.8 224.8 %all-reduce.16.cloned.1.call-done = (f32[1536,768]{1,0:T(8,128)}, f32[1536,128]{1,0:T(8,128)}, f32[1536,128]{1,0:T(8,128)}, f32[768,1536]{1,0:T(8,128)}) async-done(((f32[1536,768]{1,0:T(8,128)}, f32[1536,128]{1,0:T(8,128)}, f32[1536,128]{1,0:T(8,128)}, f32[768,1536]{1,0:T(8,128)}), (f32[1536,768]{1,0:T(8,128)}, f32[1536,128]{1,0:T(8,128)}, f32[1536,128]{1,0:T(8,128)}, ...) | async-done | bytes 11010064 | tf_op jit(solution)/shard_map/psum | solution.py:252
  (224 shorter events, 139.1 us)
Async XLA Ops:
  7.2 24.9 %copy-start = (bf16[768,1536]{1,0:T(8,128)(2,1)S(1)}, bf16[768,1536]{1,0:T(8,128)(2,1)}, u32[]{:S(2)}) copy-start(bf16[768,1536]{1,0:T(8,128)(2,1)} %param.18) | copy-start | bytes 7077892
  7.2 50.8 %all-reduce.12.cloned.1.call-start = ((), (), s32[]{:S(2)}) async-start(), calls=%async_computation.6 | async-start | bytes 3145728 | tf_op jit(solution)/shard_map/psum | solution.py:158
  7.3 8.3 copy-start.55
  7.3 8.3 copy-start.47
  15.6 7.4 copy-start.20
  16.1 9.3 copy-start.33
  16.2 9.3 copy-start.35
  34.7 25.9 %copy-start.42 = (f32[1536]{0:T(1024)S(1)}, f32[1536]{0:T(1024)}, u32[]{:S(2)}) copy-start(f32[1536]{0:T(1024)} %param.19) | copy-start | bytes 18436
  89.6 7.0 copy-start.44
  89.6 244.9 %all-to-all-start = ((bf16[16,256,1536]{2,1,0:T(8,128)(2,1)}), bf16[16,256,1536]{2,1,0:T(8,128)(2,1)}, u32[]{:S(2)}, u32[]{:S(2)}) async-start(bf16[16,256,1536]{2,1,0:T(8,128)(2,1)} %bitcast.180), calls=%async_computation | async-start | bytes 25165824 | tf_op jit(solution)/shard_map/all_to_all | solution.py:101
  96.8 7.4 copy-start.18
  334.5 290.1 %all-to-all-start.2 = ((bf16[16,256,1536]{2,1,0:T(8,128)(2,1)}), bf16[16,256,1536]{2,1,0:T(8,128)(2,1)}, u32[]{:S(2)}, u32[]{:S(2)}) async-start(bf16[16,256,1536]{2,1,0:T(8,128)(2,1)} %bitcast.181), calls=%async_computation.3 | async-start | bytes 25165824 | tf_op jit(solution)/shard_map/all_to_all | solution.py:101
  389.7 350.8 %reduce-scatter.5.cloned.1.call-start = ((), (), s32[]{:S(2)}) async-start(), calls=%async_computation.8 | async-start | bytes 18874368 | tf_op jit(solution)/shard_map/reduce_scatter | solution.py:105
  390.1 11.8 copy-start.26
  641.4 12.0 copy-start.16
  668.9 96.6 %reduce-scatter.3.cloned.1.call-start = ((), (), s32[]{:S(2)}) async-start(), calls=%async_computation.7 | async-start | bytes 18874368 | tf_op jit(solution)/shard_map/reduce_scatter | solution.py:105
  740.5 126.9 %all-to-all-start.3 = ((bf16[16,128,1536]{2,1,0:T(8,128)(2,1)}), bf16[16,128,1536]{2,1,0:T(8,128)(2,1)}, u32[]{:S(2)}, u32[]{:S(2)}) async-start(bf16[16,128,1536]{2,1,0:T(8,128)(2,1)} %reduce-scatter.5.cloned.1.call-done), calls=%async_computation.5 | async-start | bytes 12582912 | tf_op jit(solution)/shard_map/all_to_all | solution.py:111
  747.3 149.5 %copy-start.50 = (s32[2048,1]{0,1:T(1,128)S(1)}, s32[2048,1]{0,1:T(1,128)}, u32[]{:S(2)}) copy-start(s32[2048,1]{0,1:T(1,128)} %get-tuple-element.40) | copy-start | bytes 24580
  867.4 146.0 %all-to-all-start.1 = ((bf16[16,128,1536]{2,1,0:T(8,128)(2,1)}), bf16[16,128,1536]{2,1,0:T(8,128)(2,1)}, u32[]{:S(2)}, u32[]{:S(2)}) async-start(bf16[16,128,1536]{2,1,0:T(8,128)(2,1)} %reduce-scatter.3.cloned.1.call-done), calls=%async_computation.2 | async-start | bytes 12582912 | tf_op jit(solution)/shard_map/all_to_all | solution.py:111
  896.7 164.2 %all-reduce.14.cloned.1.call-start = ((), (), s32[]{:S(2)}) async-start(), calls=%async_computation.9 | async-start | bytes 3145728 | tf_op jit(solution)/shard_map/psum | solution.py:122
  931.1 11.6 copy-start.40
  931.1 11.7 copy-start.46
  942.6 199.3 %all-reduce.18.cloned.1.call-start = ((), (), s32[]{:S(2)}) async-start(), calls=%async_computation.11 | async-start | bytes 6291456 | tf_op jit(solution)/shard_map/psum | solution.py:122
  1036.1 12.3 copy-start.19
  1048.4 12.6 copy-start.43
  1048.4 12.6 copy-start.52
  1070.7 8.4 slice-start
  1095.4 381.3 %all-reduce.16.cloned.1.call-start = ((), (), s32[]{:S(2)}) async-start(), calls=%async_computation.10 | async-start | bytes 22020096 | tf_op jit(solution)/shard_map/psum | solution.py:252
  1108.5 12.0 copy-start.17
  1120.5 10.9 copy-start.59
  1131.3 10.6 copy-start.41
  1131.3 10.6 copy-start.54
  (42 other events, 134.6 us)
Sparse Core Ops, SparseCore 0:
  34.8 23.0 all-reduce.11
  669.0 71.3 reduce-scatter.4
  742.9 22.6 reduce-scatter.2
  942.8 21.6 all-reduce.13
  1095.5 46.4 all-reduce.17
  1149.9 326.6 all-reduce.15
where the time goes:
time: 1500 us; the launch traced here: 1490 us
  waiting for transfers between devices  867 us (58%)
  local copies, waits for them, and re-layouts  187 us (12%)
  matrix products  155 us (10%)
  blocking collectives  100 us (7%)
  starting transfers between devices  98.9 us (7%)
  other arithmetic  68.5 us (5%)
  between operations  15.5 us (1%)
    all_to_all x2, waiting for transfers between devices, deliver(): lax.all_to_all(buffer, 'expert', split_axis=0, concat_axis=0, tiled=True)  384 us
    psum x1, waiting for transfers between devices, on_device(): lax.psum((grad_query, grad_key, grad_value, grad_output, grad_attn_gain,...  225 us
    all_to_all x2, waiting for transfers between devices, give_back(): lax.all_to_all(summed_rows, 'expert', split_axis=0, concat_axis=0, tiled=...  173 us
    psum x1, blocking collectives, on_device(): lax.psum((grad_query, grad_key, grad_value, grad_output, grad_attn_gain,...  100 us
    reduce_scatter x2, waiting for transfers between devices, give_back(): lax.psum_scatter(partial_value.reshape(experts, capacity, model_width).as...  76.9 us
    all_to_all x2, starting transfers between devices, deliver(): lax.all_to_all(buffer, 'expert', split_axis=0, concat_axis=0, tiled=True)  62.2 us
    dot_general x7, matrix products, contract_cols(): lax.dot_general(left, right, (((1,), (1,)), ((), ())), preferred_element_...  54.4 us
    gather x3, local copies, waits for them, and re-layouts, collect(): returned[back_index].astype(jnp.float32)  45.3 us
  transfers between devices with their start and end apart: 10, of which 9 were waited for; matrix products, arithmetic and copies ran while one was open for 18% of the time, Pallas kernels for 0%

commit v1 on v0

--- a/solution.py
+++ b/solution.py
@@ -50,7 +50,7 @@
     return jnp.where(causal, raw_scores, masked_score)
 
 
-def on_device(
+def routed_slots(
     hidden_in,
     attn_gain,
     w_query,
@@ -267,7 +267,290 @@
     )
 
 
+def swap(value):
+    return lax.ppermute(value, "tensor", [(0, 1), (1, 0)])
+
+
+def flip(value, bit):
+    places = lax.axis_size("expert")
+    return lax.ppermute(value, "expert", [(i, i ^ bit) for i in range(places)])
+
+
+def part(value, index, count):
+    size = value.shape[0] // count
+    return lax.dynamic_slice_in_dim(value, index * size, size, 0)
+
+
+def ordered(own, other, place):
+    return jnp.where(
+        place == 0,
+        jnp.concatenate([own, other], axis=0),
+        jnp.concatenate([other, own], axis=0),
+    )
+
+
+def add_low(kept, arrived):
+    return (kept.astype(jnp.float32) + arrived.astype(jnp.float32)).astype(jnp.bfloat16)
+
+
+def plane_scatter(value, bit_x, bit_y):
+    left, right = jnp.split(value, 2, axis=0)
+    left = add_low(part(left, bit_x, 2), flip(part(left, 1 - bit_x, 2), 1))
+    right = add_low(part(right, bit_y, 2), flip(part(right, 1 - bit_y, 2), 2))
+    left = add_low(part(left, bit_y, 2), flip(part(left, 1 - bit_y, 2), 2))
+    right = add_low(part(right, bit_x, 2), flip(part(right, 1 - bit_x, 2), 1))
+    return left, right
+
+
+def plane_gather(left, right, bit_x, bit_y):
+    left = ordered(left, flip(left, 2), bit_y)
+    right = ordered(right, flip(right, 1), bit_x)
+    left = ordered(left, flip(left, 1), bit_x)
+    right = ordered(right, flip(right, 2), bit_y)
+    return jnp.concatenate([left, right], axis=0)
+
+
+def sum_experts(value, columns, bit_x, bit_y):
+    left, right = plane_scatter(value.astype(jnp.bfloat16), bit_x, bit_y)
+    rows = left.shape[0]
+    both = lax.psum(jnp.concatenate([left, right], axis=0), "expert", axis_index_groups=columns)
+    return plane_gather(both[:rows], both[rows:], bit_x, bit_y).astype(jnp.float32)
+
+
+def planes_of_four(
+    hidden_in,
+    attn_gain,
+    w_query,
+    w_key,
+    w_value,
+    w_output,
+    moe_gain,
+    w_gate,
+    w_up,
+    w_down,
+    gate_logits,
+    routes,
+    out_grad,
+):
+    tokens, model_width = hidden_in.shape
+    half_tokens = tokens // 2
+    experts = lax.axis_size("expert")
+    planes = experts // 4
+    columns = [[4 * z + r for z in range(planes)] for r in range(4)]
+    core = lax.axis_index("tensor")
+    expert = lax.axis_index("expert")
+    bit_x = expert % 2
+    bit_y = (expert // 2) % 2
+    heads_local = w_query.shape[1] // HD
+    kv_local = w_key.shape[1] // HD
+    groups = heads_local // kv_local
+    scale_factor = 1.0 / math.sqrt(HD)
+    places = jnp.arange(tokens, dtype=jnp.int32)
+    hidden_local = w_down.shape[1]
+    gathered = planes * half_tokens
+
+    def column_gather(value):
+        arrived = lax.all_gather(value, "expert", axis_index_groups=columns, axis=0, tiled=True)
+        return jnp.concatenate([arrived, swap(arrived)], axis=0)
+
+    def column_return(partial_value):
+        own = add_low(partial_value[:gathered], swap(partial_value[gathered:].astype(jnp.bfloat16)))
+        return lax.psum_scatter(
+            own, "expert", axis_index_groups=columns, scatter_dimension=0, tiled=True
+        ).astype(jnp.float32)
+
+    gate_up = jnp.concatenate([w_gate[0], w_up[0]], axis=1)
+    down = w_down[0]
+
+    def plane_weights(own):
+        beside_x = flip(own, 1)
+        beside_y = flip(own, 2)
+        middle_row = own.shape[0] // 2
+        across = jnp.concatenate(
+            [flip(beside_y[:middle_row], 1), flip(beside_x[middle_row:], 2)], axis=0
+        )
+        return [own, beside_x, beside_y, across]
+
+    gate_up_all = plane_weights(gate_up)
+    down_all = plane_weights(down)
+    gates = jnp.concatenate([w[:, :hidden_local] for w in gate_up_all], axis=1)
+    ups = jnp.concatenate([w[:, hidden_local:] for w in gate_up_all], axis=1)
+    downs = jnp.concatenate(down_all, axis=0)
+
+    gate_weights = jax.nn.softmax(gate_logits, axis=-1)
+    names = jnp.arange(experts, dtype=jnp.int32)
+    dense = jnp.sum(
+        jnp.where(routes.T[:, None, :] == names[None, :, None], gate_weights.T[:, None, :], 0.0),
+        axis=0,
+    )
+    dense_all = lax.all_gather(dense, "expert", axis_index_groups=columns, axis=0)
+    mine = dense_all[:, expert ^ jnp.arange(4)]
+    mine = mine.reshape(planes, 4, 2, half_tokens)[:, :, core ^ jnp.arange(2)]
+    mine = mine.transpose(2, 0, 3, 1).reshape(2 * gathered, 4)
+    route_weights = jnp.repeat(mine, hidden_local, axis=1)
+
+    out_grad_half = part(out_grad, core, 2)
+    grad_out_all = column_gather(out_grad_half)
+
+    source = hidden_in.astype(jnp.float32)
+    scale_one = lax.rsqrt(jnp.mean(source * source, axis=-1, keepdims=True) + epsilon)
+    unit_one = source * scale_one
+    normed = (unit_one * attn_gain).astype(jnp.bfloat16)
+    query_pre = jnp.dot(normed, w_query, preferred_element_type=jnp.float32).reshape(
+        tokens, heads_local, HD
+    )
+    queries = (
+        rotate(query_pre, places, 1.0).astype(jnp.bfloat16).reshape(tokens, kv_local, groups, HD)
+    )
+    key_pre = jnp.dot(normed, w_key, preferred_element_type=jnp.float32).reshape(
+        tokens, kv_local, HD
+    )
+    keys_used = rotate(key_pre, places, 1.0).astype(jnp.bfloat16)
+    values_used = (
+        jnp.dot(normed, w_value, preferred_element_type=jnp.float32)
+        .astype(jnp.bfloat16)
+        .reshape(tokens, kv_local, HD)
+    )
+    raw_scores = block_scores(queries, keys_used, 0, scale_factor)
+    biggest = jnp.max(raw_scores, axis=-1, keepdims=True)
+    exponent = jnp.exp(raw_scores - biggest)
+    row_total = jnp.sum(exponent, axis=-1, keepdims=True)
+    weights_low = (exponent / row_total).astype(jnp.bfloat16)
+    logsum = biggest + jnp.log(row_total)
+    attended = jnp.einsum(
+        "cgqk,kcd->qcgd", weights_low, values_used, preferred_element_type=jnp.float32
+    )
+    mixed = attended.reshape(tokens, heads_local * HD).astype(jnp.bfloat16)
+    attn_part = jnp.dot(mixed, w_output, preferred_element_type=jnp.float32).astype(jnp.bfloat16)
+
+    source_half = part(source, core, 2)
+    middle = source_half + (
+        part(attn_part, core, 2).astype(jnp.float32)
+        + swap(part(attn_part, 1 - core, 2)).astype(jnp.float32)
+    )
+    scale_two = lax.rsqrt(jnp.mean(middle * middle, axis=-1, keepdims=True) + epsilon)
+    unit_two = middle * scale_two
+    rows_in = (unit_two * moe_gain).astype(jnp.bfloat16)
+    rows_all = column_gather(rows_in)
+
+    gate_pre = jnp.dot(rows_all, gates, preferred_element_type=jnp.float32)
+    up_pre = jnp.dot(rows_all, ups, preferred_element_type=jnp.float32)
+    sigmoid = jax.nn.sigmoid(gate_pre)
+    activated = gate_pre * sigmoid
+    grad_inner = contract_cols(grad_out_all, downs) * route_weights
+    grad_gate_pre = (grad_inner * up_pre * sigmoid * (1.0 + gate_pre * (1.0 - sigmoid))).astype(
+        jnp.bfloat16
+    )
+    grad_up_pre = (grad_inner * activated).astype(jnp.bfloat16)
+    inner = (activated * up_pre * route_weights).astype(jnp.bfloat16)
+    grad_rows = column_return(contract_cols(grad_gate_pre, gates) + contract_cols(grad_up_pre, ups))
+    moe_result = column_return(jnp.dot(inner, downs, preferred_element_type=jnp.float32))
+    block_half = (middle + moe_result).astype(jnp.bfloat16)
+    block_out = ordered(block_half, swap(block_half), core)
+
+    grad_gate_all = contract_rows(rows_all, grad_gate_pre)
+    grad_up_all = contract_rows(rows_all, grad_up_pre)
+    grad_down_all = contract_rows(inner, grad_out_all)
+
+    def plane_return(pieces):
+        own, to_x, to_y, to_across = pieces
+        middle_row = own.shape[0] // 2
+        low_own = own
+        first = flip(
+            jnp.concatenate([to_x, to_across[:middle_row]], axis=0).astype(jnp.bfloat16), 1
+        ).astype(jnp.float32)
+        second = flip(
+            jnp.concatenate([to_y, to_across[middle_row:]], axis=0).astype(jnp.bfloat16), 2
+        ).astype(jnp.float32)
+        rows = own.shape[0]
+        on_y = flip(first[rows:].astype(jnp.bfloat16), 2).astype(jnp.float32)
+        on_x = flip(second[rows:].astype(jnp.bfloat16), 1).astype(jnp.float32)
+        return low_own + first[:rows] + second[:rows] + jnp.concatenate([on_y, on_x], axis=0)
+
+    def pieces_of(value, axis):
+        return jnp.split(value, 4, axis=axis)
+
+    grad_gate = plane_return(pieces_of(grad_gate_all, 1))
+    grad_up = plane_return(pieces_of(grad_up_all, 1))
+    grad_down = plane_return(pieces_of(grad_down_all, 0))
+
+    grad_out = out_grad_half.astype(jnp.float32)
+    grad_unit_two = grad_rows * moe_gain
+    grad_moe_gain = jnp.sum(grad_rows * unit_two, axis=0)
+    grad_middle = grad_out + scale_two * (
+        grad_unit_two - unit_two * jnp.mean(grad_unit_two * unit_two, axis=-1, keepdims=True)
+    )
+    grad_attn_half = grad_middle.astype(jnp.bfloat16)
+    grad_attn = ordered(grad_attn_half, swap(grad_attn_half), core)
+    grad_output = contract_rows(mixed, grad_attn)
+    grad_mixed = (
+        contract_cols(grad_attn, w_output)
+        .astype(jnp.bfloat16)
+        .reshape(tokens, kv_local, groups, HD)
+    )
+    raw_scores = block_scores(queries, keys_used, 0, scale_factor)
+    probs = jnp.exp(raw_scores - logsum)
+    probs_low = probs.astype(jnp.bfloat16)
+    grad_probs = jnp.einsum(
+        "qcgd,kcd->cgqk", grad_mixed, values_used, preferred_element_type=jnp.float32
+    )
+    delta = jnp.sum(probs * grad_probs, axis=-1, keepdims=True)
+    grad_scores = (probs * (grad_probs - delta)).astype(jnp.bfloat16)
+    grad_queries = (
+        jnp.einsum("cgqk,kcd->qcgd", grad_scores, keys_used, preferred_element_type=jnp.float32)
+        * scale_factor
+    ).reshape(tokens, heads_local, HD)
+    grad_keys = (
+        jnp.einsum("cgqk,qcgd->kcd", grad_scores, queries, preferred_element_type=jnp.float32)
+        * scale_factor
+    )
+    grad_values = jnp.einsum(
+        "cgqk,qcgd->kcd", probs_low, grad_mixed, preferred_element_type=jnp.float32
+    )
+    grad_query_pre = (
+        rotate(grad_queries, places, -1.0).astype(jnp.bfloat16).reshape(tokens, heads_local * HD)
+    )
+    grad_key_pre = (
+        rotate(grad_keys, places, -1.0).astype(jnp.bfloat16).reshape(tokens, kv_local * HD)
+    )
+    grad_value_pre = grad_values.astype(jnp.bfloat16).reshape(tokens, kv_local * HD)
+    grad_all_pre = jnp.concatenate([grad_query_pre, grad_key_pre, grad_value_pre], axis=1)
+    w_all = jnp.concatenate([w_query, w_key, w_value], axis=1)
+    grad_projections = contract_rows(normed, grad_all_pre)
+    grad_normed_part = contract_cols(grad_all_pre, w_all).astype(jnp.bfloat16)
+    grad_normed = part(grad_normed_part, core, 2).astype(jnp.float32) + swap(
+        part(grad_normed_part, 1 - core, 2)
+    ).astype(jnp.float32)
+    grad_unit_one = grad_normed * attn_gain
+    unit_half = part(unit_one, core, 2)
+    scale_half = part(scale_one, core, 2)
+    grad_attn_gain = jnp.sum(grad_normed * unit_half, axis=0)
+    grad_in_half = grad_middle + scale_half * (
+        grad_unit_one - unit_half * jnp.mean(grad_unit_one * unit_half, axis=-1, keepdims=True)
+    )
+    grad_in = ordered(grad_in_half, swap(grad_in_half), core)
+    gains = lax.psum(jnp.stack([grad_attn_gain, grad_moe_gain]), ("expert", "tensor"))
+    output_sum = sum_experts(grad_output, columns, bit_x, bit_y)
+    projection_sum = sum_experts(grad_projections, columns, bit_x, bit_y)
+    query_width = w_query.shape[1]
+    key_width = w_key.shape[1]
+    return (
+        block_out,
+        grad_in,
+        gains[0],
+        projection_sum[:, :query_width],
+        projection_sum[:, query_width : query_width + key_width],
+        projection_sum[:, query_width + key_width :],
+        output_sum,
+        gains[1],
+        grad_gate[None],
+        grad_up[None],
+        grad_down[None],
+    )
+
+
 def solution(mesh):
+    on_device = planes_of_four if mesh.shape["expert"] == 16 else routed_slots
     return jax.shard_map(
         on_device,
         mesh=mesh,

time: 1500 us -> 699 us (0.47)
  waiting for transfers between devices: 867 us -> 179 us
  local copies, waits for them, and re-layouts: 187 us -> 118 us
  starting transfers between devices: 98.9 us -> 42.6 us
  blocking collectives: 100 us -> 56.6 us
  matrix products: 155 us -> 190 us
  other arithmetic: 68.5 us -> 86.8 us
    all_to_all x4 -> x0, waiting for transfers between devices: 557 us -> none  [the longest x2 384 us: deliver(): lax.all_to_all(buffer, 'expert', split_axis=0, concat_axis=0, tiled=True)]
    psum x4 -> x1, waiting for transfers between devices: 234 us -> 13.5 us  [sum_experts(): lax.psum(jnp.concatenate([left, right], axis=0), 'expert', axis_index_gro...]
    ppermute x0 -> x45, waiting for transfers between devices: none -> 166 us  [the longest x36 166 us: flip(): return lax.ppermute(value, 'expert', [(i, i ^ bit) for i in range(places)])]
    all_to_all x4 -> x0, starting transfers between devices: 98.3 us -> none  [the longest x2 62.2 us: deliver(): lax.all_to_all(buffer, 'expert', split_axis=0, concat_axis=0, tiled=True)]
    gather x5 -> x2, local copies, waits for them, and re-layouts: 101 us -> 4.15 us  [the longest x1 2.21 us: planes_of_four(): mine = dense_all[:, expert ^ jnp.arange(4)]]
    reduce_scatter x2, waiting for transfers between devices: 76.9 us -> 0.02 us  [column_return(): lax.psum_scatter(own, 'expert', axis_index_groups=columns, scatter_dimens...]
    psum x1, blocking collectives: 100 us -> 41.3 us  [planes_of_four(): lax.psum(jnp.stack([grad_attn_gain, grad_moe_gain]), ('expert', 'tensor'))]
    ppermute x0 -> x45, starting transfers between devices: none -> 42.3 us  [the longest x36 41.2 us: flip(): return lax.ppermute(value, 'expert', [(i, i ^ bit) for i in range(places)])]
  transfers between devices with their start and end apart: 10 -> 50, of which waited for: 9 -> 18; matrix products, arithmetic and copies ran while one was open for 18% -> 40% of each run, Pallas kernels for 0% -> 0%
where the time goes in v1:
time: 699 us; the launch traced here: 688 us
  matrix products  190 us (27%)
  waiting for transfers between devices  179 us (26%)
  local copies, waits for them, and re-layouts  118 us (17%)
  other arithmetic  86.8 us (12%)
  blocking collectives  56.6 us (8%)
  starting transfers between devices  42.6 us (6%)
  between operations  15.7 us (2%)
    ppermute x36, waiting for transfers between devices, flip(): return lax.ppermute(value, 'expert', [(i, i ^ bit) for i in range(places)])  166 us
    dot_general x5, matrix products, contract_cols(): lax.dot_general(left, right, (((1,), (1,)), ((), ())), preferred_element_...  56.6 us
    dot_general x5, matrix products, contract_rows(): lax.dot_general(left, right, (((0,), (0,)), ((), ())), preferred_element_...  54.3 us
    unnamed x172, local copies, waits for them, and re-layouts  42.6 us
    psum x1, blocking collectives, planes_of_four(): lax.psum(jnp.stack([grad_attn_gain, grad_moe_gain]), ('expert', 'tensor'))  41.3 us
    ppermute x36, starting transfers between devices, flip(): return lax.ppermute(value, 'expert', [(i, i ^ bit) for i in range(places)])  41.2 us
    dot_general x1, matrix products, planes_of_four(): gate_pre = jnp.dot(rows_all, gates, preferred_element_type=jnp.float32)  30.1 us
    all_gather x1, blocking collectives, planes_of_four(): lax.all_gather(dense, 'expert', axis_index_groups=columns, axis=0)  15.4 us
  transfers between devices with their start and end apart: 50, of which 18 were waited for; matrix products, arithmetic and copies ran while one was open for 40% of the time, Pallas kernels for 0%

profile of v1, /device:TPU:0, one launch (start us, length us, event | category | flops | bytes accessed | tf_op | source)
XLA Modules:
  0.0 688.5 jit_solution(4500524747102188334)
XLA Ops:
  52.9 15.4 %all-gather = f32[64,512]{1,0:T(8,128)S(1)} all-gather(f32[16,512]{1,0:T(8,128)} %select_reduce_fusion), channel_id=2, replica_groups={{0,8,16,24},{2,10,18,26},{4,12,20,28},{6,14,22,30},{1,9,17,25},{3,11,19..., dimensions={0}, use_global_device_ids=true | all-gather | bytes 163840 | tf_op jit(solution)/shard_map/all_gather | solution.py:386
  78.4 40.8 %collective-permute-done.7 = bf16[384,1536]{1,0:T(8,128)(2,1)S(1)} collective-permute-done((bf16[384,1536]{1,0:T(8,128)(2,1)}, bf16[384,1536]{1,0:T(8,128)(2,1)S(1)}, u32[]{:S(2)}, u32[]{:S(2)}) %collective-permute-start.7) | collective-permute-done | bytes 1179680 | tf_op jit(solution)/shard_map/ppermute | solution.py:276
  124.9 7.3 %broadcast_in_dim.34 = f32[2048,4,384]{2,1,0:T(4,128)} broadcast(f32[2048,4]{1,0:T(8,128)S(1)} %copy.79), dimensions={0,1} | broadcast | bytes 12615680 | tf_op jit(solution)/shard_map/broadcast_in_dim | solution.py:390
  132.2 10.5 %copy.102 = f32[256,8,4,384]{3,1,2,0:T(8,128)} copy(f32[256,8,4,384]{3,2,1,0:T(4,128)} %bitcast.144) | data formatting | bytes 25165824
  153.5 5.8 collective-permute-done.9
  170.4 11.0 %collective-permute-done.4 = bf16[768,768]{1,0:T(8,128)(2,1)S(1)} collective-permute-done((bf16[768,768]{1,0:T(8,128)(2,1)S(1)}, bf16[768,768]{1,0:T(8,128)(2,1)S(1)}, u32[]{:S(2)}, u32[]{:S(2)}) %collective-permute-start.4) | collective-permute-done | bytes 1179680 | tf_op jit(solution)/shard_map/ppermute | solution.py:276
  181.5 7.3 %collective-permute-done.5 = bf16[768,768]{1,0:T(8,128)(2,1)S(1)} collective-permute-done((bf16[768,768]{1,0:T(8,128)(2,1)S(1)}, bf16[768,768]{1,0:T(8,128)(2,1)S(1)}, u32[]{:S(2)}, u32[]{:S(2)}) %collective-permute-start.5) | collective-permute-done | bytes 1179680 | tf_op jit(solution)/shard_map/ppermute | solution.py:276
  201.2 17.9 %convolution_multiply_fusion = f32[2048,1536]{1,0:T(8,128)} fusion(f32[2048,1536]{1,0:T(8,128)} %bitcast.145, bf16[2048,1536]{1,0:T(8,128)(2,1)} %constant_dynamic-update-slice_fusion.9, bf16[1536,1536]{1,0:T(8,128)(2,1)} %constant_dynamic-update-slice_fusion.4), kind=kOutput, calls=%fused_computation.7 | convolution fusion | flops 9666822144 | bytes 36175872 | tf_op jit(solution)/shard_map/dot_general | solution.py:36
  222.5 14.6 %fusion.56 = f32[2048,1536]{1,0:T(8,128)} fusion(bf16[2048,1536]{1,0:T(8,128)(2,1)} %constant_dynamic-update-slice_fusion, bf16[1536,384]{1,0:T(8,128)(2,1)S(1)} %copy-done.36, bf16[1536,384]{1,0:T(8,128)(2,1)S(1)} %copy-done.34, bf16[1536,384]{1,0:T(8,128)(2,1)S(1)} %copy-done.32, bf16[1536,384]{1,0:T(8,128)(2,1)S(1)} %bitcast.153), kind=kOutput, calls=%fused_computation.115 | convolution fusion | flops 9682550784 | bytes 23592960 | tf_op jit(solution)/shard_map/dot_general | solution.py:437
  237.2 30.1 %multiply_convert_fusion.1 = (bf16[2048,1536]{1,0:T(8,128)(2,1)}, bf16[2048,1536]{1,0:T(8,128)(2,1)}, bf16[2048,1536]{1,0:T(8,128)(2,1)}) fusion(f32[2048,1536]{1,0:T(8,128)} %convolution_multiply_fusion, f32[2048,1536]{1,0:T(8,128)} %fusion.56, f32[2048,1536]{1,0:T(8,128)} %bitcast.146, bf16[2048,1536]{1,0:T(8,128)(2,1)} %constant_dynamic-update-slice_fusion, ...), kind=kOutput, calls=%fused_computation.3 | convolution fusion | flops 9732882432 | bytes 67633152 | tf_op jit(solution)/shard_map/dot_general | solution.py:436
  267.3 15.7 %fusion.112 = (bf16[1536,1536]{1,0:T(8,128)(2,1)S(1)}, f32[1536,1536]{1,0:T(8,128)}) fusion(bf16[2048,1536]{1,0:T(8,128)(2,1)} %get-tuple-element.23, bf16[2048,1536]{1,0:T(8,128)(2,1)} %constant_dynamic-update-slice_fusion.9), kind=kOutput, calls=%fused_computation.231 | convolution fusion | flops 9666035712 | bytes 26738688 | tf_op jit(solution)/shard_map/dot_general | solution.py:30
  285.7 15.4 %fusion.111 = (bf16[1536,1536]{1,0:T(8,128)(2,1)}, f32[1536,1536]{1,0:T(8,128)}) fusion(bf16[2048,1536]{1,0:T(8,128)(2,1)S(1)} %copy-done.26, bf16[2048,1536]{1,0:T(8,128)(2,1)} %get-tuple-element.22), kind=kOutput, calls=%fused_computation.230 | convolution fusion | flops 9666035712 | bytes 26738688 | tf_op jit(solution)/shard_map/dot_general | solution.py:30
  301.1 15.1 %fusion.55 = f32[2048,1536]{1,0:T(8,128)} fusion(bf16[2048,1536]{1,0:T(8,128)(2,1)} %get-tuple-element.22, bf16[1536,384]{1,0:T(8,128)(2,1)} %get-tuple-element.49, bf16[1536,384]{1,0:T(8,128)(2,1)S(1)} %copy-done.35, bf16[1536,384]{1,0:T(8,128)(2,1)S(1)} %copy-done.33, bf16[1536,384]{1,0:T(8,128)(2,1)S(1)} %bitcast.154), kind=kOutput, calls=%fused_computation.114 | convolution fusion | flops 9682550784 | bytes 23592960 | tf_op jit(solution)/shard_map/dot_general | solution.py:36
  321.0 18.0 %convolution_add_fusion = f32[2048,1536]{1,0:T(8,128)} fusion(f32[2048,1536]{1,0:T(8,128)} %fusion.55, bf16[2048,1536]{1,0:T(8,128)(2,1)} %get-tuple-element.21, bf16[1536,384]{1,0:T(8,128)(2,1)} %get-tuple-element.48, bf16[1536,384]{1,0:T(8,128)(2,1)S(1)} %copy-done.31, bf16[1536,384]{1,0:T(8,128)(2,1)S(1)} %get-tuple-element.44, ...), kind=kOutput, calls=%fused_computation.8 | convolution fusion | flops 9685696512 | bytes 36175872 | tf_op jit(solution)/shard_map/dot_general | solution.py:36
  350.4 18.1 %fusion.110 = (bf16[1536,1536]{1,0:T(8,128)(2,1)}, f32[1536,1536]{1,0:T(8,128)}) fusion(bf16[2048,1536]{1,0:T(8,128)(2,1)} %constant_dynamic-update-slice_fusion, bf16[2048,1536]{1,0:T(8,128)(2,1)} %get-tuple-element.21), kind=kOutput, calls=%fused_computation.229 | convolution fusion | flops 9666035712 | bytes 26738688 | tf_op jit(solution)/shard_map/dot_general | solution.py:30
  384.3 12.9 %collective-permute-done.37 = bf16[2304,384]{1,0:T(8,128)(2,1)} collective-permute-done((bf16[2304,384]{1,0:T(8,128)(2,1)}, bf16[2304,384]{1,0:T(8,128)(2,1)}, u32[]{:S(2)}, u32[]{:S(2)}) %collective-permute-start.37) | collective-permute-done | bytes 1769504 | tf_op jit(solution)/shard_map/ppermute | solution.py:276
  398.2 12.0 %fusion.113 = f32[2048,1536]{1,0:T(8,128)S(1)} fusion(bf16[2048,1536]{1,0:T(8,128)(2,1)} %get-tuple-element.23, bf16[1536,1536]{1,0:T(8,128)(2,1)S(1)} %bitcast.164), kind=kOutput, calls=%fused_computation.232 | convolution fusion | flops 9663676416 | bytes 23592960 | tf_op jit(solution)/shard_map/dot_general | solution.py:447
  410.2 4.6 copy-done.8
  420.6 14.6 %collective-permute-done.33 = bf16[2304,384]{1,0:T(8,128)(2,1)} collective-permute-done((bf16[2304,384]{1,0:T(8,128)(2,1)}, bf16[2304,384]{1,0:T(8,128)(2,1)}, u32[]{:S(2)}, u32[]{:S(2)}) %collective-permute-start.33) | collective-permute-done | bytes 1769504 | tf_op jit(solution)/shard_map/ppermute | solution.py:276
  439.7 10.3 %collective-permute-done.43 = bf16[192,1536]{1,0:T(8,128)(2,1)S(1)} collective-permute-done((bf16[192,1536]{1,0:T(8,128)(2,1)}, bf16[192,1536]{1,0:T(8,128)(2,1)S(1)}, u32[]{:S(2)}, u32[]{:S(2)}) %collective-permute-start.43) | collective-permute-done | bytes 589856 | tf_op jit(solution)/shard_map/ppermute | solution.py:276
  456.9 5.7 collective-permute-done.39
  467.0 7.6 %collective-permute-done.35 = bf16[768,384]{1,0:T(8,128)(2,1)S(1)} collective-permute-done((bf16[768,384]{1,0:T(8,128)(2,1)S(1)}, bf16[768,384]{1,0:T(8,128)(2,1)S(1)}, u32[]{:S(2)}, u32[]{:S(2)}) %collective-permute-start.35) | collective-permute-done | bytes 589856 | tf_op jit(solution)/shard_map/ppermute | solution.py:276
  483.1 6.6 fusion.2
  495.1 4.8 fusion.3
  534.4 10.5 %collective-permute-done.17 = bf16[384,1024]{1,0:T(8,128)(2,1)S(1)} collective-permute-done((bf16[384,1024]{1,0:T(8,128)(2,1)S(1)}, bf16[384,1024]{1,0:T(8,128)(2,1)S(1)}, u32[]{:S(2)}, u32[]{:S(2)}) %collective-permute-start.17) | collective-permute-done | bytes 786464 | tf_op jit(solution)/shard_map/ppermute | solution.py:276
  553.0 5.8 collective-permute-done.18
  562.6 5.0 multiply_add_fusion
  568.1 41.3 %psum.21 = f32[2,1536]{1,0:T(2,128)S(1)} all-reduce(f32[2,1536]{1,0:T(2,128)S(1)} %pad_maximum_fusion.22), channel_id=1, replica_groups=mesh['expert'=16,'tensor'=2] {'expert','tensor'}, use_global_device_ids=true, to_apply=%region_14.15 | all-reduce | flops 3072 | bytes 24576 | tf_op jit(solution)/shard_map/psum | solution.py:532
  610.0 13.5 %all-reduce.3.cloned.1.call-done = (bf16[384,1024]{1,0:T(8,128)(2,1)}, bf16[192,1536]{1,0:T(8,128)(2,1)}) async-done(((bf16[384,1024]{1,0:T(8,128)(2,1)}, bf16[192,1536]{1,0:T(8,128)(2,1)}), (bf16[384,1024]{1,0:T(8,128)(2,1)}, bf16[192,1536]{1,0:T(8,128)(2,1)})) %all-reduce.3.cloned.1.call-update) | async-done | bytes 1376272 | tf_op jit(solution)/shard_map/psum | solution.py:316
  639.9 5.2 maximum_select_fusion
  648.8 11.4 %collective-permute-done.30 = bf16[192,1536]{1,0:T(8,128)(2,1)S(1)} collective-permute-done((bf16[192,1536]{1,0:T(8,128)(2,1)S(1)}, bf16[192,1536]{1,0:T(8,128)(2,1)S(1)}, u32[]{:S(2)}, u32[]{:S(2)}) %collective-permute-start.30) | collective-permute-done | bytes 589856 | tf_op jit(solution)/shard_map/ppermute | solution.py:276
  663.8 11.6 %collective-permute-done.22 = bf16[384,1024]{1,0:T(8,128)(2,1)S(1)} collective-permute-done((bf16[384,1024]{1,0:T(8,128)(2,1)S(1)}, bf16[384,1024]{1,0:T(8,128)(2,1)S(1)}, u32[]{:S(2)}, u32[]{:S(2)}) %collective-permute-start.22) | collective-permute-done | bytes 786464 | tf_op jit(solution)/shard_map/ppermute | solution.py:276
  (397 shorter events, 246.2 us)
Async XLA Ops:
  7.2 141.4 %all-gather.6.cloned.1.call-start = ((), (), s32[]{:S(2)}) async-start(), calls=%async_computation.4 | async-start | bytes 3932160 | tf_op jit(solution)/shard_map/all_gather | solution.py:353
  9.5 184.0 %all-gather.4.cloned.1.call-start = ((), (), s32[]{:S(2)}) async-start(), calls=%async_computation.2 | async-start | bytes 3932160 | tf_op jit(solution)/shard_map/all_gather | solution.py:353
  39.3 112.3 %collective-permute-start.3 = (bf16[1536,768]{1,0:T(8,128)(2,1)}, bf16[1536,768]{1,0:T(8,128)(2,1)}, u32[]{:S(2)}, u32[]{:S(2)}) collective-permute-start(bf16[1536,768]{1,0:T(8,128)(2,1)} %pad_maximum_fusion.2), channel_id=1, source_target_pairs={{0,4},{2,6},{4,0},{6,2},{8,12},{10,14},{12,8},{14,10},{16,20},{18,... | collective-permute-start | bytes 7077896 | tf_op jit(solution)/shard_map/ppermute | solution.py:276
  42.1 119.1 %collective-permute-start.2 = (bf16[1536,768]{1,0:T(8,128)(2,1)}, bf16[1536,768]{1,0:T(8,128)(2,1)}, u32[]{:S(2)}, u32[]{:S(2)}) collective-permute-start(bf16[1536,768]{1,0:T(8,128)(2,1)} %pad_maximum_fusion.2), channel_id=1, source_target_pairs={{0,2},{2,0},{4,6},{6,4},{8,10},{10,8},{12,14},{14,12},{16,18},{18,... | collective-permute-start | bytes 7077896 | tf_op jit(solution)/shard_map/ppermute | solution.py:276
  43.6 99.0 %collective-permute-start.6 = (bf16[384,1536]{1,0:T(8,128)(2,1)}, bf16[384,1536]{1,0:T(8,128)(2,1)}, u32[]{:S(2)}, u32[]{:S(2)}) collective-permute-start(bf16[384,1536]{1,0:T(8,128)(2,1)} %bitcast.22), channel_id=1, source_target_pairs={{0,2},{2,0},{4,6},{6,4},{8,10},{10,8},{12,14},{14,12},{16,18},{18,... | collective-permute-start | bytes 3538952 | tf_op jit(solution)/shard_map/ppermute | solution.py:276
  44.2 75.0 %collective-permute-start.7 = (bf16[384,1536]{1,0:T(8,128)(2,1)}, bf16[384,1536]{1,0:T(8,128)(2,1)S(1)}, u32[]{:S(2)}, u32[]{:S(2)}) collective-permute-start(bf16[384,1536]{1,0:T(8,128)(2,1)} %bitcast.22), channel_id=1, source_target_pairs={{0,4},{2,6},{4,0},{6,2},{8,12},{10,14},{12,8},{14,10},{16,20},{18,... | collective-permute-start | bytes 3538952 | tf_op jit(solution)/shard_map/ppermute | solution.py:276
  52.8 426.0 %reduce-scatter.5.cloned.1.call-start = ((), (), s32[]{:S(2)}) async-start(), calls=%async_computation.5 | async-start | bytes 3932160 | tf_op jit(solution)/shard_map/reduce_scatter | solution.py:358
  120.1 29.6 %collective-permute-start.8 = (bf16[192,1536]{1,0:T(8,128)(2,1)}, bf16[192,1536]{1,0:T(8,128)(2,1)}, u32[]{:S(2)}, u32[]{:S(2)}) collective-permute-start(bf16[192,1536]{1,0:T(8,128)(2,1)} %slice.256), channel_id=1, source_target_pairs={{0,2},{2,0},{4,6},{6,4},{8,10},{10,8},{12,14},{14,12},{16,18},{18,... | collective-permute-start | bytes 1769480 | tf_op jit(solution)/shard_map/ppermute | solution.py:276
  148.6 48.7 %collective-permute-start.12 = (bf16[1024,1536]{1,0:T(8,128)(2,1)}, bf16[1024,1536]{1,0:T(8,128)(2,1)}, u32[]{:S(2)}, u32[]{:S(2)}) collective-permute-start(bf16[1024,1536]{1,0:T(8,128)(2,1)} %all-gather.6.cloned.1.call-done), channel_id=1, source_target_pairs={{0,1},{1,0},{2,3},{3,2},{4,5},{5,4},{6,7},{7,6},{8,9},{9,8},{10,11... | collective-permute-start | bytes 9437192 | tf_op jit(solution)/shard_map/ppermute | solution.py:271
  152.9 28.4 %collective-permute-start.4 = (bf16[768,768]{1,0:T(8,128)(2,1)S(1)}, bf16[768,768]{1,0:T(8,128)(2,1)S(1)}, u32[]{:S(2)}, u32[]{:S(2)}) collective-permute-start(bf16[768,768]{1,0:T(8,128)(2,1)S(1)} %slice.250), channel_id=1, source_target_pairs={{0,2},{2,0},{4,6},{6,4},{8,10},{10,8},{12,14},{14,12},{16,18},{18,... | collective-permute-start | bytes 3538952 | tf_op jit(solution)/shard_map/ppermute | solution.py:276
  162.6 26.1 %collective-permute-start.5 = (bf16[768,768]{1,0:T(8,128)(2,1)S(1)}, bf16[768,768]{1,0:T(8,128)(2,1)S(1)}, u32[]{:S(2)}, u32[]{:S(2)}) collective-permute-start(bf16[768,768]{1,0:T(8,128)(2,1)S(1)} %slice.251), channel_id=1, source_target_pairs={{0,4},{2,6},{4,0},{6,2},{8,12},{10,14},{12,8},{14,10},{16,20},{18,... | collective-permute-start | bytes 3538952 | tf_op jit(solution)/shard_map/ppermute | solution.py:276
  193.5 25.6 %collective-permute-start.1 = (bf16[1024,1536]{1,0:T(8,128)(2,1)}, bf16[1024,1536]{1,0:T(8,128)(2,1)S(1)}, u32[]{:S(2)}, u32[]{:S(2)}) collective-permute-start(bf16[1024,1536]{1,0:T(8,128)(2,1)} %all-gather.4.cloned.1.call-done), channel_id=1, source_target_pairs={{0,1},{1,0},{2,3},{3,2},{4,5},{5,4},{6,7},{7,6},{8,9},{9,8},{10,11... | collective-permute-start | bytes 9437192 | tf_op jit(solution)/shard_map/ppermute | solution.py:271
  317.6 60.8 %collective-permute-start.41 = (bf16[576,1536]{1,0:T(8,128)(2,1)}, bf16[576,1536]{1,0:T(8,128)(2,1)}, u32[]{:S(2)}, u32[]{:S(2)}) collective-permute-start(bf16[576,1536]{1,0:T(8,128)(2,1)} %pad_maximum_fusion.7), channel_id=1, source_target_pairs={{0,2},{2,0},{4,6},{6,4},{8,10},{10,8},{12,14},{14,12},{16,18},{18,... | collective-permute-start | bytes 5308424 | tf_op jit(solution)/shard_map/ppermute | solution.py:276
  319.9 61.6 %collective-permute-start.42 = (bf16[576,1536]{1,0:T(8,128)(2,1)}, bf16[576,1536]{1,0:T(8,128)(2,1)}, u32[]{:S(2)}, u32[]{:S(2)}) collective-permute-start(bf16[576,1536]{1,0:T(8,128)(2,1)} %pad_maximum_fusion.8), channel_id=1, source_target_pairs={{0,4},{2,6},{4,0},{6,2},{8,12},{10,14},{12,8},{14,10},{16,20},{18,... | collective-permute-start | bytes 5308424 | tf_op jit(solution)/shard_map/ppermute | solution.py:276
  342.2 26.2 %collective-permute-start.13 = (bf16[1024,1536]{1,0:T(8,128)(2,1)S(1)}, bf16[1024,1536]{1,0:T(8,128)(2,1)S(1)}, u32[]{:S(2)}, u32[]{:S(2)}) collective-permute-start(bf16[1024,1536]{1,0:T(8,128)(2,1)S(1)} %slice.341), channel_id=1, source_target_pairs={{0,1},{1,0},{2,3},{3,2},{4,5},{5,4},{6,7},{7,6},{8,9},{9,8},{10,11... | collective-permute-start | bytes 9437192 | tf_op jit(solution)/shard_map/ppermute | solution.py:271
  347.0 50.3 %collective-permute-start.37 = (bf16[2304,384]{1,0:T(8,128)(2,1)}, bf16[2304,384]{1,0:T(8,128)(2,1)}, u32[]{:S(2)}, u32[]{:S(2)}) collective-permute-start(bf16[2304,384]{1,0:T(8,128)(2,1)} %pad_maximum_fusion.5), channel_id=1, source_target_pairs={{0,2},{2,0},{4,6},{6,4},{8,10},{10,8},{12,14},{14,12},{16,18},{18,... | collective-permute-start | bytes 5308424 | tf_op jit(solution)/shard_map/ppermute | solution.py:276
  349.9 67.0 %collective-permute-start.38 = (bf16[2304,384]{1,0:T(8,128)(2,1)}, bf16[2304,384]{1,0:T(8,128)(2,1)}, u32[]{:S(2)}, u32[]{:S(2)}) collective-permute-start(bf16[2304,384]{1,0:T(8,128)(2,1)} %pad_maximum_fusion.6), channel_id=1, source_target_pairs={{0,4},{2,6},{4,0},{6,2},{8,12},{10,14},{12,8},{14,10},{16,20},{18,... | collective-permute-start | bytes 5308424 | tf_op jit(solution)/shard_map/ppermute | solution.py:276
  371.2 191.3 %reduce-scatter.3.cloned.1.call-start = ((), (), s32[]{:S(2)}) async-start(), calls=%async_computation.3 | async-start | bytes 3932160 | tf_op jit(solution)/shard_map/reduce_scatter | solution.py:358
  376.1 59.1 %collective-permute-start.33 = (bf16[2304,384]{1,0:T(8,128)(2,1)}, bf16[2304,384]{1,0:T(8,128)(2,1)}, u32[]{:S(2)}, u32[]{:S(2)}) collective-permute-start(bf16[2304,384]{1,0:T(8,128)(2,1)} %pad_maximum_fusion.3), channel_id=1, source_target_pairs={{0,2},{2,0},{4,6},{6,4},{8,10},{10,8},{12,14},{14,12},{16,18},{18,... | collective-permute-start | bytes 5308424 | tf_op jit(solution)/shard_map/ppermute | solution.py:276
  378.5 59.4 %collective-permute-start.34 = (bf16[2304,384]{1,0:T(8,128)(2,1)}, bf16[2304,384]{1,0:T(8,128)(2,1)}, u32[]{:S(2)}, u32[]{:S(2)}) collective-permute-start(bf16[2304,384]{1,0:T(8,128)(2,1)} %pad_maximum_fusion.4), channel_id=1, source_target_pairs={{0,4},{2,6},{4,0},{6,2},{8,12},{10,14},{12,8},{14,10},{16,20},{18,... | collective-permute-start | bytes 5308424 | tf_op jit(solution)/shard_map/ppermute | solution.py:276
  381.5 68.5 %collective-permute-start.43 = (bf16[192,1536]{1,0:T(8,128)(2,1)}, bf16[192,1536]{1,0:T(8,128)(2,1)S(1)}, u32[]{:S(2)}, u32[]{:S(2)}) collective-permute-start(bf16[192,1536]{1,0:T(8,128)(2,1)} %slice.289), channel_id=1, source_target_pairs={{0,4},{2,6},{4,0},{6,2},{8,12},{10,14},{12,8},{14,10},{16,20},{18,... | collective-permute-start | bytes 1769480 | tf_op jit(solution)/shard_map/ppermute | solution.py:276
  397.3 53.9 %collective-permute-start.44 = (bf16[192,1536]{1,0:T(8,128)(2,1)}, bf16[192,1536]{1,0:T(8,128)(2,1)S(1)}, u32[]{:S(2)}, u32[]{:S(2)}) collective-permute-start(bf16[192,1536]{1,0:T(8,128)(2,1)} %slice.290), channel_id=1, source_target_pairs={{0,2},{2,0},{4,6},{6,4},{8,10},{10,8},{12,14},{14,12},{16,18},{18,... | collective-permute-start | bytes 1769480 | tf_op jit(solution)/shard_map/ppermute | solution.py:276
  416.9 66.2 %collective-permute-start.10 = (bf16[1024,1536]{1,0:T(8,128)(2,1)}, bf16[1024,1536]{1,0:T(8,128)(2,1)}, u32[]{:S(2)}, u32[]{:S(2)}) collective-permute-start(bf16[1024,1536]{1,0:T(8,128)(2,1)} %slice.342), channel_id=1, source_target_pairs={{0,1},{1,0},{2,3},{3,2},{4,5},{5,4},{6,7},{7,6},{8,9},{9,8},{10,11... | collective-permute-start | bytes 9437192 | tf_op jit(solution)/shard_map/ppermute | solution.py:271
  435.2 27.5 %collective-permute-start.39 = (bf16[768,384]{1,0:T(8,128)(2,1)S(1)}, bf16[768,384]{1,0:T(8,128)(2,1)S(1)}, u32[]{:S(2)}, u32[]{:S(2)}) collective-permute-start(bf16[768,384]{1,0:T(8,128)(2,1)S(1)} %slice.283), channel_id=1, source_target_pairs={{0,4},{2,6},{4,0},{6,2},{8,12},{10,14},{12,8},{14,10},{16,20},{18,... | collective-permute-start | bytes 1769480 | tf_op jit(solution)/shard_map/ppermute | solution.py:276
  437.8 24.9 %collective-permute-start.40 = (bf16[768,384]{1,0:T(8,128)(2,1)S(1)}, bf16[768,384]{1,0:T(8,128)(2,1)S(1)}, u32[]{:S(2)}, u32[]{:S(2)}) collective-permute-start(bf16[768,384]{1,0:T(8,128)(2,1)S(1)} %slice.284), channel_id=1, source_target_pairs={{0,2},{2,0},{4,6},{6,4},{8,10},{10,8},{12,14},{14,12},{16,18},{18,... | collective-permute-start | bytes 1769480 | tf_op jit(solution)/shard_map/ppermute | solution.py:276
  489.7 133.9 %all-reduce.3.cloned.1.call-start = ((), (), s32[]{:S(2)}) async-start(), calls=%async_computation.6 | async-start | bytes 2752512 | tf_op jit(solution)/shard_map/psum | solution.py:316
  529.0 31.1 %collective-permute-start.15 = (bf16[256,1536]{1,0:T(8,128)(2,1)}, bf16[256,1536]{1,0:T(8,128)(2,1)}, u32[]{:S(2)}, u32[]{:S(2)}) collective-permute-start(bf16[256,1536]{1,0:T(8,128)(2,1)} %constant_dynamic-slice_fusion.8), channel_id=1, source_target_pairs={{0,1},{1,0},{2,3},{3,2},{4,5},{5,4},{6,7},{7,6},{8,9},{9,8},{10,11... | collective-permute-start | bytes 2359304 | tf_op jit(solution)/shard_map/ppermute | solution.py:271
  567.6 72.3 %collective-permute-start.16 = (f32[256,1536]{1,0:T(8,128)}, f32[256,1536]{1,0:T(8,128)}, u32[]{:S(2)}, u32[]{:S(2)}) collective-permute-start(f32[256,1536]{1,0:T(8,128)} %get-tuple-element.52), channel_id=1, source_target_pairs={{0,1},{1,0},{2,3},{3,2},{4,5},{5,4},{6,7},{7,6},{8,9},{9,8},{10,11... | collective-permute-start | bytes 4718600 | tf_op jit(solution)/shard_map/ppermute | solution.py:271
  567.6 58.7 %collective-permute-start.11 = (bf16[256,1536]{1,0:T(8,128)(2,1)}, bf16[256,1536]{1,0:T(8,128)(2,1)S(1)}, u32[]{:S(2)}, u32[]{:S(2)}) collective-permute-start(bf16[256,1536]{1,0:T(8,128)(2,1)} %get-tuple-element.53), channel_id=1, source_target_pairs={{0,1},{1,0},{2,3},{3,2},{4,5},{5,4},{6,7},{7,6},{8,9},{9,8},{10,11... | collective-permute-start | bytes 2359304 | tf_op jit(solution)/shard_map/ppermute | solution.py:271
  634.3 25.9 %collective-permute-start.30 = (bf16[192,1536]{1,0:T(8,128)(2,1)S(1)}, bf16[192,1536]{1,0:T(8,128)(2,1)S(1)}, u32[]{:S(2)}, u32[]{:S(2)}) collective-permute-start(bf16[192,1536]{1,0:T(8,128)(2,1)S(1)} %maximum_select_fusion.9), channel_id=1, source_target_pairs={{0,2},{2,0},{4,6},{6,4},{8,10},{10,8},{12,14},{14,12},{16,18},{18,... | collective-permute-start | bytes 1769480 | tf_op jit(solution)/shard_map/ppermute | solution.py:276
  645.4 30.0 %collective-permute-start.22 = (bf16[384,1024]{1,0:T(8,128)(2,1)S(1)}, bf16[384,1024]{1,0:T(8,128)(2,1)S(1)}, u32[]{:S(2)}, u32[]{:S(2)}) collective-permute-start(bf16[384,1024]{1,0:T(8,128)(2,1)S(1)} %maximum_select_fusion.7), channel_id=1, source_target_pairs={{0,2},{2,0},{4,6},{6,4},{8,10},{10,8},{12,14},{14,12},{16,18},{18,... | collective-permute-start | bytes 2359304 | tf_op jit(solution)/shard_map/ppermute | solution.py:276
  647.9 28.2 %collective-permute-start.24 = (bf16[384,1024]{1,0:T(8,128)(2,1)S(1)}, bf16[384,1024]{1,0:T(8,128)(2,1)S(1)}, u32[]{:S(2)}, u32[]{:S(2)}) collective-permute-start(bf16[384,1024]{1,0:T(8,128)(2,1)S(1)} %maximum_select_fusion.8), channel_id=1, source_target_pairs={{0,4},{2,6},{4,0},{6,2},{8,12},{10,14},{12,8},{14,10},{16,20},{18,... | collective-permute-start | bytes 2359304 | tf_op jit(solution)/shard_map/ppermute | solution.py:276
  (99 other events, 804.0 us)
Sparse Core Ops, SparseCore 0:
  10.2 68.1 all-gather.5
  80.5 62.1 all-gather.3
  371.3 60.6 reduce-scatter.4
  489.8 61.0 reduce-scatter.2
  560.2 63.2 all-reduce.2

commit v2 on v0

--- a/solution.py
+++ b/solution.py
@@ -2,7 +2,10 @@
 
 import jax
 import jax.numpy as jnp
+import numpy as np
 from jax import lax
+from jax.experimental import pallas as pl
+from jax.experimental.pallas import tpu as pltpu
 from jax.sharding import PartitionSpec as P
 
 HD = 128
@@ -50,7 +53,7 @@
     return jnp.where(causal, raw_scores, masked_score)
 
 
-def on_device(
+def routed_slots(
     hidden_in,
     attn_gain,
     w_query,
@@ -267,7 +270,777 @@
     )
 
 
+VMEM_BYTES = 60 * 2**20
+
+
+def small_cost(**_):
+    return pl.CostEstimate(flops=1000, bytes_accessed=1000, transcendentals=0)
+
+
+def dot(left, right):
+    return jnp.dot(left, right, preferred_element_type=jnp.float32)
+
+
+def whole(*shape):
+    return pl.BlockSpec(shape, lambda *_: (0,) * len(shape), pipeline_mode=pl.Buffered(1))
+
+
+def swap(value):
+    return lax.ppermute(value, "tensor", [(0, 1), (1, 0)])
+
+
+def flip(value, bit):
+    places = lax.axis_size("expert")
+    return lax.ppermute(value, "expert", [(i, i ^ bit) for i in range(places)])
+
+
+def climb(value):
+    places = lax.axis_size("expert")
+    return lax.ppermute(value, "expert", [(i, i + 4) for i in range(places - 4)])
+
+
+def descend(value):
+    places = lax.axis_size("expert")
+    return lax.ppermute(value, "expert", [(i + 4, i) for i in range(places - 4)])
+
+
+def part(value, index, count):
+    size = value.shape[0] // count
+    return lax.dynamic_slice_in_dim(value, index * size, size, 0)
+
+
+def ordered(own, other, place):
+    return jnp.where(
+        place == 0,
+        jnp.concatenate([own, other], axis=0),
+        jnp.concatenate([other, own], axis=0),
+    )
+
+
+def add_low(kept, arrived):
+    return (kept.astype(jnp.float32) + arrived.astype(jnp.float32)).astype(jnp.bfloat16)
+
+
+def plane_scatter_first(value, bit_x, bit_y):
+    left, right = jnp.split(value, 2, axis=0)
+    left = add_low(part(left, bit_x, 2), flip(part(left, 1 - bit_x, 2), 1))
+    right = add_low(part(right, bit_y, 2), flip(part(right, 1 - bit_y, 2), 2))
+    return left, right
+
+
+def plane_scatter_second(halves, bit_x, bit_y):
+    left, right = halves
+    left = add_low(part(left, bit_y, 2), flip(part(left, 1 - bit_y, 2), 2))
+    right = add_low(part(right, bit_x, 2), flip(part(right, 1 - bit_x, 2), 1))
+    return left, right
+
+
+def plane_gather(left, right, bit_x, bit_y):
+    left = ordered(left, flip(left, 2), bit_y)
+    right = ordered(right, flip(right, 1), bit_x)
+    left = ordered(left, flip(left, 1), bit_x)
+    right = ordered(right, flip(right, 2), bit_y)
+    return jnp.concatenate([left, right], axis=0)
+
+
+def rotary_tables(tokens):
+    halfway = HD // 2
+    frequency = rope_base ** (-np.arange(halfway, dtype=np.float64) / halfway)
+    angles = np.arange(tokens)[:, None] * frequency[None, :]
+    cosine, sine = np.cos(angles), np.sin(angles)
+    return (
+        np.concatenate([cosine, cosine], axis=1).astype(np.float32),
+        np.concatenate([-sine, sine], axis=1).astype(np.float32),
+    )
+
+
+def causal_scores(query_block, keys, row_start, scale_factor):
+    raw = contract_cols(query_block, keys) * scale_factor
+    row_ids = row_start + lax.broadcasted_iota(jnp.int32, raw.shape, 0)
+    return jnp.where(lax.broadcasted_iota(jnp.int32, raw.shape, 1) <= row_ids, raw, masked_score)
+
+
+def softmax_rows(raw):
+    exponent = jnp.exp(raw - jnp.max(raw, axis=-1, keepdims=True))
+    return exponent / jnp.sum(exponent, axis=-1, keepdims=True)
+
+
+def attention_forward(core, hidden, gain, w_query, w_key, w_value, w_output, cosine, sine):
+    tokens, width = hidden.shape
+    half = tokens // 2
+    local = w_query.shape[1]
+    heads = local // HD
+    scale_factor = 1.0 / math.sqrt(HD)
+
+    def kernel(
+        core_ref, hidden_ref, gain_ref, wq_ref, wk_ref, wv_ref, wo_ref, cos_ref, sin_ref,
+        normed_ref, query_ref, key_ref, value_ref, mixed_ref, keep_ref, send_ref, part_ref,
+    ):
+        for block in range(2):
+            rows = pl.ds(block * half, half)
+            source = hidden_ref[rows, :].astype(jnp.float32)
+            scale = lax.rsqrt(jnp.mean(source * source, axis=-1, keepdims=True) + epsilon)
+            normed = (source * scale * gain_ref[...]).astype(jnp.bfloat16)
+            normed_ref[rows, :] = normed
+            cos, sin = cos_ref[rows, :], sin_ref[rows, :]
+
+            def turned(value):
+                return (value * cos + pltpu.roll(value, HD // 2, 1) * sin).astype(jnp.bfloat16)
+
+            query_pre = dot(normed, wq_ref[...])
+            for head in range(heads):
+                lanes = slice(head * HD, (head + 1) * HD)
+                query_ref[rows, lanes] = turned(query_pre[:, lanes])
+            key_ref[rows, :] = turned(dot(normed, wk_ref[...]))
+            value_ref[rows, :] = dot(normed, wv_ref[...]).astype(jnp.bfloat16)
+        for block in range(2):
+            rows = pl.ds(block * half, half)
+            seen = pl.ds(0, (block + 1) * half)
+            keys, values = key_ref[seen, :], value_ref[seen, :]
+            for head in range(heads):
+                lanes = slice(head * HD, (head + 1) * HD)
+                raw = causal_scores(query_ref[rows, lanes], keys, block * half, scale_factor)
+                probs_low = softmax_rows(raw).astype(jnp.bfloat16)
+                mixed_ref[rows, lanes] = dot(probs_low, values).astype(jnp.bfloat16)
+            part_ref[rows, :] = dot(mixed_ref[rows, :], wo_ref[...])
+        own = pl.ds(pl.multiple_of(core_ref[0] * half, half), half)
+        other = pl.ds(pl.multiple_of((1 - core_ref[0]) * half, half), half)
+        keep_ref[...] = hidden_ref[own, :].astype(jnp.float32) + part_ref[own, :]
+        send_ref[...] = part_ref[other, :].astype(jnp.bfloat16)
+
+    def low(rows, columns):
+        return jax.ShapeDtypeStruct((rows, columns), jnp.bfloat16)
+
+    shapes = [
+        low(tokens, width), low(tokens, local), low(tokens, HD), low(tokens, HD),
+        low(tokens, local), jax.ShapeDtypeStruct((half, width), jnp.float32), low(half, width),
+    ]
+    operands = [hidden, gain, w_query, w_key, w_value, w_output, cosine, sine]
+    return pl.pallas_call(
+        kernel,
+        out_shape=shapes,
+        in_specs=[pl.BlockSpec(memory_space=pltpu.SMEM)]
+        + [pl.BlockSpec(memory_space=pltpu.VMEM) for _ in operands],
+        out_specs=[pl.BlockSpec(memory_space=pltpu.VMEM) for _ in shapes],
+        scratch_shapes=[pltpu.VMEM((tokens, width), jnp.float32)],
+        compiler_params=pltpu.CompilerParams(vmem_limit_bytes=VMEM_BYTES),
+        cost_estimate=small_cost(
+            flops=40 * 10**9, bytes_accessed=16 * 10**6, transcendentals=2 * 10**6
+        ),
+        name="attention_forward",
+    )(core, *operands)
+
+
+def attention_backward(grad_mixed, queries, keys, values, cosine, sine):
+    tokens, local = queries.shape
+    half = tokens // 2
+    heads = local // HD
+    scale_factor = 1.0 / math.sqrt(HD)
+
+    def kernel(gm_ref, query_ref, key_ref, value_ref, cos_ref, sin_ref, grad_ref, gk_ref, gv_ref):
+        for block in range(2):
+            rows = pl.ds(block * half, half)
+            seen = pl.ds(0, (block + 1) * half)
+            keys, values = key_ref[seen, :], value_ref[seen, :]
+            cos, sin = cos_ref[rows, :], sin_ref[rows, :]
+            grad_keys = jnp.zeros(((block + 1) * half, HD), jnp.float32)
+            grad_values = grad_keys
+            for head in range(heads):
+                lanes = slice(head * HD, (head + 1) * HD)
+                query, grad = query_ref[rows, lanes], gm_ref[rows, lanes]
+                probs = softmax_rows(causal_scores(query, keys, block * half, scale_factor))
+                grad_probs = contract_cols(grad, values)
+                delta = jnp.sum(probs * grad_probs, axis=-1, keepdims=True)
+                grad_scores = (probs * (grad_probs - delta)).astype(jnp.bfloat16)
+                turned = dot(grad_scores, keys) * scale_factor
+                grad_ref[rows, lanes] = (
+                    turned * cos - pltpu.roll(turned, HD // 2, 1) * sin
+                ).astype(jnp.bfloat16)
+                grad_keys = grad_keys + contract_rows(grad_scores, query)
+                grad_values = grad_values + contract_rows(probs.astype(jnp.bfloat16), grad)
+            if block == 0:
+                gk_ref[pl.ds(0, half), :] = grad_keys
+                gv_ref[pl.ds(0, half), :] = grad_values
+            else:
+                first = pl.ds(0, half)
+                gk_ref[first, :] = gk_ref[first, :] + grad_keys[:half]
+                gv_ref[first, :] = gv_ref[first, :] + grad_values[:half]
+                gk_ref[rows, :] = grad_keys[half:]
+                gv_ref[rows, :] = grad_values[half:]
+        turned = gk_ref[...] * scale_factor
+        grad_ref[:, local : local + HD] = (
+            turned * cos_ref[...] - pltpu.roll(turned, HD // 2, 1) * sin_ref[...]
+        ).astype(jnp.bfloat16)
+        grad_ref[:, local + HD :] = gv_ref[...].astype(jnp.bfloat16)
+
+    return pl.pallas_call(
+        kernel,
+        out_shape=jax.ShapeDtypeStruct((tokens, local + 2 * HD), jnp.bfloat16),
+        in_specs=[pl.BlockSpec(memory_space=pltpu.VMEM)] * 6,
+        out_specs=pl.BlockSpec(memory_space=pltpu.VMEM),
+        scratch_shapes=[pltpu.VMEM((tokens, HD), jnp.float32)] * 2,
+        compiler_params=pltpu.CompilerParams(vmem_limit_bytes=VMEM_BYTES),
+        cost_estimate=small_cost(
+            flops=10 * 10**9, bytes_accessed=4 * 10**6, transcendentals=2 * 10**6
+        ),
+        name="attention_backward",
+    )(grad_mixed, queries, keys, values, cosine, sine)
+
+
+def expert_weights_of(expert_ref, packs, half):
+    start = 2 * half
+    count = packs[0].shape[0] - start
+    row_ids = lax.broadcasted_iota(jnp.int32, (count, 128), 0)
+    lane_ids = lax.broadcasted_iota(jnp.int32, (count, 128), 1)
+    pick = (row_ids == (expert_ref[0] ^ lane_ids)).astype(jnp.bfloat16)
+    sides = []
+    for ref in packs:
+        coarse, fine = ref[start:, :half], ref[start:, half : 2 * half]
+        sides.append(contract_rows(coarse, pick) + contract_rows(fine, pick))
+    return jnp.concatenate(sides, axis=0)
+
+
+def expert_terms(expert, sequences, counts, pieces, first, keep):
+    width = sequences[0][0].shape[1]
+    half = sequences[0][0].shape[0] // 2 // 128 * 128
+    stacked = not isinstance(pieces, list)
+    number = pieces.shape[0] if stacked else len(pieces)
+    flat_pieces = [pieces] if stacked else [piece for own in pieces for piece in own]
+    columns = flat_pieces[0].shape[-1]
+    hidden = columns // 3
+    tokens = 2 * half
+    total = len(sequences)
+    flat = [array for sequence in sequences for array in sequence]
+
+    loads = []
+    if stacked:
+        loads = [[(0, e, 0, width)] for e in range(number)]
+    else:
+        n = 0
+        for own in pieces:
+            loads.append([])
+            place = 0
+            for piece in own:
+                loads[-1].append((n, None, place, piece.shape[0]))
+                place += piece.shape[0]
+                n += 1
+    copy_count = sum(len(own) for own in loads)
+
+    def kernel(expert_ref, *refs):
+        sources, refs = refs[: len(flat)], refs[len(flat) :]
+        piece_refs, refs = refs[: len(flat_pieces)], refs[len(flat_pieces) :]
+        results, (w_ref, gate_all, semaphores) = refs[:-3], refs[-3:]
+        e = pl.program_id(0)
+
+        def copies_of(one):
+            n = sum(len(own) for own in loads[:one])
+            for which, index, place, rows in loads[one]:
+                source = piece_refs[which] if index is None else piece_refs[which].at[index]
+                yield pltpu.make_async_copy(
+                    source, w_ref.at[one, pl.ds(place, rows), :], semaphores.at[n]
+                )
+                n += 1
+
+        def kept(one):
+            return pltpu.make_async_copy(
+                w_ref.at[one], results[-1].at[one], semaphores.at[copy_count + one]
+            )
+
+        @pl.when(e == 0)
+        def _():
+            for one in range(number):
+                for copy in copies_of(one):
+                    copy.start()
+            for s in range(total):
+                gate_all[s * tokens : (s + 1) * tokens, :] = expert_weights_of(
+                    expert_ref, sources[2 * s : 2 * s + 2], half
+                )
+
+        for one in range(number):
+
+            @pl.when(e == one)
+            def _(one=one):
+                for copy in copies_of(one):
+                    copy.wait()
+                if keep:
+                    kept(one).start()
+
+        lanes = lax.broadcasted_iota(jnp.int32, (half, 128), 1)
+        n = 0
+        for joined, count in enumerate(counts):
+            inner_ref, grad_ref = results[2 * joined : 2 * joined + 2]
+            for s in range(count):
+                for side in range(2):
+                    pack = sources[2 * n + side]
+                    here = pl.ds(s * tokens + side * half, half)
+                    gate = gate_all[n * tokens + side * half : n * tokens + (side + 1) * half, :]
+                    weight = jnp.sum(jnp.where(lanes == e + first, gate, 0.0), axis=1, keepdims=True)
+                    both = dot(pack[:half, :], w_ref[e, :, : 2 * hidden])
+                    grad_inner = dot(pack[half : 2 * half, :], w_ref[e, :, 2 * hidden :]) * weight
+                    gate_pre, up_pre = both[:, :hidden], both[:, hidden:]
+                    sigmoid = jax.nn.sigmoid(gate_pre)
+                    activated = gate_pre * sigmoid
+                    grad_gate = grad_inner * up_pre * sigmoid * (1.0 + gate_pre * (1.0 - sigmoid))
+                    grad_ref[here, :hidden] = grad_gate.astype(jnp.bfloat16)
+                    grad_ref[here, hidden:] = (grad_inner * activated).astype(jnp.bfloat16)
+                    inner_ref[here, :] = (activated * up_pre * weight).astype(jnp.bfloat16)
+                n += 1
+
+        if keep:
+
+            @pl.when(e == number - 1)
+            def _():
+                for one in range(number):
+                    kept(one).wait()
+
+    out_specs, out_shape = [], []
+    for count in counts:
+        for size in (hidden, 2 * hidden):
+            out_specs.append(pl.BlockSpec((count * tokens, size), lambda e: (0, e)))
+            out_shape.append(jax.ShapeDtypeStruct((count * tokens, number * size), jnp.bfloat16))
+    if keep:
+        out_specs.append(pl.BlockSpec(memory_space=pl.ANY))
+        out_shape.append(jax.ShapeDtypeStruct((number, width, columns), jnp.bfloat16))
+    results = pl.pallas_call(
+        kernel,
+        grid=(number,),
+        in_specs=[pl.BlockSpec(memory_space=pltpu.SMEM)]
+        + [whole(*array.shape) for array in flat]
+        + [pl.BlockSpec(memory_space=pl.ANY)] * len(flat_pieces),
+        out_specs=out_specs,
+        out_shape=out_shape,
+        scratch_shapes=[
+            pltpu.VMEM((number, width, columns), jnp.bfloat16),
+            pltpu.VMEM((total * tokens, 128), jnp.float32),
+            pltpu.SemaphoreType.DMA((copy_count + number,)),
+        ],
+        compiler_params=pltpu.CompilerParams(vmem_limit_bytes=VMEM_BYTES),
+        cost_estimate=small_cost(
+            flops=total * number * 6 * tokens * width * hidden,
+            bytes_accessed=(total + number) * 4 * 10**6,
+            transcendentals=total * number * tokens * hidden,
+        ),
+        name="expert_terms",
+    )(expert, *flat, *flat_pieces)
+    terms = [tuple(results[2 * n : 2 * n + 2]) for n in range(len(counts))]
+    return (*terms, results[-1]) if keep else tuple(terms)
+
+
+def expert_sums(near, far, near_weights, far_weights, half):
+    rows, columns = near[0].shape
+    number, width = near_weights.shape[:2]
+    hidden = columns // number
+    count = rows // (2 * half)
+    block = 256
+
+    def kernel(inner_ref, grad_ref, inner_far, grad_far, w_ref, w_far, back_own, back_other, out_own, out_other):
+        def added(near_ref, far_ref, size, lanes):
+            total = contract_cols(far_ref[...], w_far[0, :, lanes])
+            for e in range(number):
+                total += contract_cols(near_ref[:, e * size : (e + 1) * size], w_ref[e, :, lanes])
+            return total
+
+        back = added(grad_ref, grad_far, 2 * hidden, slice(0, 2 * hidden))
+        out = added(inner_ref, inner_far, hidden, slice(2 * hidden, 3 * hidden))
+        for s in range(count):
+            start = 2 * s * half
+            back_own[s] = back[start : start + half]
+            back_other[s] = back[start + half : start + 2 * half].astype(jnp.bfloat16)
+            out_own[s] = out[start : start + half]
+            out_other[s] = out[start + half : start + 2 * half].astype(jnp.bfloat16)
+
+    wide = jax.ShapeDtypeStruct((count, half, width), jnp.float32)
+    low = jax.ShapeDtypeStruct((count, half, width), jnp.bfloat16)
+    return pl.pallas_call(
+        kernel,
+        grid=(width // block,),
+        in_specs=[whole(*a.shape) for a in (*near, *far)]
+        + [
+            pl.BlockSpec((number, block, 3 * hidden), lambda n: (0, n, 0)),
+            pl.BlockSpec((1, block, 3 * hidden), lambda n: (0, n, 0)),
+        ],
+        out_specs=[pl.BlockSpec((count, half, block), lambda n: (0, 0, n))] * 4,
+        out_shape=[wide, low, wide, low],
+        compiler_params=pltpu.CompilerParams(vmem_limit_bytes=VMEM_BYTES),
+        cost_estimate=small_cost(
+            flops=(number + 1) * 6 * rows * width * hidden,
+            bytes_accessed=3 * 10**7,
+            transcendentals=0,
+        ),
+        name="expert_sums",
+    )(*near, *far, near_weights, far_weights)
+
+
+def load_copies(sequence, half, sources, x_all, dy_all, semaphores):
+    for n in range(4):
+        target = x_all if n < 2 else dy_all
+        yield pltpu.make_async_copy(
+            sources[2 * sequence + n % 2].at[pl.ds((n // 2) * half, half), :],
+            target.at[pl.ds((2 * sequence + n % 2) * half, half), :],
+            semaphores.at[4 * sequence + n],
+        )
+
+
+def expert_weight_grads(sequences, terms, experts, hidden):
+    width = sequences[0][0].shape[1]
+    half = sequences[0][0].shape[0] // 2 // 128 * 128
+    start, number = experts
+    tokens = 2 * half
+    counts = [pair[0].shape[0] // tokens for pair in terms]
+    flat = [array for sequence in sequences for array in sequence]
+    total = len(sequences)
+    quarter = width // 4
+
+    def kernel(*refs):
+        sources, refs = refs[: len(flat)], refs[len(flat) :]
+        term_refs, refs = refs[: 2 * len(counts)], refs[2 * len(counts) :]
+        result_refs, (x_all, dy_all, semaphores) = refs[:-3], refs[-3:]
+        e = pl.program_id(0)
+
+        @pl.when(e == 0)
+        def _():
+            for s in range(total):
+                for copy in load_copies(s, half, sources, x_all, dy_all, semaphores):
+                    copy.start()
+
+        gate_up = down = None
+        first = 0
+        for joined, count in enumerate(counts):
+
+            @pl.when(e == 0)
+            def _(first=first, count=count):
+                for s in range(first, first + count):
+                    for copy in load_copies(s, half, sources, x_all, dy_all, semaphores):
+                        copy.wait()
+
+            span = pl.ds(first * tokens, count * tokens)
+            one = contract_rows(x_all[span, :], term_refs[2 * joined + 1][...])
+            two = contract_rows(dy_all[span, :], term_refs[2 * joined][...])
+            gate_up = one if gate_up is None else gate_up + one
+            down = two if down is None else down + two
+            first += count
+        for n in range(number):
+
+            @pl.when(e == n)
+            def _(n=n):
+                for q in range(4):
+                    rows = slice(q * quarter, (q + 1) * quarter)
+                    result_refs[4 * n + q][:, : 2 * hidden] = gate_up[rows].astype(jnp.bfloat16)
+                    result_refs[4 * n + q][:, 2 * hidden :] = down[rows].astype(jnp.bfloat16)
+
+    def beside(count, columns):
+        return pl.BlockSpec((count * tokens, columns), lambda e: (0, e + start))
+
+    return pl.pallas_call(
+        kernel,
+        grid=(number,),
+        in_specs=[pl.BlockSpec(memory_space=pl.ANY)] * len(flat)
+        + [beside(count, columns) for count in counts for columns in (hidden, 2 * hidden)],
+        out_specs=[whole(quarter, 3 * hidden)] * (4 * number),
+        scratch_shapes=[pltpu.VMEM((total * tokens, width), jnp.bfloat16)] * 2
+        + [pltpu.SemaphoreType.DMA((4 * total,))],
+        out_shape=[jax.ShapeDtypeStruct((quarter, 3 * hidden), jnp.bfloat16)] * (4 * number),
+        compiler_params=pltpu.CompilerParams(vmem_limit_bytes=VMEM_BYTES),
+        cost_estimate=small_cost(),
+        name="expert_weight_grads",
+    )(*flat, *(array for pair in terms for array in pair))
+
+
+def own_weight_grads(sequences, terms, arrived, hidden):
+    width = sequences[0][0].shape[1]
+    half = sequences[0][0].shape[0] // 2 // 128 * 128
+    tokens = 2 * half
+    counts = [pair[0].shape[0] // tokens for pair in terms]
+    flat = [array for sequence in sequences for array in sequence]
+    total = len(sequences)
+    quarter = width // 4
+
+    def kernel(*refs):
+        sources, refs = refs[: len(flat)], refs[len(flat) :]
+        term_refs, refs = refs[: 2 * len(counts)], refs[2 * len(counts) :]
+        arrived_refs, refs = refs[:6], refs[6:]
+        gate_ref, up_ref, down_ref, x_all, dy_all, semaphores = refs
+        for s in range(total):
+            for copy in load_copies(s, half, sources, x_all, dy_all, semaphores):
+                copy.start()
+        gate_up = down = None
+        first = 0
+        for joined, count in enumerate(counts):
+            for s in range(first, first + count):
+                for copy in load_copies(s, half, sources, x_all, dy_all, semaphores):
+                    copy.wait()
+            span = pl.ds(first * tokens, count * tokens)
+            one = contract_rows(x_all[span, :], term_refs[2 * joined + 1][...])
+            two = contract_rows(term_refs[2 * joined][...], dy_all[span, :])
+            gate_up = one if gate_up is None else gate_up + one
+            down = two if down is None else down + two
+            first += count
+        for q in range(4):
+            rows = slice(q * quarter, (q + 1) * quarter)
+            inside = slice(q % 2 * quarter, (q % 2 + 1) * quarter)
+            more = arrived_refs[q][...].astype(jnp.float32) + arrived_refs[4 + q // 2][
+                inside, :
+            ].astype(jnp.float32)
+            both = gate_up[rows] + more[:, : 2 * hidden]
+            gate_ref[0, rows, :] = both[:, :hidden]
+            up_ref[0, rows, :] = both[:, hidden:]
+            down_ref[0, :, rows] = down[:, rows] + more[:, 2 * hidden :].T
+
+    def beside(count, columns):
+        return pl.BlockSpec((count * tokens, columns), lambda e: (0, 0))
+
+    tall = jax.ShapeDtypeStruct((1, width, hidden), jnp.float32)
+    flat_down = jax.ShapeDtypeStruct((1, hidden, width), jnp.float32)
+    return pl.pallas_call(
+        kernel,
+        grid=(1,),
+        in_specs=[pl.BlockSpec(memory_space=pl.ANY)] * len(flat)
+        + [beside(count, columns) for count in counts for columns in (hidden, 2 * hidden)]
+        + [whole(quarter, 3 * hidden)] * 4
+        + [whole(2 * quarter, 3 * hidden)] * 2,
+        out_specs=[whole(*tall.shape), whole(*tall.shape), whole(*flat_down.shape)],
+        scratch_shapes=[pltpu.VMEM((total * tokens, width), jnp.bfloat16)] * 2
+        + [pltpu.SemaphoreType.DMA((4 * total,))],
+        out_shape=[tall, tall, flat_down],
+        compiler_params=pltpu.CompilerParams(vmem_limit_bytes=VMEM_BYTES),
+        cost_estimate=small_cost(),
+        name="own_weight_grads",
+    )(*flat, *(array for pair in terms for array in pair), *arrived)
+
+
+def planes_of_four(
+    hidden_in,
+    attn_gain,
+    w_query,
+    w_key,
+    w_value,
+    w_output,
+    moe_gain,
+    w_gate,
+    w_up,
+    w_down,
+    gate_logits,
+    routes,
+    out_grad,
+):
+    tokens, width = hidden_in.shape
+    half = tokens // 2
+    experts = lax.axis_size("expert")
+    columns = [[4 * z + r for z in range(4)] for r in range(4)]
+    core = lax.axis_index("tensor")
+    expert = lax.axis_index("expert")
+    plane = expert // 4
+    bit_x = expert % 2
+    bit_y = (expert // 2) % 2
+    hidden = w_down.shape[1]
+    together = lax.optimization_barrier
+
+    own_weights = jnp.concatenate([w_gate[0], w_up[0], w_down[0].T], axis=1)
+    quarter = width // 4
+    pieces = [own_weights[:quarter], own_weights[quarter : 2 * quarter], own_weights[2 * quarter :]]
+    gate_weights = jax.nn.softmax(gate_logits, axis=-1)
+    names = jnp.arange(experts, dtype=jnp.int32)
+    dense = jnp.sum(
+        jnp.where(routes.T[:, None, :] == names[None, :, None], gate_weights.T[:, None, :], 0.0),
+        axis=0,
+    )
+    dense = lax.dynamic_slice_in_dim(dense, core * half, half, 1)
+    coarse = dense.astype(jnp.bfloat16)
+    fine = (dense - coarse.astype(jnp.float32)).astype(jnp.bfloat16)
+    extra = jnp.pad(jnp.concatenate([coarse, fine], axis=1), ((0, 0), (0, width - 2 * half)))
+    out_grad_half = part(out_grad, core, 2)
+    dy_own = jnp.concatenate([out_grad_half, extra], axis=0)
+
+    x0, y0 = flip(pieces[0], 1), flip(pieces[0], 2)
+    dy_up_one, dy_down_one = climb(dy_own), descend(dy_own)
+    cosine, sine = (jnp.asarray(table) for table in rotary_tables(tokens))
+    normed, queries, keys, values, mixed, keep, send = attention_forward(
+        core.reshape(1), hidden_in, attn_gain[None], w_query, w_key, w_value, w_output, cosine, sine
+    )
+    send, x0, y0, dy_up_one, dy_down_one, piece = together(
+        (send, x0, y0, dy_up_one, dy_down_one, pieces[1])
+    )
+    x1, y1 = flip(piece, 1), flip(piece, 2)
+    middle = keep + swap(send).astype(jnp.float32)
+    scale_two = lax.rsqrt(jnp.mean(middle * middle, axis=-1, keepdims=True) + epsilon)
+    unit_two = middle * scale_two
+    rows_in = (unit_two * moe_gain).astype(jnp.bfloat16)
+    up_one, down_one = climb(rows_in), descend(rows_in)
+    x1, y1, up_one, down_one, dy_up_one, dy_down_one, piece = together(
+        (x1, y1, up_one, down_one, dy_up_one, dy_down_one, pieces[2])
+    )
+    up_one = jnp.concatenate([up_one, dy_up_one], axis=0)
+    down_one = jnp.concatenate([down_one, dy_down_one], axis=0)
+    up_one, down_one, piece = together((up_one, down_one, piece))
+    x2, y2 = flip(piece, 1), flip(piece, 2)
+    up_two, down_two = climb(up_one), descend(down_one)
+    own = jnp.concatenate([rows_in, dy_own], axis=0)
+    first = jnp.where(plane == 0, down_one, up_one)
+    own, first = (own, swap(own)), (first, swap(first))
+    far_from_y = jnp.concatenate([y0, y1], axis=0)
+    x2, y2, up_two, down_two, own, first, far_from_y = together(
+        (x2, y2, up_two, down_two, own, first, far_from_y)
+    )
+    far_weights = [flip(far_from_y, 1), flip(x2, 2)]
+    up_three, down_three = climb(up_two), descend(down_two)
+    number = expert.reshape(1)
+    near_early, near_weights = expert_terms(
+        number, [own, first], [2], [[own_weights], [x0, x1, x2], [y0, y1, y2]], 0, True
+    )
+    second = jnp.where(plane == 0, down_two, jnp.where(plane == 3, up_two, down_one))
+    second = (second, swap(second))
+    far_weights, up_three, down_three, near_early, second = together(
+        (far_weights, up_three, down_three, near_early, second)
+    )
+    third = jnp.where(
+        plane == 0,
+        down_three,
+        jnp.where(plane == 1, down_two, jnp.where(plane == 2, up_two, up_three)),
+    )
+    third = (third, swap(third))
+    sequences = [own, first, third, second]
+    far_early, far_late, far_weights = expert_terms(
+        number, sequences, [2, 2], [far_weights], 3, True
+    )
+    to_far = expert_weight_grads(sequences, [far_early, far_late], (0, 1), hidden)
+
+    over_x, over_y = [flip(to_far[0], 1)], [flip(to_far[2], 2)]
+    to_far, late = together((to_far, sequences[2:]))
+    (near_late,) = expert_terms(number, late, [2], near_weights, 0, False)
+    near_late, over_x, over_y, to_far = together((near_late, over_x, over_y, to_far))
+    over_x, over_y = over_x + [flip(to_far[1], 1)], over_y + [flip(to_far[3], 2)]
+    late_sums = expert_sums(near_late, far_late, near_weights, far_weights, half)
+    late_sums, over_x, over_y, near_early, near_late = together(
+        (late_sums, over_x, over_y, near_early, near_late)
+    )
+    back_late = add_low(late_sums[0], swap(late_sums[1]))
+    second_back, third_back = back_late[1], back_late[0]
+
+    falling, rising = descend(third_back), climb(third_back)
+    third_back, near_early, near_late = together((third_back, near_early, near_late))
+    beside = expert_weight_grads(sequences, [near_early, near_late], (1, 2), hidden)
+    falling, rising, beside, near_early, far_early = together(
+        (falling, rising, beside, near_early, far_early)
+    )
+    to_x, to_y = beside[:4], beside[4:]
+    falling = add_low(jnp.where(plane == 3, second_back, third_back), falling)
+    rising = add_low(jnp.where(plane == 0, second_back, third_back), rising)
+    falling, rising, near_early, far_early = together((falling, rising, near_early, far_early))
+    falling, rising = descend(falling), climb(rising)
+    from_x, from_y = [flip(to_x[0], 1)], [flip(to_y[2], 2)]
+    early_sums = expert_sums(near_early, far_early, near_weights, far_weights, half)
+    falling, rising, early_sums, from_x, from_y, to_x, to_y = together(
+        (falling, rising, early_sums, from_x, from_y, to_x, to_y)
+    )
+    back_early = add_low(early_sums[0], swap(early_sums[1]))
+    own_back, first_back = back_early[0], back_early[1]
+    falling = add_low(first_back, falling)
+    rising = add_low(jnp.where(plane == 0, first_back, second_back), rising)
+    falling, rising = descend(falling), climb(rising)
+    from_x, from_y = from_x + [flip(to_x[1], 1)], from_y + [flip(to_y[3], 2)]
+    with_x = jnp.concatenate([add_low(to_y[n], over_x[n]) for n in range(2)], axis=0)
+    with_y = jnp.concatenate([add_low(to_x[2 + n], over_y[n]) for n in range(2)], axis=0)
+    out_late = add_low(late_sums[2], swap(late_sums[3]))
+    out_early = add_low(early_sums[2], swap(early_sums[3]))
+    own_out, first_out, second_out, third_out = out_early[0], out_early[1], out_late[1], out_late[0]
+    by_plane = [
+        jnp.where(plane == 0, own_out, jnp.where(plane == 1, first_out, third_out)),
+        jnp.where(plane == 1, own_out, jnp.where(plane == 3, second_out, first_out)),
+        jnp.where(plane == 2, own_out, jnp.where(plane == 3, first_out, second_out)),
+        jnp.where(plane == 3, own_out, jnp.where(plane == 2, second_out, third_out)),
+    ]
+    results = jnp.concatenate(by_plane, axis=0)
+    falling, rising, results, from_x, from_y, with_x, with_y = together(
+        (falling, rising, results, from_x, from_y, with_x, with_y)
+    )
+    moe_result = lax.psum_scatter(
+        results, "expert", axis_index_groups=columns, scatter_dimension=0, tiled=True
+    )
+    grad_rows = (
+        own_back.astype(jnp.float32) + falling.astype(jnp.float32) + rising.astype(jnp.float32)
+    )
+    grad_out = out_grad_half.astype(jnp.float32)
+    grad_unit_two = grad_rows * moe_gain
+    grad_moe_gain = jnp.sum(grad_rows * unit_two, axis=0)
+    grad_middle = grad_out + scale_two * (
+        grad_unit_two - unit_two * jnp.mean(grad_unit_two * unit_two, axis=-1, keepdims=True)
+    )
+    grad_attn_half = grad_middle.astype(jnp.bfloat16)
+    grad_attn = ordered(grad_attn_half, swap(grad_attn_half), core)
+    grad_mixed = contract_cols(grad_attn, w_output).astype(jnp.bfloat16)
+    grad_output = contract_rows(mixed, grad_attn).astype(jnp.bfloat16)
+    grad_mixed, grad_output = together((grad_mixed, grad_output))
+    output_parts = plane_scatter_first(grad_output, bit_x, bit_y)
+    grad_all_pre = attention_backward(grad_mixed, queries, keys, values, cosine, sine)
+    grad_all_pre, output_parts = together((grad_all_pre, output_parts))
+    grad_projections = contract_rows(normed, grad_all_pre).astype(jnp.bfloat16)
+    output_parts = plane_scatter_second(output_parts, bit_x, bit_y)
+    projection_parts = plane_scatter_first(grad_projections, bit_x, bit_y)
+    w_all = jnp.concatenate([w_query, w_key, w_value], axis=1)
+    grad_normed_part = contract_cols(grad_all_pre, w_all).astype(jnp.bfloat16)
+    grad_normed = part(grad_normed_part, core, 2).astype(jnp.float32) + swap(
+        part(grad_normed_part, 1 - core, 2)
+    ).astype(jnp.float32)
+    source_half = part(hidden_in, core, 2).astype(jnp.float32)
+    scale_half = lax.rsqrt(jnp.mean(source_half * source_half, axis=-1, keepdims=True) + epsilon)
+    unit_half = source_half * scale_half
+    grad_unit_one = grad_normed * attn_gain
+    grad_attn_gain = jnp.sum(grad_normed * unit_half, axis=0)
+    grad_in_half = grad_middle + scale_half * (
+        grad_unit_one - unit_half * jnp.mean(grad_unit_one * unit_half, axis=-1, keepdims=True)
+    )
+    gains = jnp.stack([grad_attn_gain, grad_moe_gain])
+    projection_parts, output_parts, gains, grad_in_half = together(
+        (projection_parts, output_parts, gains, grad_in_half)
+    )
+    projection_parts = plane_scatter_second(projection_parts, bit_x, bit_y)
+    gains = (gains + swap(gains)).reshape(-1, grad_projections.shape[1])
+    gain_rows = gains.shape[0]
+    gains = jnp.pad(gains, ((0, 16 - gain_rows), (0, 0))).astype(jnp.bfloat16)
+    grad_in = ordered(grad_in_half, swap(grad_in_half), core)
+    output_both = jnp.concatenate(output_parts, axis=0)
+    projection_both = jnp.concatenate([*projection_parts, gains], axis=0)
+    projection_both, output_both, grad_in, moe_result, with_x, with_y = together(
+        (projection_both, output_both, grad_in, moe_result, with_x, with_y)
+    )
+    output_both, projection_both = lax.psum(
+        (output_both, projection_both), "expert", axis_index_groups=columns
+    )
+    block_half = (middle + moe_result.astype(jnp.float32)).astype(jnp.bfloat16)
+    block_out = ordered(block_half, swap(block_half), core)
+    then_y, then_x = flip(with_x, 2), flip(with_y, 1)
+    arrived = (*from_x, *from_y, then_y, then_x)
+    expert_grads = own_weight_grads(sequences, [near_early, near_late], arrived, hidden)
+    output_both, projection_both, expert_grads, block_out = together(
+        (output_both, projection_both, expert_grads, block_out)
+    )
+    output_sum = plane_gather(*jnp.split(output_both, 2), bit_x, bit_y)
+    gains = projection_both[-16:].astype(jnp.float32)
+    gains = gains + flip(gains, 1)
+    gains = gains + flip(gains, 2)
+    gains_sum = gains[:gain_rows].reshape(2, width)
+    projection_both = projection_both[:-16]
+    grad_gate, grad_up, grad_down = expert_grads
+    projections = plane_gather(*jnp.split(projection_both, 2), bit_x, bit_y).astype(jnp.float32)
+    query_width = w_query.shape[1]
+    key_width = w_key.shape[1]
+    return (
+        block_out,
+        grad_in,
+        gains_sum[0],
+        projections[:, :query_width],
+        projections[:, query_width : query_width + key_width],
+        projections[:, query_width + key_width :],
+        output_sum.astype(jnp.float32),
+        gains_sum[1],
+        grad_gate,
+        grad_up,
+        grad_down,
+    )
+
+
 def solution(mesh):
+    on_device = planes_of_four if mesh.shape["expert"] == 16 else routed_slots
     return jax.shard_map(
         on_device,
         mesh=mesh,

time: 1500 us -> 608 us (0.41)
  waiting for transfers between devices: 867 us -> 200 us
  Pallas kernels: 0 us -> 191 us
  local copies, waits for them, and re-layouts: 187 us -> 28.8 us
  matrix products: 155 us -> 11 us
  blocking collectives: 100 us -> 0 us
    all_to_all x4 -> x0, waiting for transfers between devices: 557 us -> none  [the longest x2 384 us: deliver(): lax.all_to_all(buffer, 'expert', split_axis=0, concat_axis=0, tiled=True)]
    psum x4 -> x1, waiting for transfers between devices: 234 us -> 3.96 us  [planes_of_four(): lax.psum((output_both, projection_both), 'expert', axis_index_groups=colu...]
    ppermute x0 -> x64, waiting for transfers between devices: none -> 196 us  [the longest x36 101 us: flip(): return lax.ppermute(value, 'expert', [(i, i ^ bit) for i in range(places)])]
    pallas_call x0 -> x10, Pallas kernels: none -> 191 us  [the longest x3 56.7 us: expert_terms(): pl.pallas_call(kernel, grid=(number,), in_specs=[pl.BlockSpec(memory_spac...]
    gather x5 -> x0, local copies, waits for them, and re-layouts: 101 us -> none  [the longest x3 45.3 us: collect(): returned[back_index].astype(jnp.float32)]
    psum x1 -> x0, blocking collectives: 100 us -> none  [on_device(): lax.psum((grad_query, grad_key, grad_value, grad_output, grad_attn_gain,...]
    all_to_all x4 -> x0, starting transfers between devices: 98.3 us -> none  [the longest x2 62.2 us: deliver(): lax.all_to_all(buffer, 'expert', split_axis=0, concat_axis=0, tiled=True)]
    ppermute x0 -> x64, starting transfers between devices: none -> 86 us  [the longest x36 39.7 us: flip(): return lax.ppermute(value, 'expert', [(i, i ^ bit) for i in range(places)])]
  transfers between devices with their start and end apart: 10 -> 66, of which waited for: 9 -> 34; matrix products, arithmetic and copies ran while one was open for 18% -> 12% of each run, Pallas kernels for 0% -> 26%
where the time goes in v2:
time: 608 us; the launch traced here: 599 us
  waiting for transfers between devices  200 us (33%)
  Pallas kernels  191 us (31%)
  starting transfers between devices  86.3 us (14%)
  other arithmetic  66.1 us (11%)
  local copies, waits for them, and re-layouts  28.8 us (5%)
  between operations  15.6 us (3%)
  matrix products  11 us (2%)
    ppermute x36, waiting for transfers between devices, flip(): return lax.ppermute(value, 'expert', [(i, i ^ bit) for i in range(places)])  101 us
    pallas_call x3, Pallas kernels, expert_terms(): pl.pallas_call(kernel, grid=(number,), in_specs=[pl.BlockSpec(memory_spac...  56.7 us
    ppermute x7, waiting for transfers between devices, climb(): lax.ppermute(value, 'expert', [(i, i + 4) for i in range(places - 4)])  53.9 us
    pallas_call x2, Pallas kernels, expert_sums(): pl.pallas_call(kernel, grid=(width // block,), in_specs=[whole(*a.shape)...  46.8 us
    pallas_call x2, Pallas kernels, expert_weight_grads(): pl.pallas_call(kernel, grid=(number,), in_specs=[pl.BlockSpec(memory_spac...  46.1 us
    ppermute x36, starting transfers between devices, flip(): return lax.ppermute(value, 'expert', [(i, i ^ bit) for i in range(places)])  39.7 us
    ppermute x7, starting transfers between devices, climb(): lax.ppermute(value, 'expert', [(i, i + 4) for i in range(places - 4)])  34.9 us
    ppermute x7, waiting for transfers between devices, descend(): lax.ppermute(value, 'expert', [(i + 4, i) for i in range(places - 4)])  27.6 us
  transfers between devices with their start and end apart: 66, of which 34 were waited for; matrix products, arithmetic and copies ran while one was open for 12% of the time, Pallas kernels for 26%

profile of v2, /device:TPU:0, one launch (start us, length us, event | category | flops | bytes accessed | tf_op | source)
XLA Modules:
  0.0 598.6 jit_solution(12424414340773871927)
XLA Ops:
  19.6 5.5 collective-permute-start.2
  25.7 12.1 %attention_forward.1 = (bf16[512,1536]{1,0:T(8,128)(2,1)}, bf16[512,768]{1,0:T(8,128)(2,1)}, bf16[512,128]{1,0:T(8,128)(2,1)}, bf16[512,128]{1,0:T(8,128)(2,1)},...) custom-call(s32[1]{0:T(128)} %bitcast.core_ref, bf16[512,1536]{1,0:T(8,128)(2,1)} %hidden_ref.1, ...), custom_call_target="tpu_custom_call" | custom-call | flops 1000 | bytes 1000 | tf_op jit(solution)/shard_map/attention_forward/pallas_call | solution.py:419
  48.4 5.9 collective-permute-start.7
  59.0 4.8 collective-permute-done.6.refs_9_
  64.2 5.5 collective-permute-done.8
  76.0 5.6 collective-permute-start.11
  87.4 26.7 %collective-permute-done.11 = bf16[528,1536]{1,0:T(8,128)(2,1)} collective-permute-done((bf16[528,1536]{1,0:T(8,128)(2,1)}, bf16[528,1536]{1,0:T(8,128)(2,1)}, u32[]{:S(2)}, u32[]{:S(2)}) %collective-permute-start.11) | collective-permute-done | bytes 1622048 | tf_op jit(solution)/shard_map/ppermute | solution.py:299
  114.1 9.2 %collective-permute-done.12 = bf16[528,1536]{1,0:T(8,128)(2,1)S(1)} collective-permute-done((bf16[528,1536]{1,0:T(8,128)(2,1)}, bf16[528,1536]{1,0:T(8,128)(2,1)S(1)}, u32[]{:S(2)}, u32[]{:S(2)}) %collective-permute-start.12) | collective-permute-done | bytes 1622048 | tf_op jit(solution)/shard_map/ppermute | solution.py:304
  127.7 4.5 collective-permute-start.17
  133.9 19.7 %expert_terms.3 = (bf16[1024,1152]{1,0:T(8,128)(2,1)}, bf16[1024,2304]{1,0:T(8,128)(2,1)}, bf16[3,1536,1152]{2,1,0:T(8,128)(2,1)}) custom-call(s32[1]{0:T(128)} %bitcast.7.expert_ref, bf16[528,1536]{1,0:T(8,128)(2,1)} %copy-done, bf16[528,1536]{1,0:T(8,128)(2,1)} %collective-permute-done.13.refs_1_, bf16[528,1536]{1,0:T(8,128)(2,1)} %copy-done.1, ...), custom_call_target="tpu_custom_call" | custom-call | flops 1000 | bytes 1000 | tf_op jit(solution)/shard_map/expert_terms/pallas_call | solution.py:604
  153.7 13.1 %collective-permute-done.17 = bf16[528,1536]{1,0:T(8,128)(2,1)} collective-permute-done((bf16[528,1536]{1,0:T(8,128)(2,1)}, bf16[528,1536]{1,0:T(8,128)(2,1)}, u32[]{:S(2)}, u32[]{:S(2)}) %collective-permute-start.17) | collective-permute-done | bytes 1622048 | tf_op jit(solution)/shard_map/ppermute | solution.py:299
  166.7 5.3 collective-permute-done.18
  177.9 17.6 %expert_terms.4 = (bf16[1024,384]{1,0:T(8,128)(2,1)}, bf16[1024,768]{1,0:T(8,128)(2,1)}, bf16[1024,384]{1,0:T(8,128)(2,1)}, bf16[1024,768]{1,0:T(8,128)(2,1)}, bf16[1,1536,1152]{2,1,0:T(8,128)(2,1)}) custom-call(s32[1]{0:T(128)} %bitcast.7.expert_ref, bf16[528,1536]{1,0:T(8,128)(2,1)} %copy-done, bf16[528,1536]{1,0:T(8,128)(2,1)} %collective-permute-done.13.refs_1_, ...), custom_call_target="tpu_custom_call" | custom-call | flops 1000 | bytes 1000 | tf_op jit(solution)/shard_map/expert_terms/pallas_call | solution.py:604
  195.5 17.2 %expert_weight_grads.2 = (bf16[384,1152]{1,0:T(8,128)(2,1)}, bf16[384,1152]{1,0:T(8,128)(2,1)}, bf16[384,1152]{1,0:T(8,128)(2,1)}, bf16[384,1152]{1,0:T(8,128)(2,1)}) custom-call(bf16[528,1536]{1,0:T(8,128)(2,1)} %copy-done, bf16[528,1536]{1,0:T(8,128)(2,1)} %collective-permute-done.13.refs_1_, bf16[528,1536]{1,0:T(8,128)(2,1)} %copy-done.1, ...), custom_call_target="tpu_custom_call" | custom-call | flops 1000 | bytes 1000 | tf_op jit(solution)/shard_map/expert_weight_grads/pallas_call | solution.py:734
  214.1 19.4 %expert_terms.5 = (bf16[1024,1152]{1,0:T(8,128)(2,1)}, bf16[1024,2304]{1,0:T(8,128)(2,1)}) custom-call(s32[1]{0:T(128)} %bitcast.7.expert_ref, bf16[528,1536]{1,0:T(8,128)(2,1)} %copy-done.3, bf16[528,1536]{1,0:T(8,128)(2,1)} %collective-permute-done.20.refs_5_.refs_1_, bf16[528,1536]{1,0:T(8,128)(2,1)} %copy-done.2, bf16[528,1536]{1,0:T(8,128)(2,1)} %copy-done.4, ...), custom_call_target="tpu_custom_call" | custom-call | flops 1000 | bytes 1000 | tf_op jit(solution)/shard_map/expert_terms/pallas_call | solution.py:604
  236.9 23.2 %expert_sums.2 = (f32[2,256,1536]{2,1,0:T(8,128)}, bf16[2,256,1536]{2,1,0:T(8,128)(2,1)}, f32[2,256,1536]{2,1,0:T(8,128)}, bf16[2,256,1536]{2,1,0:T(8,128)(2,1)}) custom-call(bf16[1024,1152]{1,0:T(8,128)(2,1)} %get-tuple-element.254.inner_ref.refs_10_, bf16[1024,2304]{1,0:T(8,128)(2,1)} %get-tuple-element.255.grad_ref.refs_11_, ...), custom_call_target="tpu_custom_call" | custom-call | flops 1000 | bytes 1000 | tf_op jit(solution)/shard_map/expert_sums/pallas_call | solution.py:654
  272.2 29.0 %expert_weight_grads.3 = (bf16[384,1152]{1,0:T(8,128)(2,1)}, bf16[384,1152]{1,0:T(8,128)(2,1)}, bf16[384,1152]{1,0:T(8,128)(2,1)}, bf16[384,1152]{1,0:T(8,128)(2...) custom-call(bf16[528,1536]{1,0:T(8,128)(2,1)} %copy-done, ...), custom_call_target="tpu_custom_call" | custom-call | flops 1000 | bytes 1000 | tf_op jit(solution)/shard_map/expert_weight_grads/pallas_call | solution.py:734
  307.6 6.1 %collective-permute-start.29 = (bf16[256,1536]{1,0:T(8,128)(2,1)}, bf16[256,1536]{1,0:T(8,128)(2,1)}, u32[]{:S(2)}, u32[]{:S(2)}) collective-permute-start(bf16[256,1536]{1,0:T(8,128)(2,1)} %get-tuple-element.271), channel_id=1, source_target_pairs={{0,8},{2,10},{4,12},{6,14},{8,16},{10,18},{12,20},{14,22},{16,24},... | collective-permute-start | bytes 2359304 | tf_op jit(solution)/shard_map/ppermute | solution.py:299
  315.4 23.7 %expert_sums.3 = (f32[2,256,1536]{2,1,0:T(8,128)}, bf16[2,256,1536]{2,1,0:T(8,128)(2,1)}, f32[2,256,1536]{2,1,0:T(8,128)}, bf16[2,256,1536]{2,1,0:T(8,128)(2,1)}) custom-call(bf16[1024,1152]{1,0:T(8,128)(2,1)} %get-tuple-element.272.refs_8_.inner_ref, bf16[1024,2304]{1,0:T(8,128)(2,1)} %get-tuple-element.273.refs_9_.grad_ref, ...), custom_call_target="tpu_custom_call" | custom-call | flops 1000 | bytes 1000 | tf_op jit(solution)/shard_map/expert_sums/pallas_call | solution.py:654
  361.0 11.8 %collective-permute-done.34 = bf16[256,1536]{1,0:T(8,128)(2,1)} collective-permute-done((bf16[256,1536]{1,0:T(8,128)(2,1)}, bf16[256,1536]{1,0:T(8,128)(2,1)}, u32[]{:S(2)}, u32[]{:S(2)}) %collective-permute-start.34) | collective-permute-done | bytes 786464 | tf_op jit(solution)/shard_map/ppermute | solution.py:299
  372.8 5.1 collective-permute-done.33
  385.9 4.5 convolution_convert_fusion.2.gm_ref
  400.9 10.4 %attention_backward.1 = bf16[512,1024]{1,0:T(8,128)(2,1)} custom-call(bf16[512,768]{1,0:T(8,128)(2,1)} %convolution_convert_fusion.2.gm_ref, bf16[512,768]{1,0:T(8,128)(2,1)} %get-tuple-element.312.query_ref, bf16[512,128]{1,0:T(8,128)(2,1)} %get-tuple-element.313.key_ref, bf16[512,128]{1,0:T(8,128)(2,1)} %get-tuple-element.314.value_ref, ...), custom_call_target="tpu_custom_call" | custom-call | flops 1000 | bytes 1000 | tf_op jit(solution)/shard_map/attention_backward/pallas_call | solution.py:476
  427.5 17.1 %collective-permute-done.42 = bf16[384,1024]{1,0:T(8,128)(2,1)S(1)} collective-permute-done((bf16[384,1024]{1,0:T(8,128)(2,1)S(1)}, bf16[384,1024]{1,0:T(8,128)(2,1)S(1)}, u32[]{:S(2)}, u32[]{:S(2)}) %collective-permute-start.42) | collective-permute-done | bytes 786464 | tf_op jit(solution)/shard_map/ppermute | solution.py:294
  452.9 8.5 %collective-permute-done.48 = bf16[192,1024]{1,0:T(8,128)(2,1)} collective-permute-done((bf16[192,1024]{1,0:T(8,128)(2,1)}, bf16[192,1024]{1,0:T(8,128)(2,1)}, u32[]{:S(2)}, u32[]{:S(2)}) %collective-permute-start.48) | collective-permute-done | bytes 393248 | tf_op jit(solution)/shard_map/ppermute | solution.py:294
  463.8 5.3 maximum_select_fusion
  475.3 33.8 %collective-permute-done.51.refs_16_ = bf16[768,1152]{1,0:T(8,128)(2,1)} collective-permute-done((bf16[768,1152]{1,0:T(8,128)(2,1)}, bf16[768,1152]{1,0:T(8,128)(2,1)}, u32[]{:S(2)}, u32[]{:S(2)}) %collective-permute-start.51) | collective-permute-done | bytes 1769504 | tf_op jit(solution)/shard_map/ppermute | solution.py:294
  509.4 18.7 %own_weight_grads.1 = (f32[1,1536,384]{2,1,0:T(8,128)}, f32[1,1536,384]{2,1,0:T(8,128)}, f32[1,384,1536]{2,1,0:T(8,128)}) custom-call(bf16[528,1536]{1,0:T(8,128)(2,1)} %copy-done, bf16[528,1536]{1,0:T(8,128)(2,1)} %collective-permute-done.13.refs_1_, bf16[528,1536]{1,0:T(8,128)(2,1)} %copy-done.1, bf16[528,1536]{1,0:T(8,128)(2,1)} %collective-permute-done.14.refs_3_, ...), custom_call_target="tpu_custom_call" | custom-call | flops 1000 | bytes 1000 | tf_op jit(solution)/shard_map/own_weight_grads/pallas_call | solution.py:794
  528.1 4.0 all-reduce.5.cloned.1.call-done
  547.3 10.6 %collective-permute-done.60 = bf16[96,1536]{1,0:T(8,128)(2,1)S(1)} collective-permute-done((bf16[96,1536]{1,0:T(8,128)(2,1)S(1)}, bf16[96,1536]{1,0:T(8,128)(2,1)S(1)}, u32[]{:S(2)}, u32[]{:S(2)}) %collective-permute-start.60) | collective-permute-done | bytes 294944 | tf_op jit(solution)/shard_map/ppermute | solution.py:294
  562.8 7.7 %collective-permute-done.63 = bf16[192,1536]{1,0:T(8,128)(2,1)S(1)} collective-permute-done((bf16[192,1536]{1,0:T(8,128)(2,1)S(1)}, bf16[192,1536]{1,0:T(8,128)(2,1)S(1)}, u32[]{:S(2)}, u32[]{:S(2)}) %collective-permute-start.63) | collective-permute-done | bytes 589856 | tf_op jit(solution)/shard_map/ppermute | solution.py:294
  577.6 7.6 %collective-permute-done.59 = bf16[384,1024]{1,0:T(8,128)(2,1)S(1)} collective-permute-done((bf16[384,1024]{1,0:T(8,128)(2,1)S(1)}, bf16[384,1024]{1,0:T(8,128)(2,1)S(1)}, u32[]{:S(2)}, u32[]{:S(2)}) %collective-permute-start.59) | collective-permute-done | bytes 786464 | tf_op jit(solution)/shard_map/ppermute | solution.py:294
  (309 shorter events, 184.2 us)
Async XLA Ops:
  7.2 461.9 %reduce-scatter.2.cloned.1.call-start = ((), (), s32[]{:S(2)}) async-start(), calls=%async_computation.1 | async-start | bytes 3932160 | tf_op jit(solution)/shard_map/reduce_scatter | solution.py:956
  11.6 29.9 %collective-permute-start.1 = (bf16[384,1152]{1,0:T(8,128)(2,1)S(1)}, bf16[384,1152]{1,0:T(8,128)(2,1)S(1)}, u32[]{:S(2)}, u32[]{:S(2)}) collective-permute-start(bf16[384,1152]{1,0:T(8,128)(2,1)S(1)} %get-tuple-element.362), channel_id=1, source_target_pairs={{0,4},{2,6},{4,0},{6,2},{8,12},{10,14},{12,8},{14,10},{16,20},{18,... | collective-permute-start | bytes 2654216 | tf_op jit(solution)/shard_map/ppermute | solution.py:294
  14.6 27.0 %collective-permute-start = (bf16[384,1152]{1,0:T(8,128)(2,1)S(1)}, bf16[384,1152]{1,0:T(8,128)(2,1)}, u32[]{:S(2)}, u32[]{:S(2)}) collective-permute-start(bf16[384,1152]{1,0:T(8,128)(2,1)S(1)} %get-tuple-element.362), channel_id=1, source_target_pairs={{0,2},{2,0},{4,6},{6,4},{8,10},{10,8},{12,14},{14,12},{16,18},{18,... | collective-permute-start | bytes 2654216 | tf_op jit(solution)/shard_map/ppermute | solution.py:294
  41.6 22.3 %collective-permute-start.6 = (bf16[384,1152]{1,0:T(8,128)(2,1)}, bf16[384,1152]{1,0:T(8,128)(2,1)S(1)}, u32[]{:S(2)}, u32[]{:S(2)}) collective-permute-start(bf16[384,1152]{1,0:T(8,128)(2,1)} %get-tuple-element.183), channel_id=1, source_target_pairs={{0,4},{2,6},{4,0},{6,2},{8,12},{10,14},{12,8},{14,10},{16,20},{18,... | collective-permute-start | bytes 2654216 | tf_op jit(solution)/shard_map/ppermute | solution.py:294
  47.1 22.5 %collective-permute-start.8 = (bf16[256,1536]{1,0:T(8,128)(2,1)}, bf16[256,1536]{1,0:T(8,128)(2,1)}, u32[]{:S(2)}, u32[]{:S(2)}) collective-permute-start(bf16[256,1536]{1,0:T(8,128)(2,1)} %multiply_convert_fusion), channel_id=1, source_target_pairs={{8,0},{10,2},{12,4},{14,6},{16,8},{18,10},{20,12},{22,14},{24,16},... | collective-permute-start | bytes 2359304 | tf_op jit(solution)/shard_map/ppermute | solution.py:304
  48.4 22.4 %collective-permute-start.7 = (bf16[256,1536]{1,0:T(8,128)(2,1)}, bf16[256,1536]{1,0:T(8,128)(2,1)}, u32[]{:S(2)}, u32[]{:S(2)}) collective-permute-start(bf16[256,1536]{1,0:T(8,128)(2,1)} %multiply_convert_fusion), channel_id=1, source_target_pairs={{0,8},{2,10},{4,12},{6,14},{8,16},{10,18},{12,20},{14,22},{16,24},... | collective-permute-start | bytes 2359304 | tf_op jit(solution)/shard_map/ppermute | solution.py:299
  55.6 27.7 %collective-permute-start.13 = (bf16[528,1536]{1,0:T(8,128)(2,1)S(1)}, bf16[528,1536]{1,0:T(8,128)(2,1)}, u32[]{:S(2)}, u32[]{:S(2)}) collective-permute-start(bf16[528,1536]{1,0:T(8,128)(2,1)S(1)} %pad_maximum_fusion.7.refs_0_), channel_id=1, source_target_pairs={{0,1},{1,0},{2,3},{3,2},{4,5},{5,4},{6,7},{7,6},{8,9},{9,8},{10,11... | collective-permute-start | bytes 4866056 | tf_op jit(solution)/shard_map/ppermute | solution.py:289
  74.7 48.6 %collective-permute-start.10 = (bf16[768,1152]{1,0:T(8,128)(2,1)}, bf16[768,1152]{1,0:T(8,128)(2,1)}, u32[]{:S(2)}, u32[]{:S(2)}) collective-permute-start(bf16[768,1152]{1,0:T(8,128)(2,1)} %slice.77), channel_id=1, source_target_pairs={{0,4},{2,6},{4,0},{6,2},{8,12},{10,14},{12,8},{14,10},{16,20},{18,... | collective-permute-start | bytes 5308424 | tf_op jit(solution)/shard_map/ppermute | solution.py:294
  75.2 48.1 %collective-permute-start.9 = (bf16[768,1152]{1,0:T(8,128)(2,1)}, bf16[768,1152]{1,0:T(8,128)(2,1)}, u32[]{:S(2)}, u32[]{:S(2)}) collective-permute-start(bf16[768,1152]{1,0:T(8,128)(2,1)} %slice.77), channel_id=1, source_target_pairs={{0,2},{2,0},{4,6},{6,4},{8,10},{10,8},{12,14},{14,12},{16,18},{18,... | collective-permute-start | bytes 5308424 | tf_op jit(solution)/shard_map/ppermute | solution.py:294
  76.0 38.0 %collective-permute-start.11 = (bf16[528,1536]{1,0:T(8,128)(2,1)}, bf16[528,1536]{1,0:T(8,128)(2,1)}, u32[]{:S(2)}, u32[]{:S(2)}) collective-permute-start(bf16[528,1536]{1,0:T(8,128)(2,1)} %get-tuple-element.192), channel_id=1, source_target_pairs={{0,8},{2,10},{4,12},{6,14},{8,16},{10,18},{12,20},{14,22},{16,24},... | collective-permute-start | bytes 4866056 | tf_op jit(solution)/shard_map/ppermute | solution.py:299
  83.3 39.9 %collective-permute-start.12 = (bf16[528,1536]{1,0:T(8,128)(2,1)}, bf16[528,1536]{1,0:T(8,128)(2,1)S(1)}, u32[]{:S(2)}, u32[]{:S(2)}) collective-permute-start(bf16[528,1536]{1,0:T(8,128)(2,1)} %get-tuple-element.193), channel_id=1, source_target_pairs={{8,0},{10,2},{12,4},{14,6},{16,8},{18,10},{20,12},{22,14},{24,16},... | collective-permute-start | bytes 4866056 | tf_op jit(solution)/shard_map/ppermute | solution.py:304
  123.2 48.8 %collective-permute-start.15 = (bf16[768,1152]{1,0:T(8,128)(2,1)}, bf16[768,1152]{1,0:T(8,128)(2,1)}, u32[]{:S(2)}, u32[]{:S(2)}) collective-permute-start(bf16[768,1152]{1,0:T(8,128)(2,1)} %pad_maximum_fusion.2), channel_id=1, source_target_pairs={{0,2},{2,0},{4,6},{6,4},{8,10},{10,8},{12,14},{14,12},{16,18},{18,... | collective-permute-start | bytes 5308424 | tf_op jit(solution)/shard_map/ppermute | solution.py:294
  124.5 47.6 %collective-permute-start.16 = (bf16[768,1152]{1,0:T(8,128)(2,1)}, bf16[768,1152]{1,0:T(8,128)(2,1)}, u32[]{:S(2)}, u32[]{:S(2)}) collective-permute-start(bf16[768,1152]{1,0:T(8,128)(2,1)} %collective-permute-done.9.refs_7_), channel_id=1, source_target_pairs={{0,4},{2,6},{4,0},{6,2},{8,12},{10,14},{12,8},{14,10},{16,20},{18,... | collective-permute-start | bytes 5308424 | tf_op jit(solution)/shard_map/ppermute | solution.py:294
  127.6 26.0 %collective-permute-start.19 = (bf16[528,1536]{1,0:T(8,128)(2,1)S(1)}, bf16[528,1536]{1,0:T(8,128)(2,1)S(1)}, u32[]{:S(2)}, u32[]{:S(2)}) collective-permute-start(bf16[528,1536]{1,0:T(8,128)(2,1)S(1)} %select_select_fusion.1.refs_6_.refs_2_), channel_id=1, source_target_pairs={{0,1},{1,0},{2,3},{3,2},{4,5},{5,4},{6,7},{7,6},{8,9},{9,8},{10,11... | collective-permute-start | bytes 4866056 | tf_op jit(solution)/shard_map/ppermute | solution.py:289
  127.7 39.0 %collective-permute-start.17 = (bf16[528,1536]{1,0:T(8,128)(2,1)}, bf16[528,1536]{1,0:T(8,128)(2,1)}, u32[]{:S(2)}, u32[]{:S(2)}) collective-permute-start(bf16[528,1536]{1,0:T(8,128)(2,1)} %collective-permute-done.11), channel_id=1, source_target_pairs={{0,8},{2,10},{4,12},{6,14},{8,16},{10,18},{12,20},{14,22},{16,24},... | collective-permute-start | bytes 4866056 | tf_op jit(solution)/shard_map/ppermute | solution.py:299
  132.2 39.8 %collective-permute-start.18 = (bf16[528,1536]{1,0:T(8,128)(2,1)}, bf16[528,1536]{1,0:T(8,128)(2,1)}, u32[]{:S(2)}, u32[]{:S(2)}) collective-permute-start(bf16[528,1536]{1,0:T(8,128)(2,1)} %copy-done.9), channel_id=1, source_target_pairs={{8,0},{10,2},{12,4},{14,6},{16,8},{18,10},{20,12},{22,14},{24,16},... | collective-permute-start | bytes 4866056 | tf_op jit(solution)/shard_map/ppermute | solution.py:304
  234.9 25.2 %collective-permute-start.23 = (bf16[384,1152]{1,0:T(8,128)(2,1)}, bf16[384,1152]{1,0:T(8,128)(2,1)S(1)}, u32[]{:S(2)}, u32[]{:S(2)}) collective-permute-start(bf16[384,1152]{1,0:T(8,128)(2,1)} %get-tuple-element.240), channel_id=1, source_target_pairs={{0,2},{2,0},{4,6},{6,4},{8,10},{10,8},{12,14},{14,12},{16,18},{18,... | collective-permute-start | bytes 2654216 | tf_op jit(solution)/shard_map/ppermute | solution.py:294
  236.4 23.7 %collective-permute-start.24 = (bf16[384,1152]{1,0:T(8,128)(2,1)}, bf16[384,1152]{1,0:T(8,128)(2,1)S(1)}, u32[]{:S(2)}, u32[]{:S(2)}) collective-permute-start(bf16[384,1152]{1,0:T(8,128)(2,1)} %get-tuple-element.242), channel_id=1, source_target_pairs={{0,4},{2,6},{4,0},{6,2},{8,12},{10,14},{12,8},{14,10},{16,20},{18,... | collective-permute-start | bytes 2654216 | tf_op jit(solution)/shard_map/ppermute | solution.py:294
  261.4 52.3 %collective-permute-start.36 = (bf16[2,256,1536]{2,1,0:T(8,128)(2,1)}, bf16[2,256,1536]{2,1,0:T(8,128)(2,1)S(1)}, u32[]{:S(2)}, u32[]{:S(2)}) collective-permute-start(bf16[2,256,1536]{2,1,0:T(8,128)(2,1)} %get-tuple-element.295), channel_id=1, source_target_pairs={{0,1},{1,0},{2,3},{3,2},{4,5},{5,4},{6,7},{7,6},{8,9},{9,8},{10,11... | collective-permute-start | bytes 4718600 | tf_op jit(solution)/shard_map/ppermute | solution.py:289
  267.5 33.6 %collective-permute-start.27 = (bf16[256,1536]{1,0:T(8,128)(2,1)S(1)}, bf16[256,1536]{1,0:T(8,128)(2,1)}, u32[]{:S(2)}, u32[]{:S(2)}) collective-permute-start(bf16[256,1536]{1,0:T(8,128)(2,1)S(1)} %slice_bitcast_fusion.2), channel_id=1, source_target_pairs={{0,8},{2,10},{4,12},{6,14},{8,16},{10,18},{12,20},{14,22},{16,24},... | collective-permute-start | bytes 2359304 | tf_op jit(solution)/shard_map/ppermute | solution.py:299
  270.9 30.3 %collective-permute-start.26 = (bf16[256,1536]{1,0:T(8,128)(2,1)S(1)}, bf16[256,1536]{1,0:T(8,128)(2,1)}, u32[]{:S(2)}, u32[]{:S(2)}) collective-permute-start(bf16[256,1536]{1,0:T(8,128)(2,1)S(1)} %slice_bitcast_fusion.2), channel_id=1, source_target_pairs={{8,0},{10,2},{12,4},{14,6},{16,8},{18,10},{20,12},{22,14},{24,16},... | collective-permute-start | bytes 2359304 | tf_op jit(solution)/shard_map/ppermute | solution.py:304
  301.2 37.9 %collective-permute-start.30 = (bf16[384,1152]{1,0:T(8,128)(2,1)}, bf16[384,1152]{1,0:T(8,128)(2,1)}, u32[]{:S(2)}, u32[]{:S(2)}) collective-permute-start(bf16[384,1152]{1,0:T(8,128)(2,1)} %get-tuple-element.280), channel_id=1, source_target_pairs={{0,2},{2,0},{4,6},{6,4},{8,10},{10,8},{12,14},{14,12},{16,18},{18,... | collective-permute-start | bytes 2654216 | tf_op jit(solution)/shard_map/ppermute | solution.py:294
  302.2 37.0 %collective-permute-start.31 = (bf16[384,1152]{1,0:T(8,128)(2,1)}, bf16[384,1152]{1,0:T(8,128)(2,1)}, u32[]{:S(2)}, u32[]{:S(2)}) collective-permute-start(bf16[384,1152]{1,0:T(8,128)(2,1)} %get-tuple-element.281), channel_id=1, source_target_pairs={{0,4},{2,6},{4,0},{6,2},{8,12},{10,14},{12,8},{14,10},{16,20},{18,... | collective-permute-start | bytes 2654216 | tf_op jit(solution)/shard_map/ppermute | solution.py:294
  306.3 32.8 %collective-permute-start.28 = (bf16[256,1536]{1,0:T(8,128)(2,1)}, bf16[256,1536]{1,0:T(8,128)(2,1)}, u32[]{:S(2)}, u32[]{:S(2)}) collective-permute-start(bf16[256,1536]{1,0:T(8,128)(2,1)} %get-tuple-element.270), channel_id=1, source_target_pairs={{8,0},{10,2},{12,4},{14,6},{16,8},{18,10},{20,12},{22,14},{24,16},... | collective-permute-start | bytes 2359304 | tf_op jit(solution)/shard_map/ppermute | solution.py:304
  307.6 31.5 %collective-permute-start.29 = (bf16[256,1536]{1,0:T(8,128)(2,1)}, bf16[256,1536]{1,0:T(8,128)(2,1)}, u32[]{:S(2)}, u32[]{:S(2)}) collective-permute-start(bf16[256,1536]{1,0:T(8,128)(2,1)} %get-tuple-element.271), channel_id=1, source_target_pairs={{0,8},{2,10},{4,12},{6,14},{8,16},{10,18},{12,20},{14,22},{16,24},... | collective-permute-start | bytes 2359304 | tf_op jit(solution)/shard_map/ppermute | solution.py:299
  400.6 131.4 %all-reduce.5.cloned.1.call-start = ((), (), s32[]{:S(2)}) async-start(), calls=%async_computation.2 | async-start | bytes 2818048 | tf_op jit(solution)/shard_map/psum | solution.py:1006
  469.1 40.0 %collective-permute-start.51 = (bf16[768,1152]{1,0:T(8,128)(2,1)}, bf16[768,1152]{1,0:T(8,128)(2,1)}, u32[]{:S(2)}, u32[]{:S(2)}) collective-permute-start(bf16[768,1152]{1,0:T(8,128)(2,1)} %pad_maximum_fusion.3), channel_id=1, source_target_pairs={{0,4},{2,6},{4,0},{6,2},{8,12},{10,14},{12,8},{14,10},{16,20},{18,... | collective-permute-start | bytes 5308424 | tf_op jit(solution)/shard_map/ppermute | solution.py:294
  469.7 39.7 %collective-permute-start.52 = (bf16[768,1152]{1,0:T(8,128)(2,1)}, bf16[768,1152]{1,0:T(8,128)(2,1)}, u32[]{:S(2)}, u32[]{:S(2)}) collective-permute-start(bf16[768,1152]{1,0:T(8,128)(2,1)} %pad_maximum_fusion.4), channel_id=1, source_target_pairs={{0,2},{2,0},{4,6},{6,4},{8,10},{10,8},{12,14},{14,12},{16,18},{18,... | collective-permute-start | bytes 5308424 | tf_op jit(solution)/shard_map/ppermute | solution.py:294
  539.5 23.0 %collective-permute-start.56 = (bf16[192,1024]{1,0:T(8,128)(2,1)S(1)}, bf16[192,1024]{1,0:T(8,128)(2,1)S(1)}, u32[]{:S(2)}, u32[]{:S(2)}) collective-permute-start(bf16[192,1024]{1,0:T(8,128)(2,1)S(1)} %get-tuple-element.377), channel_id=1, source_target_pairs={{0,4},{2,6},{4,0},{6,2},{8,12},{10,14},{12,8},{14,10},{16,20},{18,... | collective-permute-start | bytes 1179656 | tf_op jit(solution)/shard_map/ppermute | solution.py:294
  545.6 25.0 %collective-permute-start.63 = (bf16[192,1536]{1,0:T(8,128)(2,1)S(1)}, bf16[192,1536]{1,0:T(8,128)(2,1)S(1)}, u32[]{:S(2)}, u32[]{:S(2)}) collective-permute-start(bf16[192,1536]{1,0:T(8,128)(2,1)S(1)} %maximum_select_fusion.10), channel_id=1, source_target_pairs={{0,4},{2,6},{4,0},{6,2},{8,12},{10,14},{12,8},{14,10},{16,20},{18,... | collective-permute-start | bytes 1769480 | tf_op jit(solution)/shard_map/ppermute | solution.py:294
  561.1 24.1 %collective-permute-start.59 = (bf16[384,1024]{1,0:T(8,128)(2,1)S(1)}, bf16[384,1024]{1,0:T(8,128)(2,1)S(1)}, u32[]{:S(2)}, u32[]{:S(2)}) collective-permute-start(bf16[384,1024]{1,0:T(8,128)(2,1)S(1)} %maximum_select_fusion.8), channel_id=1, source_target_pairs={{0,4},{2,6},{4,0},{6,2},{8,12},{10,14},{12,8},{14,10},{16,20},{18,... | collective-permute-start | bytes 2359304 | tf_op jit(solution)/shard_map/ppermute | solution.py:294
  562.7 23.2 %collective-permute-start.57 = (bf16[384,1024]{1,0:T(8,128)(2,1)S(1)}, bf16[384,1024]{1,0:T(8,128)(2,1)S(1)}, u32[]{:S(2)}, u32[]{:S(2)}) collective-permute-start(bf16[384,1024]{1,0:T(8,128)(2,1)S(1)} %maximum_select_fusion.7), channel_id=1, source_target_pairs={{0,2},{2,0},{4,6},{6,4},{8,10},{10,8},{12,14},{14,12},{16,18},{18,... | collective-permute-start | bytes 2359304 | tf_op jit(solution)/shard_map/ppermute | solution.py:294
  (84 other events, 805.5 us)
Sparse Core Ops, SparseCore 0:
  400.7 57.5 reduce-scatter.1
  471.1 60.9 all-reduce.4

commit v3 on v2

--- a/solution.py
+++ b/solution.py
@@ -335,12 +335,39 @@
     return left, right
 
 
-def plane_gather(left, right, bit_x, bit_y):
-    left = ordered(left, flip(left, 2), bit_y)
-    right = ordered(right, flip(right, 1), bit_x)
-    left = ordered(left, flip(left, 1), bit_x)
-    right = ordered(right, flip(right, 2), bit_y)
-    return jnp.concatenate([left, right], axis=0)
+def plane_gather_first(left, right, bit_x, bit_y):
+    return ordered(left, flip(left, 2), bit_y), ordered(right, flip(right, 1), bit_x)
+
+
+def plane_gather_second(halves, bit_x, bit_y):
+    left, right = halves
+    return left, flip(left, 1), right, flip(right, 2)
+
+
+def lay_out(bits, pieces, widths):
+    rows, columns = pieces[0].shape
+    def kernel(bits_ref, *refs):
+        sources, results = refs[:4], refs[4:]
+        for side in range(2):
+            bit = bits_ref[side]
+            for n in range(2):
+                value = sources[2 * side + n][...].astype(jnp.float32)
+                place = pl.multiple_of((2 * side + jnp.where(bit == n, 0, 1)) * rows, rows)
+                start = 0
+                for result, size in zip(results, widths, strict=True):
+                    result[pl.ds(place, rows), :] = value[:, start : start + size]
+                    start += size
+
+    return pl.pallas_call(
+        kernel,
+        in_specs=[pl.BlockSpec(memory_space=pltpu.SMEM)]
+        + [pl.BlockSpec(memory_space=pltpu.VMEM)] * 4,
+        out_specs=[pl.BlockSpec(memory_space=pltpu.VMEM)] * len(widths),
+        out_shape=[jax.ShapeDtypeStruct((4 * rows, size), jnp.float32) for size in widths],
+        compiler_params=pltpu.CompilerParams(vmem_limit_bytes=VMEM_BYTES),
+        cost_estimate=small_cost(),
+        name="lay_out",
+    )(bits, *pieces)
 
 
 def rotary_tables(tokens):
@@ -431,13 +458,16 @@
     )(core, *operands)
 
 
-def attention_backward(grad_mixed, queries, keys, values, cosine, sine):
+def attention_backward(grad_attn, w_output, queries, keys, values, cosine, sine):
     tokens, local = queries.shape
     half = tokens // 2
     heads = local // HD
     scale_factor = 1.0 / math.sqrt(HD)
 
-    def kernel(gm_ref, query_ref, key_ref, value_ref, cos_ref, sin_ref, grad_ref, gk_ref, gv_ref):
+    def kernel(
+        ga_ref, wo_ref, query_ref, key_ref, value_ref, cos_ref, sin_ref, grad_ref, gk_ref, gv_ref, gm_ref
+    ):
+        gm_ref[...] = contract_cols(ga_ref[...], wo_ref[...]).astype(jnp.bfloat16)
         for block in range(2):
             rows = pl.ds(block * half, half)
             seen = pl.ds(0, (block + 1) * half)
@@ -476,15 +506,16 @@
     return pl.pallas_call(
         kernel,
         out_shape=jax.ShapeDtypeStruct((tokens, local + 2 * HD), jnp.bfloat16),
-        in_specs=[pl.BlockSpec(memory_space=pltpu.VMEM)] * 6,
+        in_specs=[pl.BlockSpec(memory_space=pltpu.VMEM)] * 7,
         out_specs=pl.BlockSpec(memory_space=pltpu.VMEM),
-        scratch_shapes=[pltpu.VMEM((tokens, HD), jnp.float32)] * 2,
+        scratch_shapes=[pltpu.VMEM((tokens, HD), jnp.float32)] * 2
+        + [pltpu.VMEM((tokens, local), jnp.bfloat16)],
         compiler_params=pltpu.CompilerParams(vmem_limit_bytes=VMEM_BYTES),
         cost_estimate=small_cost(
             flops=10 * 10**9, bytes_accessed=4 * 10**6, transcendentals=2 * 10**6
         ),
         name="attention_backward",
-    )(grad_mixed, queries, keys, values, cosine, sine)
+    )(grad_attn, w_output, queries, keys, values, cosine, sine)
 
 
 def expert_weights_of(expert_ref, packs, half):
@@ -500,61 +531,61 @@
     return jnp.concatenate(sides, axis=0)
 
 
-def expert_terms(expert, sequences, counts, pieces, first, keep):
+def expert_terms(expert, joins, pieces, first, keep):
+    sequences = [sequence for own, _ in joins for sequence in own]
     width = sequences[0][0].shape[1]
     half = sequences[0][0].shape[0] // 2 // 128 * 128
-    stacked = not isinstance(pieces, list)
-    number = pieces.shape[0] if stacked else len(pieces)
-    flat_pieces = [pieces] if stacked else [piece for own in pieces for piece in own]
-    columns = flat_pieces[0].shape[-1]
+    number = len(pieces)
+    arrays = [array for own in pieces for array, _ in own]
+    columns = arrays[0].shape[-1]
     hidden = columns // 3
     tokens = 2 * half
     total = len(sequences)
     flat = [array for sequence in sequences for array in sequence]
 
     loads = []
-    if stacked:
-        loads = [[(0, e, 0, width)] for e in range(number)]
-    else:
-        n = 0
-        for own in pieces:
-            loads.append([])
-            place = 0
-            for piece in own:
-                loads[-1].append((n, None, place, piece.shape[0]))
-                place += piece.shape[0]
-                n += 1
-    copy_count = sum(len(own) for own in loads)
+    n = 0
+    for own in pieces:
+        loads.append([])
+        place = 0
+        for array, index in own:
+            loads[-1].append((n, index, place, array.shape[-2]))
+            place += array.shape[-2]
+            n += 1
+    copy_count = n
 
     def kernel(expert_ref, *refs):
         sources, refs = refs[: len(flat)], refs[len(flat) :]
-        piece_refs, refs = refs[: len(flat_pieces)], refs[len(flat_pieces) :]
-        results, (w_ref, gate_all, semaphores) = refs[:-3], refs[-3:]
+        piece_refs, refs = refs[: len(arrays)], refs[len(arrays) :]
+        results, (w_ref, packs, gate_all, semaphores) = refs[:-4], refs[-4:]
         e = pl.program_id(0)
 
         def copies_of(one):
-            n = sum(len(own) for own in loads[:one])
             for which, index, place, rows in loads[one]:
                 source = piece_refs[which] if index is None else piece_refs[which].at[index]
                 yield pltpu.make_async_copy(
-                    source, w_ref.at[one, pl.ds(place, rows), :], semaphores.at[n]
+                    source, w_ref.at[one, pl.ds(place, rows), :], semaphores.at[which]
                 )
-                n += 1
 
         def kept(one):
             return pltpu.make_async_copy(
                 w_ref.at[one], results[-1].at[one], semaphores.at[copy_count + one]
             )
 
+        def pack_copy(n):
+            return pltpu.make_async_copy(
+                sources[n], packs.at[n], semaphores.at[copy_count + number + n]
+            )
+
         @pl.when(e == 0)
         def _():
-            for one in range(number):
+            for copy in copies_of(0):
+                copy.start()
+            for n in range(2 * total):
+                pack_copy(n).start()
+            for one in range(1, number):
                 for copy in copies_of(one):
                     copy.start()
-            for s in range(total):
-                gate_all[s * tokens : (s + 1) * tokens, :] = expert_weights_of(
-                    expert_ref, sources[2 * s : 2 * s + 2], half
-                )
 
         for one in range(number):
 
@@ -567,23 +598,42 @@
 
         lanes = lax.broadcasted_iota(jnp.int32, (half, 128), 1)
         n = 0
-        for joined, count in enumerate(counts):
-            inner_ref, grad_ref = results[2 * joined : 2 * joined + 2]
-            for s in range(count):
-                for side in range(2):
-                    pack = sources[2 * n + side]
-                    here = pl.ds(s * tokens + side * half, half)
-                    gate = gate_all[n * tokens + side * half : n * tokens + (side + 1) * half, :]
-                    weight = jnp.sum(jnp.where(lanes == e + first, gate, 0.0), axis=1, keepdims=True)
-                    both = dot(pack[:half, :], w_ref[e, :, : 2 * hidden])
-                    grad_inner = dot(pack[half : 2 * half, :], w_ref[e, :, 2 * hidden :]) * weight
-                    gate_pre, up_pre = both[:, :hidden], both[:, hidden:]
-                    sigmoid = jax.nn.sigmoid(gate_pre)
-                    activated = gate_pre * sigmoid
-                    grad_gate = grad_inner * up_pre * sigmoid * (1.0 + gate_pre * (1.0 - sigmoid))
-                    grad_ref[here, :hidden] = grad_gate.astype(jnp.bfloat16)
-                    grad_ref[here, hidden:] = (grad_inner * activated).astype(jnp.bfloat16)
-                    inner_ref[here, :] = (activated * up_pre * weight).astype(jnp.bfloat16)
+        for join, (own, start) in enumerate(joins):
+            inner_ref, grad_ref = results[2 * join : 2 * join + 2]
+            for s in range(len(own)):
+
+                @pl.when(e == 0)
+                def _(n=n):
+                    for side in range(2):
+                        pack_copy(2 * n + side).wait()
+                    gate_all[n * tokens : (n + 1) * tokens, :] = expert_weights_of(
+                        expert_ref, [packs.at[2 * n], packs.at[2 * n + 1]], half
+                    )
+
+                def run(n=n, s=s, inner_ref=inner_ref, grad_ref=grad_ref):
+                    for side in range(2):
+                        pack = packs.at[2 * n + side]
+                        here = pl.ds(s * tokens + side * half, half)
+                        gate = gate_all[n * tokens + side * half : n * tokens + (side + 1) * half, :]
+                        weight = jnp.sum(
+                            jnp.where(lanes == e + first, gate, 0.0), axis=1, keepdims=True
+                        )
+                        both = dot(pack[:half, :], w_ref[e, :, : 2 * hidden])
+                        grad_inner = dot(pack[half : 2 * half, :], w_ref[e, :, 2 * hidden :]) * weight
+                        gate_pre, up_pre = both[:, :hidden], both[:, hidden:]
+                        sigmoid = jax.nn.sigmoid(gate_pre)
+                        activated = gate_pre * sigmoid
+                        grad_gate = (
+                            grad_inner * up_pre * sigmoid * (1.0 + gate_pre * (1.0 - sigmoid))
+                        )
+                        grad_ref[here, :hidden] = grad_gate.astype(jnp.bfloat16)
+                        grad_ref[here, hidden:] = (grad_inner * activated).astype(jnp.bfloat16)
+                        inner_ref[here, :] = (activated * up_pre * weight).astype(jnp.bfloat16)
+
+                if start:
+                    pl.when(e >= start)(run)
+                else:
+                    run()
                 n += 1
 
         if keep:
@@ -594,10 +644,16 @@
                     kept(one).wait()
 
     out_specs, out_shape = [], []
-    for count in counts:
+    for own, start in joins:
         for size in (hidden, 2 * hidden):
-            out_specs.append(pl.BlockSpec((count * tokens, size), lambda e: (0, e)))
-            out_shape.append(jax.ShapeDtypeStruct((count * tokens, number * size), jnp.bfloat16))
+            out_specs.append(
+                pl.BlockSpec(
+                    (len(own) * tokens, size), lambda e, start=start: (0, jnp.maximum(e - start, 0))
+                )
+            )
+            out_shape.append(
+                jax.ShapeDtypeStruct((len(own) * tokens, (number - start) * size), jnp.bfloat16)
+            )
     if keep:
         out_specs.append(pl.BlockSpec(memory_space=pl.ANY))
         out_shape.append(jax.ShapeDtypeStruct((number, width, columns), jnp.bfloat16))
@@ -605,70 +661,71 @@
         kernel,
         grid=(number,),
         in_specs=[pl.BlockSpec(memory_space=pltpu.SMEM)]
-        + [whole(*array.shape) for array in flat]
-        + [pl.BlockSpec(memory_space=pl.ANY)] * len(flat_pieces),
+        + [pl.BlockSpec(memory_space=pl.ANY)] * (len(flat) + len(arrays)),
         out_specs=out_specs,
         out_shape=out_shape,
         scratch_shapes=[
             pltpu.VMEM((number, width, columns), jnp.bfloat16),
+            pltpu.VMEM((2 * total, *flat[0].shape), jnp.bfloat16),
             pltpu.VMEM((total * tokens, 128), jnp.float32),
-            pltpu.SemaphoreType.DMA((copy_count + number,)),
+            pltpu.SemaphoreType.DMA((copy_count + number + 2 * total,)),
         ],
         compiler_params=pltpu.CompilerParams(vmem_limit_bytes=VMEM_BYTES),
-        cost_estimate=small_cost(
-            flops=total * number * 6 * tokens * width * hidden,
-            bytes_accessed=(total + number) * 4 * 10**6,
-            transcendentals=total * number * tokens * hidden,
-        ),
+        cost_estimate=small_cost(),
         name="expert_terms",
-    )(expert, *flat, *flat_pieces)
-    terms = [tuple(results[2 * n : 2 * n + 2]) for n in range(len(counts))]
+    )(expert, *flat, *arrays)
+    terms = [tuple(results[2 * n : 2 * n + 2]) for n in range(len(joins))]
     return (*terms, results[-1]) if keep else tuple(terms)
 
 
-def expert_sums(near, far, near_weights, far_weights, half):
-    rows, columns = near[0].shape
-    number, width = near_weights.shape[:2]
-    hidden = columns // number
-    count = rows // (2 * half)
+def expert_sums(groups, weights, half):
+    number, width = weights.shape[:2]
+    hidden = weights.shape[2] // 3
+    counts = [group[0][0].shape[0] // (2 * half) for group in groups]
+    total = sum(counts)
+    flat = [array for group in groups for part in group for array in part[:2]]
     block = 256
 
-    def kernel(inner_ref, grad_ref, inner_far, grad_far, w_ref, w_far, back_own, back_other, out_own, out_other):
-        def added(near_ref, far_ref, size, lanes):
-            total = contract_cols(far_ref[...], w_far[0, :, lanes])
-            for e in range(number):
-                total += contract_cols(near_ref[:, e * size : (e + 1) * size], w_ref[e, :, lanes])
-            return total
-
-        back = added(grad_ref, grad_far, 2 * hidden, slice(0, 2 * hidden))
-        out = added(inner_ref, inner_far, hidden, slice(2 * hidden, 3 * hidden))
-        for s in range(count):
-            start = 2 * s * half
-            back_own[s] = back[start : start + half]
-            back_other[s] = back[start + half : start + 2 * half].astype(jnp.bfloat16)
-            out_own[s] = out[start : start + half]
-            out_other[s] = out[start + half : start + 2 * half].astype(jnp.bfloat16)
-
-    wide = jax.ShapeDtypeStruct((count, half, width), jnp.float32)
-    low = jax.ShapeDtypeStruct((count, half, width), jnp.bfloat16)
+    def kernel(*refs):
+        terms, refs = refs[: len(flat)], refs[len(flat) :]
+        w_ref, back_own, back_other, out_own, out_other = refs
+        n = place = 0
+        for group, count in zip(groups, counts, strict=True):
+            back = out = None
+            for inner, _, start in group:
+                for e in range(inner.shape[1] // hidden):
+                    grad = terms[n + 1][:, 2 * e * hidden : 2 * (e + 1) * hidden]
+                    one = contract_cols(grad, w_ref[start + e, :, : 2 * hidden])
+                    back = one if back is None else back + one
+                n += 2
+            n -= 2 * len(group)
+            for inner, _, start in group:
+                for e in range(inner.shape[1] // hidden):
+                    one = contract_cols(
+                        terms[n][:, e * hidden : (e + 1) * hidden], w_ref[start + e, :, 2 * hidden :]
+                    )
+                    out = one if out is None else out + one
+                n += 2
+            for s in range(count):
+                start = 2 * s * half
+                back_own[place + s] = back[start : start + half].astype(jnp.bfloat16)
+                back_other[place + s] = back[start + half : start + 2 * half].astype(jnp.bfloat16)
+                out_own[place + s] = out[start : start + half].astype(jnp.bfloat16)
+                out_other[place + s] = out[start + half : start + 2 * half].astype(jnp.bfloat16)
+            place += count
+
+    low = jax.ShapeDtypeStruct((total, half, width), jnp.bfloat16)
     return pl.pallas_call(
         kernel,
         grid=(width // block,),
-        in_specs=[whole(*a.shape) for a in (*near, *far)]
-        + [
-            pl.BlockSpec((number, block, 3 * hidden), lambda n: (0, n, 0)),
-            pl.BlockSpec((1, block, 3 * hidden), lambda n: (0, n, 0)),
-        ],
-        out_specs=[pl.BlockSpec((count, half, block), lambda n: (0, 0, n))] * 4,
-        out_shape=[wide, low, wide, low],
+        in_specs=[whole(*a.shape) for a in flat]
+        + [pl.BlockSpec((number, block, 3 * hidden), lambda n: (0, n, 0))],
+        out_specs=[pl.BlockSpec((total, half, block), lambda n: (0, 0, n))] * 4,
+        out_shape=[low] * 4,
         compiler_params=pltpu.CompilerParams(vmem_limit_bytes=VMEM_BYTES),
-        cost_estimate=small_cost(
-            flops=(number + 1) * 6 * rows * width * hidden,
-            bytes_accessed=3 * 10**7,
-            transcendentals=0,
-        ),
+        cost_estimate=small_cost(),
         name="expert_sums",
-    )(*near, *far, near_weights, far_weights)
+    )(*flat, weights)
 
 
 def load_copies(sequence, half, sources, x_all, dy_all, semaphores):
@@ -681,69 +738,84 @@
         )
 
 
-def expert_weight_grads(sequences, terms, experts, hidden):
+def expert_weight_grads(sequences, terms, number, hidden):
     width = sequences[0][0].shape[1]
     half = sequences[0][0].shape[0] // 2 // 128 * 128
-    start, number = experts
     tokens = 2 * half
-    counts = [pair[0].shape[0] // tokens for pair in terms]
     flat = [array for sequence in sequences for array in sequence]
     total = len(sequences)
     quarter = width // 4
+    per_load = 4 * total
 
     def kernel(*refs):
         sources, refs = refs[: len(flat)], refs[len(flat) :]
-        term_refs, refs = refs[: 2 * len(counts)], refs[2 * len(counts) :]
-        result_refs, (x_all, dy_all, semaphores) = refs[:-3], refs[-3:]
-        e = pl.program_id(0)
-
-        @pl.when(e == 0)
-        def _():
+        term_refs, refs = refs[: 2 * len(terms)], refs[2 * len(terms) :]
+        result_refs, refs = refs[: 4 * number], refs[4 * number :]
+        x_all, dy_all, inner_all, grad_all, result, semaphores, term_semaphores, out_semaphores = refs
+
+        def row_copies(of_gradients):
             for s in range(total):
-                for copy in load_copies(s, half, sources, x_all, dy_all, semaphores):
-                    copy.start()
-
-        gate_up = down = None
-        first = 0
-        for joined, count in enumerate(counts):
-
-            @pl.when(e == 0)
-            def _(first=first, count=count):
-                for s in range(first, first + count):
-                    for copy in load_copies(s, half, sources, x_all, dy_all, semaphores):
-                        copy.wait()
-
-            span = pl.ds(first * tokens, count * tokens)
-            one = contract_rows(x_all[span, :], term_refs[2 * joined + 1][...])
-            two = contract_rows(dy_all[span, :], term_refs[2 * joined][...])
-            gate_up = one if gate_up is None else gate_up + one
-            down = two if down is None else down + two
-            first += count
-        for n in range(number):
-
-            @pl.when(e == n)
-            def _(n=n):
-                for q in range(4):
-                    rows = slice(q * quarter, (q + 1) * quarter)
-                    result_refs[4 * n + q][:, : 2 * hidden] = gate_up[rows].astype(jnp.bfloat16)
-                    result_refs[4 * n + q][:, 2 * hidden :] = down[rows].astype(jnp.bfloat16)
-
-    def beside(count, columns):
-        return pl.BlockSpec((count * tokens, columns), lambda e: (0, e + start))
-
+                copies = list(load_copies(s, half, sources, x_all, dy_all, semaphores))
+                yield from copies[2:] if of_gradients else copies[:2]
+
+        def term_copies(e, of_products):
+            place = 0
+            for n, (inner, _, start) in enumerate(terms):
+                rows = inner.shape[0]
+                size = 2 * hidden if of_products else hidden
+                yield pltpu.make_async_copy(
+                    term_refs[2 * n + of_products].at[:, pl.ds((start + e) * size, size)],
+                    (grad_all if of_products else inner_all).at[e, pl.ds(place, rows), :],
+                    term_semaphores.at[2 * len(terms) * e + 2 * n + of_products],
+                )
+                place += rows
+
+        def out_copies(e):
+            for q in range(4):
+                yield pltpu.make_async_copy(
+                    result.at[e, pl.ds(q * quarter, quarter), :],
+                    result_refs[4 * e + q],
+                    out_semaphores.at[4 * e + q],
+                )
+
+        first = [*row_copies(True), *term_copies(0, 0)]
+        second = [*row_copies(False), *term_copies(0, 1)]
+        later = [[*term_copies(e, 0), *term_copies(e, 1)] for e in range(1, number)]
+        for copy in [*first, *second, *(copy for one in later for copy in one)]:
+            copy.start()
+        for e in range(number):
+            for copy in first if e == 0 else later[e - 1]:
+                copy.wait()
+            result[e, :, 2 * hidden :] = contract_rows(dy_all[...], inner_all[e]).astype(jnp.bfloat16)
+            if e == 0:
+                for copy in second:
+                    copy.wait()
+            result[e, :, : 2 * hidden] = contract_rows(x_all[...], grad_all[e]).astype(jnp.bfloat16)
+            for copy in out_copies(e):
+                copy.start()
+        for e in range(number):
+            for copy in out_copies(e):
+                copy.wait()
+
+    anywhere = pl.BlockSpec(memory_space=pl.ANY)
     return pl.pallas_call(
         kernel,
-        grid=(number,),
-        in_specs=[pl.BlockSpec(memory_space=pl.ANY)] * len(flat)
-        + [beside(count, columns) for count in counts for columns in (hidden, 2 * hidden)],
-        out_specs=[whole(quarter, 3 * hidden)] * (4 * number),
+        in_specs=[anywhere] * (len(flat) + 2 * len(terms)),
+        out_specs=[anywhere] * (4 * number),
         scratch_shapes=[pltpu.VMEM((total * tokens, width), jnp.bfloat16)] * 2
-        + [pltpu.SemaphoreType.DMA((4 * total,))],
+        + [
+            pltpu.VMEM((number, total * tokens, hidden), jnp.bfloat16),
+            pltpu.VMEM((number, total * tokens, 2 * hidden), jnp.bfloat16),
+            pltpu.VMEM((number, width, 3 * hidden), jnp.bfloat16),
+            pltpu.SemaphoreType.DMA((per_load,)),
+            pltpu.SemaphoreType.DMA((2 * len(terms) * number,)),
+            pltpu.SemaphoreType.DMA((4 * number,)),
+        ],
         out_shape=[jax.ShapeDtypeStruct((quarter, 3 * hidden), jnp.bfloat16)] * (4 * number),
         compiler_params=pltpu.CompilerParams(vmem_limit_bytes=VMEM_BYTES),
         cost_estimate=small_cost(),
         name="expert_weight_grads",
-    )(*flat, *(array for pair in terms for array in pair))
+    )(*flat, *(array for term in terms for array in term[:2]))
 
 
 def own_weight_grads(sequences, terms, arrived, hidden):
@@ -884,13 +956,18 @@
     far_weights = [flip(far_from_y, 1), flip(x2, 2)]
     up_three, down_three = climb(up_two), descend(down_two)
     number = expert.reshape(1)
-    near_early, near_weights = expert_terms(
-        number, [own, first], [2], [[own_weights], [x0, x1, x2], [y0, y1, y2]], 0, True
-    )
     second = jnp.where(plane == 0, down_two, jnp.where(plane == 3, up_two, down_one))
     second = (second, swap(second))
-    far_weights, up_three, down_three, near_early, second = together(
-        (far_weights, up_three, down_three, near_early, second)
+    near_pieces = [[own_weights], [x0, x1, x2], [y0, y1, y2]]
+    near_early, near_second, near_weights = expert_terms(
+        number,
+        [([own, first], 0), ([second], 0)],
+        [[(piece, None) for piece in one] for one in near_pieces],
+        0,
+        True,
+    )
+    far_weights, up_three, down_three, near_early, near_second, second = together(
+        (far_weights, up_three, down_three, near_early, near_second, second)
     )
     third = jnp.where(
         plane == 0,
@@ -898,37 +975,46 @@
         jnp.where(plane == 1, down_two, jnp.where(plane == 2, up_two, up_three)),
     )
     third = (third, swap(third))
-    sequences = [own, first, third, second]
-    far_early, far_late, far_weights = expert_terms(
-        number, sequences, [2, 2], [far_weights], 3, True
-    )
-    to_far = expert_weight_grads(sequences, [far_early, far_late], (0, 1), hidden)
-
+    far_pieces = [(piece, None) for piece in far_weights]
+    all_third, far_second, weights = expert_terms(
+        number,
+        [([third], 0), ([second], 3)],
+        [[(near_weights, 0)], [(near_weights, 1)], [(near_weights, 2)], far_pieces],
+        0,
+        True,
+    )
+    (far_early,) = expert_terms(number, [([own, first], 0)], [[(weights, 3)]], 3, False)
+    to_far = expert_weight_grads(
+        [third, second, own, first], [(*all_third, 3), (*far_second, 0), (*far_early, 0)], 1, hidden
+    )
     over_x, over_y = [flip(to_far[0], 1)], [flip(to_far[2], 2)]
-    to_far, late = together((to_far, sequences[2:]))
-    (near_late,) = expert_terms(number, late, [2], near_weights, 0, False)
-    near_late, over_x, over_y, to_far = together((near_late, over_x, over_y, to_far))
+    to_far, near_second, far_second = together((to_far, near_second, far_second))
+    late_sums = expert_sums(
+        [[(*all_third, 0)], [(*near_second, 0), (*far_second, 3)]], weights, half
+    )
+    late_sums, over_x, over_y, to_far = together((late_sums, over_x, over_y, to_far))
+    back_late = add_low(late_sums[0], swap(late_sums[1]))
+    back_late, near_early, all_third = together((back_late, near_early, all_third))
+    second_back, third_back = back_late[1], back_late[0]
+
+    falling, rising = descend(third_back), climb(third_back)
     over_x, over_y = over_x + [flip(to_far[1], 1)], over_y + [flip(to_far[3], 2)]
-    late_sums = expert_sums(near_late, far_late, near_weights, far_weights, half)
-    late_sums, over_x, over_y, near_early, near_late = together(
-        (late_sums, over_x, over_y, near_early, near_late)
-    )
-    back_late = add_low(late_sums[0], swap(late_sums[1]))
-    second_back, third_back = back_late[1], back_late[0]
-
-    falling, rising = descend(third_back), climb(third_back)
-    third_back, near_early, near_late = together((third_back, near_early, near_late))
-    beside = expert_weight_grads(sequences, [near_early, near_late], (1, 2), hidden)
-    falling, rising, beside, near_early, far_early = together(
-        (falling, rising, beside, near_early, far_early)
+    beside = expert_weight_grads(
+        [own, first, second, third],
+        [(*near_early, 1), (*near_second, 1), (*all_third, 1)],
+        2,
+        hidden,
+    )
+    falling, rising, beside, over_x, over_y, far_early = together(
+        (falling, rising, beside, over_x, over_y, far_early)
     )
     to_x, to_y = beside[:4], beside[4:]
     falling = add_low(jnp.where(plane == 3, second_back, third_back), falling)
     rising = add_low(jnp.where(plane == 0, second_back, third_back), rising)
-    falling, rising, near_early, far_early = together((falling, rising, near_early, far_early))
+    falling, rising, far_early = together((falling, rising, far_early))
     falling, rising = descend(falling), climb(rising)
     from_x, from_y = [flip(to_x[0], 1)], [flip(to_y[2], 2)]
-    early_sums = expert_sums(near_early, far_early, near_weights, far_weights, half)
+    early_sums = expert_sums([[(*near_early, 0), (*far_early, 3)]], weights, half)
     falling, rising, early_sums, from_x, from_y, to_x, to_y = together(
         (falling, rising, early_sums, from_x, from_y, to_x, to_y)
     )
@@ -936,6 +1022,9 @@
     own_back, first_back = back_early[0], back_early[1]
     falling = add_low(first_back, falling)
     rising = add_low(jnp.where(plane == 0, first_back, second_back), rising)
+    falling, rising, early_sums, late_sums, over_x = together(
+        (falling, rising, early_sums, late_sums, over_x)
+    )
     falling, rising = descend(falling), climb(rising)
     from_x, from_y = from_x + [flip(to_x[1], 1)], from_y + [flip(to_y[3], 2)]
     with_x = jnp.concatenate([add_low(to_y[n], over_x[n]) for n in range(2)], axis=0)
@@ -967,14 +1056,14 @@
     )
     grad_attn_half = grad_middle.astype(jnp.bfloat16)
     grad_attn = ordered(grad_attn_half, swap(grad_attn_half), core)
-    grad_mixed = contract_cols(grad_attn, w_output).astype(jnp.bfloat16)
     grad_output = contract_rows(mixed, grad_attn).astype(jnp.bfloat16)
-    grad_mixed, grad_output = together((grad_mixed, grad_output))
+    grad_attn, grad_output = together((grad_attn, grad_output))
     output_parts = plane_scatter_first(grad_output, bit_x, bit_y)
-    grad_all_pre = attention_backward(grad_mixed, queries, keys, values, cosine, sine)
+    grad_all_pre = attention_backward(grad_attn, w_output, queries, keys, values, cosine, sine)
     grad_all_pre, output_parts = together((grad_all_pre, output_parts))
     grad_projections = contract_rows(normed, grad_all_pre).astype(jnp.bfloat16)
     output_parts = plane_scatter_second(output_parts, bit_x, bit_y)
+    grad_projections, output_parts = together((grad_projections, output_parts))
     projection_parts = plane_scatter_first(grad_projections, bit_x, bit_y)
     w_all = jnp.concatenate([w_query, w_key, w_value], axis=1)
     grad_normed_part = contract_cols(grad_all_pre, w_all).astype(jnp.bfloat16)
@@ -990,9 +1079,7 @@
         grad_unit_one - unit_half * jnp.mean(grad_unit_one * unit_half, axis=-1, keepdims=True)
     )
     gains = jnp.stack([grad_attn_gain, grad_moe_gain])
-    projection_parts, output_parts, gains, grad_in_half = together(
-        (projection_parts, output_parts, gains, grad_in_half)
-    )
+    projection_parts, gains, grad_in_half = together((projection_parts, gains, grad_in_half))
     projection_parts = plane_scatter_second(projection_parts, bit_x, bit_y)
     gains = (gains + swap(gains)).reshape(-1, grad_projections.shape[1])
     gain_rows = gains.shape[0]
@@ -1009,29 +1096,36 @@
     block_half = (middle + moe_result.astype(jnp.float32)).astype(jnp.bfloat16)
     block_out = ordered(block_half, swap(block_half), core)
     then_y, then_x = flip(with_x, 2), flip(with_y, 1)
+    output_both, projection_both, block_out, then_x, then_y = together(
+        (output_both, projection_both, block_out, then_x, then_y)
+    )
+    gains, projection_both = projection_both[-16:].astype(jnp.float32), projection_both[:-16]
+    output_halves = plane_gather_first(*jnp.split(output_both, 2), bit_x, bit_y)
+    projection_halves = plane_gather_first(*jnp.split(projection_both, 2), bit_x, bit_y)
+    output_halves, projection_halves, gains, then_x, then_y = together(
+        (output_halves, projection_halves, gains, then_x, then_y)
+    )
     arrived = (*from_x, *from_y, then_y, then_x)
-    expert_grads = own_weight_grads(sequences, [near_early, near_late], arrived, hidden)
-    output_both, projection_both, expert_grads, block_out = together(
-        (output_both, projection_both, expert_grads, block_out)
-    )
-    output_sum = plane_gather(*jnp.split(output_both, 2), bit_x, bit_y)
-    gains = projection_both[-16:].astype(jnp.float32)
-    gains = gains + flip(gains, 1)
-    gains = gains + flip(gains, 2)
+    expert_grads = own_weight_grads(
+        [own, first, second, third], [near_early, near_second, all_third], arrived, hidden
+    )
+    output_pieces = plane_gather_second(output_halves, bit_x, bit_y)
+    projection_pieces = plane_gather_second(projection_halves, bit_x, bit_y)
+    expert_grads, output_pieces, projection_pieces, gains = together(
+        (expert_grads, output_pieces, projection_pieces, gains)
+    )
+    gains = (gains + flip(gains, 1)) + (flip(gains, 2) + flip(gains, 3))
     gains_sum = gains[:gain_rows].reshape(2, width)
-    projection_both = projection_both[:-16]
     grad_gate, grad_up, grad_down = expert_grads
-    projections = plane_gather(*jnp.split(projection_both, 2), bit_x, bit_y).astype(jnp.float32)
-    query_width = w_query.shape[1]
-    key_width = w_key.shape[1]
+    bits = jnp.stack([bit_x, bit_y])
+    (output_sum,) = lay_out(bits, output_pieces, (width,))
+    projections = lay_out(bits, projection_pieces, [w.shape[1] for w in (w_query, w_key, w_value)])
     return (
         block_out,
         grad_in,
         gains_sum[0],
-        projections[:, :query_width],
-        projections[:, query_width : query_width + key_width],
-        projections[:, query_width + key_width :],
-        output_sum.astype(jnp.float32),
+        *projections,
+        output_sum,
         gains_sum[1],
         grad_gate,
         grad_up,

time: 608 us -> 588 us (0.967)
  waiting for transfers between devices: 200 us -> 193 us
    psum x1, waiting for transfers between devices: 3.96 us -> 58 us  [planes_of_four(): lax.psum((output_both, projection_both), 'expert', axis_index_groups=colu...]
    ppermute x36 -> x37, waiting for transfers between devices: 101 us -> 53.4 us  [flip(): return lax.ppermute(value, 'expert', [(i, i ^ bit) for i in range(places)])]
    ppermute x7, waiting for transfers between devices: 53.9 us -> 40.7 us  [climb(): lax.ppermute(value, 'expert', [(i, i + 4) for i in range(places - 4)])]
    pallas_call x2 -> x4, Pallas kernels: 46.1 us -> 53.5 us  [the longest x2 44.5 us: expert_weight_grads(): pl.pallas_call(kernel, in_specs=[anywhere] * (len(flat) + 2 * len(terms))...]
    ppermute x36 -> x37, starting transfers between devices: 39.7 us -> 42.6 us  [flip(): return lax.ppermute(value, 'expert', [(i, i ^ bit) for i in range(places)])]
  transfers between devices with their start and end apart: 66 -> 67, of which waited for: 34 -> 32; matrix products, arithmetic and copies ran while one was open for 12% -> 11% of each run, Pallas kernels for 26% -> 26%
where the time goes in v3:
time: 588 us; the launch traced here: 579 us
  Pallas kernels  196 us (33%)
  waiting for transfers between devices  193 us (33%)
  starting transfers between devices  84.3 us (14%)
  other arithmetic  61 us (10%)
  local copies, waits for them, and re-layouts  24.7 us (4%)
  between operations  15.6 us (3%)
    psum x1, waiting for transfers between devices, planes_of_four(): lax.psum((output_both, projection_both), 'expert', axis_index_groups=colu...  58 us
    ppermute x37, waiting for transfers between devices, flip(): return lax.ppermute(value, 'expert', [(i, i ^ bit) for i in range(places)])  53.4 us
    pallas_call x3, Pallas kernels, expert_terms(): pl.pallas_call(kernel, grid=(number,), in_specs=[pl.BlockSpec(memory_spac...  53.1 us
    pallas_call x2, Pallas kernels, expert_sums(): pl.pallas_call(kernel, grid=(width // block,), in_specs=[whole(*a.shape)...  45.8 us
    pallas_call x2, Pallas kernels, expert_weight_grads(): pl.pallas_call(kernel, in_specs=[anywhere] * (len(flat) + 2 * len(terms))...  44.5 us
    ppermute x37, starting transfers between devices, flip(): return lax.ppermute(value, 'expert', [(i, i ^ bit) for i in range(places)])  42.6 us
    ppermute x7, waiting for transfers between devices, climb(): lax.ppermute(value, 'expert', [(i, i + 4) for i in range(places - 4)])  40.7 us
    ppermute x7, starting transfers between devices, climb(): lax.ppermute(value, 'expert', [(i, i + 4) for i in range(places - 4)])  30.3 us
  transfers between devices with their start and end apart: 67, of which 32 were waited for; matrix products, arithmetic and copies ran while one was open for 11% of the time, Pallas kernels for 26%

profile of v3, /device:TPU:0, one launch (start us, length us, event | category | flops | bytes accessed | tf_op | source)
XLA Modules:
  0.0 579.3 jit_solution(5142916090459274720)
XLA Ops:
  18.4 4.4 collective-permute-start.2
  24.6 12.1 %attention_forward.1 = (bf16[512,1536]{1,0:T(8,128)(2,1)}, bf16[512,768]{1,0:T(8,128)(2,1)}, bf16[512,128]{1,0:T(8,128)(2,1)}, bf16[512,128]{1,0:T(8,128)(2,1)},...) custom-call(s32[1]{0:T(128)} %bitcast.core_ref, bf16[512,1536]{1,0:T(8,128)(2,1)} %hidden_ref.1, ...), custom_call_target="tpu_custom_call" | custom-call | flops 1000 | bytes 1000 | tf_op jit(solution)/shard_map/attention_forward/pallas_call | solution.py:446
  39.4 5.0 collective-permute-done.3
  59.5 7.4 %collective-permute-done.5.refs_8_ = bf16[384,1152]{1,0:T(8,128)(2,1)} collective-permute-done((bf16[384,1152]{1,0:T(8,128)(2,1)}, bf16[384,1152]{1,0:T(8,128)(2,1)}, u32[]{:S(2)}, u32[]{:S(2)}) %collective-permute-start.5) | collective-permute-done | bytes 884768 | tf_op jit(solution)/shard_map/ppermute | solution.py:294
  70.1 5.0 collective-permute-done.8
  75.1 3.8 pad_maximum_fusion.5
  90.3 25.9 %collective-permute-done.11 = bf16[528,1536]{1,0:T(8,128)(2,1)} collective-permute-done((bf16[528,1536]{1,0:T(8,128)(2,1)}, bf16[528,1536]{1,0:T(8,128)(2,1)}, u32[]{:S(2)}, u32[]{:S(2)}) %collective-permute-start.11) | collective-permute-done | bytes 1622048 | tf_op jit(solution)/shard_map/ppermute | solution.py:299
  116.2 5.3 collective-permute-done.12
  131.9 26.5 %expert_terms.3 = (bf16[1024,1152]{1,0:T(8,128)(2,1)}, bf16[1024,2304]{1,0:T(8,128)(2,1)}, bf16[512,1152]{1,0:T(8,128)(2,1)}, bf16[512,2304]{1,0:T(8,128)(2,1)}, bf16[3,1536,1152]{2,1,0:T(8,128)(2,1)}) custom-call(s32[1]{0:T(128)} %bitcast.7.expert_ref, bf16[528,1536]{1,0:T(8,128)(2,1)} %copy-done, ...), custom_call_target="tpu_custom_call" | custom-call | flops 1000 | bytes 1000 | tf_op jit(solution)/shard_map/expert_terms/pallas_call | solution.py:660
  158.4 5.5 collective-permute-done.17
  163.9 5.3 collective-permute-done.18
  176.1 17.5 %expert_terms.4 = (bf16[512,1536]{1,0:T(8,128)(2,1)}, bf16[512,3072]{1,0:T(8,128)(2,1)}, bf16[512,384]{1,0:T(8,128)(2,1)}, bf16[512,768]{1,0:T(8,128)(2,1)}, bf16[4,1536,1152]{2,1,0:T(8,128)(2,1)}) custom-call(s32[1]{0:T(128)} %bitcast.7.expert_ref, bf16[528,1536]{1,0:T(8,128)(2,1)} %copy-done.5, bf16[528,1536]{1,0:T(8,128)(2,1)} %copy-done.9, ...), custom_call_target="tpu_custom_call" | custom-call | flops 1000 | bytes 1000 | tf_op jit(solution)/shard_map/expert_terms/pallas_call | solution.py:660
  193.7 9.0 %expert_terms.5 = (bf16[1024,384]{1,0:T(8,128)(2,1)}, bf16[1024,768]{1,0:T(8,128)(2,1)}) custom-call(s32[1]{0:T(128)} %bitcast.7.expert_ref, bf16[528,1536]{1,0:T(8,128)(2,1)} %copy-done, bf16[528,1536]{1,0:T(8,128)(2,1)} %collective-permute-done.13.refs_1_.refs_5_, bf16[528,1536]{1,0:T(8,128)(2,1)} %copy-done.1, bf16[528,1536]{1,0:T(8,128)(2,1)} %copy-done.3, ...), custom_call_target="tpu_custom_call" | custom-call | flops 1000 | bytes 1000 | tf_op jit(solution)/shard_map/expert_terms/pallas_call | solution.py:660
  202.7 18.1 %expert_weight_grads.2 = (bf16[384,1152]{1,0:T(8,128)(2,1)}, bf16[384,1152]{1,0:T(8,128)(2,1)}, bf16[384,1152]{1,0:T(8,128)(2,1)}, bf16[384,1152]{1,0:T(8,128)(2,1)}) custom-call(bf16[528,1536]{1,0:T(8,128)(2,1)} %copy-done.5, bf16[528,1536]{1,0:T(8,128)(2,1)} %copy-done.9, bf16[528,1536]{1,0:T(8,128)(2,1)} %copy-done.2, bf16[528,1536]{1,0:T(8,128)(2,1)} %copy-done.4, ...), custom_call_target="tpu_custom_call" | custom-call | flops 1000 | bytes 1000 | tf_op jit(solution)/shard_map/expert_weight_grads/pallas_call | solution.py:801
  222.5 22.9 %expert_sums.2 = (bf16[2,256,1536]{2,1,0:T(8,128)(2,1)}, bf16[2,256,1536]{2,1,0:T(8,128)(2,1)}, bf16[2,256,1536]{2,1,0:T(8,128)(2,1)}, bf16[2,256,1536]{2,1,0:T(8,128)(2,1)}) custom-call(bf16[512,1536]{1,0:T(8,128)(2,1)} %get-tuple-element.272.refs_8_.refs_0_.refs_12_, bf16[512,3072]{1,0:T(8,128)(2,1)} %get-tuple-element.273.refs_9_.refs_1_.refs_13_, ...), custom_call_target="tpu_custom_call" | custom-call | flops 1000 | bytes 1000 | tf_op jit(solution)/shard_map/expert_sums/pallas_call | solution.py:718
  253.1 5.5 collective-permute-start.25
  258.6 26.4 %expert_weight_grads.3 = (bf16[384,1152]{1,0:T(8,128)(2,1)}, bf16[384,1152]{1,0:T(8,128)(2,1)}, bf16[384,1152]{1,0:T(8,128)(2,1)}, bf16[384,1152]{1,0:T(8,128)(2...) custom-call(bf16[528,1536]{1,0:T(8,128)(2,1)} %copy-done, ...), custom_call_target="tpu_custom_call" | custom-call | flops 1000 | bytes 1000 | tf_op jit(solution)/shard_map/expert_weight_grads/pallas_call | solution.py:801
  291.6 5.4 collective-permute-start.29
  297.1 22.9 %expert_sums.3 = (bf16[2,256,1536]{2,1,0:T(8,128)(2,1)}, bf16[2,256,1536]{2,1,0:T(8,128)(2,1)}, bf16[2,256,1536]{2,1,0:T(8,128)(2,1)}, bf16[2,256,1536]{2,1,0:T(8,128)(2,1)}) custom-call(bf16[1024,1152]{1,0:T(8,128)(2,1)} %get-tuple-element.270.refs_8_.refs_0_, bf16[1024,2304]{1,0:T(8,128)(2,1)} %get-tuple-element.271.refs_9_.refs_1_, ...), custom_call_target="tpu_custom_call" | custom-call | flops 1000 | bytes 1000 | tf_op jit(solution)/shard_map/expert_sums/pallas_call | solution.py:718
  334.1 5.3 collective-permute-start.34
  343.3 9.2 %collective-permute-done.33 = bf16[256,1536]{1,0:T(8,128)(2,1)} collective-permute-done((bf16[256,1536]{1,0:T(8,128)(2,1)}, bf16[256,1536]{1,0:T(8,128)(2,1)}, u32[]{:S(2)}, u32[]{:S(2)}) %collective-permute-start.33) | collective-permute-done | bytes 786464 | tf_op jit(solution)/shard_map/ppermute | solution.py:304
  375.4 12.5 %attention_backward.1 = bf16[512,1024]{1,0:T(8,128)(2,1)} custom-call(bf16[512,1536]{1,0:T(8,128)(2,1)} %copy-done.12, bf16[768,1536]{1,0:T(8,128)(2,1)} %wo_ref.3, bf16[512,768]{1,0:T(8,128)(2,1)} %get-tuple-element.338.query_ref, bf16[512,128]{1,0:T(8,128)(2,1)} %get-tuple-element.339.key_ref, bf16[512,128]{1,0:T(8,128)(2,1)} %get-tuple-element.340.value_ref, ...), custom_call_target="tpu_custom_call" | custom-call | flops 1000 | bytes 1000 | tf_op jit(solution)/shard_map/attention_backward/pallas_call | solution.py:506
  405.8 12.8 %collective-permute-done.44 = bf16[384,1024]{1,0:T(8,128)(2,1)S(1)} collective-permute-done((bf16[384,1024]{1,0:T(8,128)(2,1)S(1)}, bf16[384,1024]{1,0:T(8,128)(2,1)S(1)}, u32[]{:S(2)}, u32[]{:S(2)}) %collective-permute-start.44) | collective-permute-done | bytes 786464 | tf_op jit(solution)/shard_map/ppermute | solution.py:294
  425.2 8.1 %collective-permute-done.48 = bf16[192,1024]{1,0:T(8,128)(2,1)} collective-permute-done((bf16[192,1024]{1,0:T(8,128)(2,1)}, bf16[192,1024]{1,0:T(8,128)(2,1)}, u32[]{:S(2)}, u32[]{:S(2)}) %collective-permute-start.48) | collective-permute-done | bytes 393248 | tf_op jit(solution)/shard_map/ppermute | solution.py:294
  435.8 5.3 maximum_select_fusion
  447.9 58.0 %all-reduce.5.cloned.1.call-done = (bf16[192,1536]{1,0:T(8,128)(2,1)}, bf16[400,1024]{1,0:T(8,128)(2,1)}) async-done(((bf16[192,1536]{1,0:T(8,128)(2,1)}, bf16[400,1024]{1,0:T(8,128)(2,1)}), (bf16[192,1536]{1,0:T(8,128)(2,1)}, bf16[400,1024]{1,0:T(8,128)(2,1)})) %all-reduce.5.cloned.1.call-update) | async-done | bytes 1409040 | tf_op jit(solution)/shard_map/psum | solution.py:1093
  511.9 5.2 collective-permute-done.54
  518.7 5.4 collective-permute-done.56
  529.7 19.0 %own_weight_grads.1 = (f32[1,1536,384]{2,1,0:T(8,128)}, f32[1,1536,384]{2,1,0:T(8,128)}, f32[1,384,1536]{2,1,0:T(8,128)}) custom-call(bf16[528,1536]{1,0:T(8,128)(2,1)} %copy-done, bf16[528,1536]{1,0:T(8,128)(2,1)} %collective-permute-done.13.refs_1_.refs_5_, bf16[528,1536]{1,0:T(8,128)(2,1)} %copy-done.1, bf16[528,1536]{1,0:T(8,128)(2,1)} %copy-done.3, ...), custom_call_target="tpu_custom_call" | custom-call | flops 1000 | bytes 1000 | tf_op jit(solution)/shard_map/own_weight_grads/pallas_call | solution.py:866
  548.7 7.4 %collective-permute-done.58.refs_1_ = bf16[192,1536]{1,0:T(8,128)(2,1)S(1)} collective-permute-done((bf16[192,1536]{1,0:T(8,128)(2,1)S(1)}, bf16[192,1536]{1,0:T(8,128)(2,1)S(1)}, u32[]{:S(2)}, u32[]{:S(2)}) %collective-permute-start.58) | collective-permute-done | bytes 589856 | tf_op jit(solution)/shard_map/ppermute | solution.py:294
  561.6 4.8 lay_out.2
  566.4 4.1 lay_out.3
  (317 shorter events, 172.6 us)
Async XLA Ops:
  7.2 433.9 %reduce-scatter.2.cloned.1.call-start = ((), (), s32[]{:S(2)}) async-start(), calls=%async_computation.1 | async-start | bytes 3932160 | tf_op jit(solution)/shard_map/reduce_scatter | solution.py:1045
  11.6 32.8 %collective-permute-start = (bf16[384,1152]{1,0:T(8,128)(2,1)S(1)}, bf16[384,1152]{1,0:T(8,128)(2,1)}, u32[]{:S(2)}, u32[]{:S(2)}) collective-permute-start(bf16[384,1152]{1,0:T(8,128)(2,1)S(1)} %get-tuple-element.410), channel_id=1, source_target_pairs={{0,2},{2,0},{4,6},{6,4},{8,10},{10,8},{12,14},{14,12},{16,18},{18,... | collective-permute-start | bytes 2654216 | tf_op jit(solution)/shard_map/ppermute | solution.py:294
  14.5 29.9 %collective-permute-start.1 = (bf16[384,1152]{1,0:T(8,128)(2,1)S(1)}, bf16[384,1152]{1,0:T(8,128)(2,1)S(1)}, u32[]{:S(2)}, u32[]{:S(2)}) collective-permute-start(bf16[384,1152]{1,0:T(8,128)(2,1)S(1)} %get-tuple-element.410), channel_id=1, source_target_pairs={{0,4},{2,6},{4,0},{6,2},{8,12},{10,14},{12,8},{14,10},{16,20},{18,... | collective-permute-start | bytes 2654216 | tf_op jit(solution)/shard_map/ppermute | solution.py:294
  44.5 22.4 %collective-permute-start.5 = (bf16[384,1152]{1,0:T(8,128)(2,1)}, bf16[384,1152]{1,0:T(8,128)(2,1)}, u32[]{:S(2)}, u32[]{:S(2)}) collective-permute-start(bf16[384,1152]{1,0:T(8,128)(2,1)} %get-tuple-element.207), channel_id=1, source_target_pairs={{0,2},{2,0},{4,6},{6,4},{8,10},{10,8},{12,14},{14,12},{16,18},{18,... | collective-permute-start | bytes 2654216 | tf_op jit(solution)/shard_map/ppermute | solution.py:294
  56.1 30.8 %collective-permute-start.13 = (bf16[528,1536]{1,0:T(8,128)(2,1)S(1)}, bf16[528,1536]{1,0:T(8,128)(2,1)}, u32[]{:S(2)}, u32[]{:S(2)}) collective-permute-start(bf16[528,1536]{1,0:T(8,128)(2,1)S(1)} %pad_maximum_fusion.7.refs_0_.refs_4_), channel_id=1, source_target_pairs={{0,1},{1,0},{2,3},{3,2},{4,5},{5,4},{6,7},{7,6},{8,9},{9,8},{10,11... | collective-permute-start | bytes 4866056 | tf_op jit(solution)/shard_map/ppermute | solution.py:289
  78.9 42.6 %collective-permute-start.9 = (bf16[768,1152]{1,0:T(8,128)(2,1)}, bf16[768,1152]{1,0:T(8,128)(2,1)}, u32[]{:S(2)}, u32[]{:S(2)}) collective-permute-start(bf16[768,1152]{1,0:T(8,128)(2,1)} %slice.65), channel_id=1, source_target_pairs={{0,2},{2,0},{4,6},{6,4},{8,10},{10,8},{12,14},{14,12},{16,18},{18,... | collective-permute-start | bytes 5308424 | tf_op jit(solution)/shard_map/ppermute | solution.py:294
  79.4 42.1 %collective-permute-start.10 = (bf16[768,1152]{1,0:T(8,128)(2,1)}, bf16[768,1152]{1,0:T(8,128)(2,1)}, u32[]{:S(2)}, u32[]{:S(2)}) collective-permute-start(bf16[768,1152]{1,0:T(8,128)(2,1)} %slice.65), channel_id=1, source_target_pairs={{0,4},{2,6},{4,0},{6,2},{8,12},{10,14},{12,8},{14,10},{16,20},{18,... | collective-permute-start | bytes 5308424 | tf_op jit(solution)/shard_map/ppermute | solution.py:294
  80.2 35.9 %collective-permute-start.11 = (bf16[528,1536]{1,0:T(8,128)(2,1)}, bf16[528,1536]{1,0:T(8,128)(2,1)}, u32[]{:S(2)}, u32[]{:S(2)}) collective-permute-start(bf16[528,1536]{1,0:T(8,128)(2,1)} %get-tuple-element.216), channel_id=1, source_target_pairs={{0,8},{2,10},{4,12},{6,14},{8,16},{10,18},{12,20},{14,22},{16,24},... | collective-permute-start | bytes 4866056 | tf_op jit(solution)/shard_map/ppermute | solution.py:299
  84.0 37.4 %collective-permute-start.12 = (bf16[528,1536]{1,0:T(8,128)(2,1)}, bf16[528,1536]{1,0:T(8,128)(2,1)}, u32[]{:S(2)}, u32[]{:S(2)}) collective-permute-start(bf16[528,1536]{1,0:T(8,128)(2,1)} %get-tuple-element.217), channel_id=1, source_target_pairs={{8,0},{10,2},{12,4},{14,6},{16,8},{18,10},{20,12},{22,14},{24,16},... | collective-permute-start | bytes 4866056 | tf_op jit(solution)/shard_map/ppermute | solution.py:304
  86.9 34.5 %collective-permute-start.14 = (bf16[528,1536]{1,0:T(8,128)(2,1)S(1)}, bf16[528,1536]{1,0:T(8,128)(2,1)S(1)}, u32[]{:S(2)}, u32[]{:S(2)}) collective-permute-start(bf16[528,1536]{1,0:T(8,128)(2,1)S(1)} %broadcast_select_fusion.refs_2_.refs_6_), channel_id=1, source_target_pairs={{0,1},{1,0},{2,3},{3,2},{4,5},{5,4},{6,7},{7,6},{8,9},{9,8},{10,11... | collective-permute-start | bytes 4866056 | tf_op jit(solution)/shard_map/ppermute | solution.py:289
  121.4 47.8 %collective-permute-start.15 = (bf16[768,1152]{1,0:T(8,128)(2,1)}, bf16[768,1152]{1,0:T(8,128)(2,1)}, u32[]{:S(2)}, u32[]{:S(2)}) collective-permute-start(bf16[768,1152]{1,0:T(8,128)(2,1)} %pad_maximum_fusion.2), channel_id=1, source_target_pairs={{0,2},{2,0},{4,6},{6,4},{8,10},{10,8},{12,14},{14,12},{16,18},{18,... | collective-permute-start | bytes 5308424 | tf_op jit(solution)/shard_map/ppermute | solution.py:294
  122.9 46.3 %collective-permute-start.16 = (bf16[768,1152]{1,0:T(8,128)(2,1)}, bf16[768,1152]{1,0:T(8,128)(2,1)}, u32[]{:S(2)}, u32[]{:S(2)}) collective-permute-start(bf16[768,1152]{1,0:T(8,128)(2,1)} %collective-permute-done.9.refs_9_), channel_id=1, source_target_pairs={{0,4},{2,6},{4,0},{6,2},{8,12},{10,14},{12,8},{14,10},{16,20},{18,... | collective-permute-start | bytes 5308424 | tf_op jit(solution)/shard_map/ppermute | solution.py:294
  126.7 37.2 %collective-permute-start.17 = (bf16[528,1536]{1,0:T(8,128)(2,1)}, bf16[528,1536]{1,0:T(8,128)(2,1)}, u32[]{:S(2)}, u32[]{:S(2)}) collective-permute-start(bf16[528,1536]{1,0:T(8,128)(2,1)} %collective-permute-done.11), channel_id=1, source_target_pairs={{0,8},{2,10},{4,12},{6,14},{8,16},{10,18},{12,20},{14,22},{16,24},... | collective-permute-start | bytes 4866056 | tf_op jit(solution)/shard_map/ppermute | solution.py:299
  129.2 40.0 %collective-permute-start.18 = (bf16[528,1536]{1,0:T(8,128)(2,1)}, bf16[528,1536]{1,0:T(8,128)(2,1)}, u32[]{:S(2)}, u32[]{:S(2)}) collective-permute-start(bf16[528,1536]{1,0:T(8,128)(2,1)} %collective-permute-done.12), channel_id=1, source_target_pairs={{8,0},{10,2},{12,4},{14,6},{16,8},{18,10},{20,12},{22,14},{24,16},... | collective-permute-start | bytes 4866056 | tf_op jit(solution)/shard_map/ppermute | solution.py:304
  220.9 24.6 %collective-permute-start.21 = (bf16[384,1152]{1,0:T(8,128)(2,1)}, bf16[384,1152]{1,0:T(8,128)(2,1)S(1)}, u32[]{:S(2)}, u32[]{:S(2)}) collective-permute-start(bf16[384,1152]{1,0:T(8,128)(2,1)} %get-tuple-element.249), channel_id=1, source_target_pairs={{0,2},{2,0},{4,6},{6,4},{8,10},{10,8},{12,14},{14,12},{16,18},{18,... | collective-permute-start | bytes 2654216 | tf_op jit(solution)/shard_map/ppermute | solution.py:294
  222.0 23.4 %collective-permute-start.22 = (bf16[384,1152]{1,0:T(8,128)(2,1)}, bf16[384,1152]{1,0:T(8,128)(2,1)S(1)}, u32[]{:S(2)}, u32[]{:S(2)}) collective-permute-start(bf16[384,1152]{1,0:T(8,128)(2,1)} %get-tuple-element.251), channel_id=1, source_target_pairs={{0,4},{2,6},{4,0},{6,2},{8,12},{10,14},{12,8},{14,10},{16,20},{18,... | collective-permute-start | bytes 2654216 | tf_op jit(solution)/shard_map/ppermute | solution.py:294
  245.5 39.5 %collective-permute-start.26 = (bf16[384,1152]{1,0:T(8,128)(2,1)}, bf16[384,1152]{1,0:T(8,128)(2,1)S(1)}, u32[]{:S(2)}, u32[]{:S(2)}) collective-permute-start(bf16[384,1152]{1,0:T(8,128)(2,1)} %get-tuple-element.283), channel_id=1, source_target_pairs={{0,2},{2,0},{4,6},{6,4},{8,10},{10,8},{12,14},{14,12},{16,18},{18,... | collective-permute-start | bytes 2654216 | tf_op jit(solution)/shard_map/ppermute | solution.py:294
  246.5 38.5 %collective-permute-start.27 = (bf16[384,1152]{1,0:T(8,128)(2,1)}, bf16[384,1152]{1,0:T(8,128)(2,1)}, u32[]{:S(2)}, u32[]{:S(2)}) collective-permute-start(bf16[384,1152]{1,0:T(8,128)(2,1)} %get-tuple-element.285), channel_id=1, source_target_pairs={{0,4},{2,6},{4,0},{6,2},{8,12},{10,14},{12,8},{14,10},{16,20},{18,... | collective-permute-start | bytes 2654216 | tf_op jit(solution)/shard_map/ppermute | solution.py:294
  251.9 33.2 %collective-permute-start.24 = (bf16[256,1536]{1,0:T(8,128)(2,1)}, bf16[256,1536]{1,0:T(8,128)(2,1)S(1)}, u32[]{:S(2)}, u32[]{:S(2)}) collective-permute-start(bf16[256,1536]{1,0:T(8,128)(2,1)} %slice_bitcast_fusion.2), channel_id=1, source_target_pairs={{8,0},{10,2},{12,4},{14,6},{16,8},{18,10},{20,12},{22,14},{24,16},... | collective-permute-start | bytes 2359304 | tf_op jit(solution)/shard_map/ppermute | solution.py:304
  253.1 31.9 %collective-permute-start.25 = (bf16[256,1536]{1,0:T(8,128)(2,1)}, bf16[256,1536]{1,0:T(8,128)(2,1)}, u32[]{:S(2)}, u32[]{:S(2)}) collective-permute-start(bf16[256,1536]{1,0:T(8,128)(2,1)} %slice_bitcast_fusion.2), channel_id=1, source_target_pairs={{0,8},{2,10},{4,12},{6,14},{8,16},{10,18},{12,20},{14,22},{16,24},... | collective-permute-start | bytes 2359304 | tf_op jit(solution)/shard_map/ppermute | solution.py:299
  285.1 35.0 %collective-permute-start.30 = (bf16[384,1152]{1,0:T(8,128)(2,1)}, bf16[384,1152]{1,0:T(8,128)(2,1)}, u32[]{:S(2)}, u32[]{:S(2)}) collective-permute-start(bf16[384,1152]{1,0:T(8,128)(2,1)} %get-tuple-element.298), channel_id=1, source_target_pairs={{0,2},{2,0},{4,6},{6,4},{8,10},{10,8},{12,14},{14,12},{16,18},{18,... | collective-permute-start | bytes 2654216 | tf_op jit(solution)/shard_map/ppermute | solution.py:294
  286.1 34.0 %collective-permute-start.31 = (bf16[384,1152]{1,0:T(8,128)(2,1)}, bf16[384,1152]{1,0:T(8,128)(2,1)}, u32[]{:S(2)}, u32[]{:S(2)}) collective-permute-start(bf16[384,1152]{1,0:T(8,128)(2,1)} %get-tuple-element.299), channel_id=1, source_target_pairs={{0,4},{2,6},{4,0},{6,2},{8,12},{10,14},{12,8},{14,10},{16,20},{18,... | collective-permute-start | bytes 2654216 | tf_op jit(solution)/shard_map/ppermute | solution.py:294
  290.3 29.6 %collective-permute-start.28 = (bf16[256,1536]{1,0:T(8,128)(2,1)}, bf16[256,1536]{1,0:T(8,128)(2,1)S(1)}, u32[]{:S(2)}, u32[]{:S(2)}) collective-permute-start(bf16[256,1536]{1,0:T(8,128)(2,1)} %get-tuple-element.290), channel_id=1, source_target_pairs={{8,0},{10,2},{12,4},{14,6},{16,8},{18,10},{20,12},{22,14},{24,16},... | collective-permute-start | bytes 2359304 | tf_op jit(solution)/shard_map/ppermute | solution.py:304
  291.6 28.4 %collective-permute-start.29 = (bf16[256,1536]{1,0:T(8,128)(2,1)}, bf16[256,1536]{1,0:T(8,128)(2,1)}, u32[]{:S(2)}, u32[]{:S(2)}) collective-permute-start(bf16[256,1536]{1,0:T(8,128)(2,1)} %get-tuple-element.291), channel_id=1, source_target_pairs={{0,8},{2,10},{4,12},{6,14},{8,16},{10,18},{12,20},{14,22},{16,24},... | collective-permute-start | bytes 2359304 | tf_op jit(solution)/shard_map/ppermute | solution.py:299
  320.1 22.4 %collective-permute-start.37 = (bf16[384,1152]{1,0:T(8,128)(2,1)}, bf16[384,1152]{1,0:T(8,128)(2,1)}, u32[]{:S(2)}, u32[]{:S(2)}) collective-permute-start(bf16[384,1152]{1,0:T(8,128)(2,1)} %get-tuple-element.323), channel_id=1, source_target_pairs={{0,2},{2,0},{4,6},{6,4},{8,10},{10,8},{12,14},{14,12},{16,18},{18,... | collective-permute-start | bytes 2654216 | tf_op jit(solution)/shard_map/ppermute | solution.py:294
  375.2 130.7 %all-reduce.5.cloned.1.call-start = ((), (), s32[]{:S(2)}) async-start(), calls=%async_computation.2 | async-start | bytes 2818048 | tf_op jit(solution)/shard_map/psum | solution.py:1093
  441.1 64.8 %collective-permute-start.52 = (bf16[768,1152]{1,0:T(8,128)(2,1)}, bf16[768,1152]{1,0:T(8,128)(2,1)}, u32[]{:S(2)}, u32[]{:S(2)}) collective-permute-start(bf16[768,1152]{1,0:T(8,128)(2,1)} %pad_maximum_fusion.4), channel_id=1, source_target_pairs={{0,2},{2,0},{4,6},{6,4},{8,10},{10,8},{12,14},{14,12},{16,18},{18,... | collective-permute-start | bytes 5308424 | tf_op jit(solution)/shard_map/ppermute | solution.py:294
  442.1 63.8 %collective-permute-start.53 = (bf16[768,1152]{1,0:T(8,128)(2,1)}, bf16[768,1152]{1,0:T(8,128)(2,1)}, u32[]{:S(2)}, u32[]{:S(2)}) collective-permute-start(bf16[768,1152]{1,0:T(8,128)(2,1)} %pad_maximum_fusion.3), channel_id=1, source_target_pairs={{0,4},{2,6},{4,0},{6,2},{8,12},{10,14},{12,8},{14,10},{16,20},{18,... | collective-permute-start | bytes 5308424 | tf_op jit(solution)/shard_map/ppermute | solution.py:294
  525.6 31.9 %collective-permute-start.60 = (bf16[384,1024]{1,0:T(8,128)(2,1)S(1)}, bf16[384,1024]{1,0:T(8,128)(2,1)S(1)}, u32[]{:S(2)}, u32[]{:S(2)}) collective-permute-start(bf16[384,1024]{1,0:T(8,128)(2,1)S(1)} %maximum_select_fusion.3.refs_0_), channel_id=1, source_target_pairs={{0,2},{2,0},{4,6},{6,4},{8,10},{10,8},{12,14},{14,12},{16,18},{18,... | collective-permute-start | bytes 2359304 | tf_op jit(solution)/shard_map/ppermute | solution.py:294
  527.1 30.3 %collective-permute-start.61 = (bf16[384,1024]{1,0:T(8,128)(2,1)S(1)}, bf16[384,1024]{1,0:T(8,128)(2,1)}, u32[]{:S(2)}, u32[]{:S(2)}) collective-permute-start(bf16[384,1024]{1,0:T(8,128)(2,1)S(1)} %maximum_select_fusion.4.refs_2_), channel_id=1, source_target_pairs={{0,4},{2,6},{4,0},{6,2},{8,12},{10,14},{12,8},{14,10},{16,20},{18,... | collective-permute-start | bytes 2359304 | tf_op jit(solution)/shard_map/ppermute | solution.py:294
  527.7 28.4 %collective-permute-start.58 = (bf16[192,1536]{1,0:T(8,128)(2,1)S(1)}, bf16[192,1536]{1,0:T(8,128)(2,1)S(1)}, u32[]{:S(2)}, u32[]{:S(2)}) collective-permute-start(bf16[192,1536]{1,0:T(8,128)(2,1)S(1)} %maximum_select_fusion.5.refs_0_), channel_id=1, source_target_pairs={{0,2},{2,0},{4,6},{6,4},{8,10},{10,8},{12,14},{14,12},{16,18},{18,... | collective-permute-start | bytes 1769480 | tf_op jit(solution)/shard_map/ppermute | solution.py:294
  528.3 29.2 %collective-permute-start.59 = (bf16[192,1536]{1,0:T(8,128)(2,1)S(1)}, bf16[192,1536]{1,0:T(8,128)(2,1)}, u32[]{:S(2)}, u32[]{:S(2)}) collective-permute-start(bf16[192,1536]{1,0:T(8,128)(2,1)S(1)} %maximum_select_fusion.6.refs_2_), channel_id=1, source_target_pairs={{0,4},{2,6},{4,0},{6,2},{8,12},{10,14},{12,8},{14,10},{16,20},{18,... | collective-permute-start | bytes 1769480 | tf_op jit(solution)/shard_map/ppermute | solution.py:294
  (91 other events, 763.3 us)
Sparse Core Ops, SparseCore 0:
  375.3 59.0 reduce-scatter.1
  443.7 62.1 all-reduce.4

commit v4 on v3

--- a/solution.py
+++ b/solution.py
@@ -339,35 +339,52 @@
     return ordered(left, flip(left, 2), bit_y), ordered(right, flip(right, 1), bit_x)
 
 
-def plane_gather_second(halves, bit_x, bit_y):
-    left, right = halves
-    return left, flip(left, 1), right, flip(right, 2)
-
-
-def lay_out(bits, pieces, widths):
-    rows, columns = pieces[0].shape
+def plane_gather_second(left, right):
+    return flip(left, 1), flip(right, 2)
+
+
+def lay_out(bits, halves, widths, arrived, earlier=()):
+    rows, columns = halves[0].shape
+
     def kernel(bits_ref, *refs):
-        sources, results = refs[:4], refs[4:]
+        sources, refs = refs[:2], refs[2 + len(earlier) :]
+        results, (wide, semaphores) = refs[: len(widths)], refs[len(widths) :]
+        copies = []
         for side in range(2):
+            wide[side] = sources[side][...].astype(jnp.float32)
             bit = bits_ref[side]
-            for n in range(2):
-                value = sources[2 * side + n][...].astype(jnp.float32)
-                place = pl.multiple_of((2 * side + jnp.where(bit == n, 0, 1)) * rows, rows)
-                start = 0
-                for result, size in zip(results, widths, strict=True):
-                    result[pl.ds(place, rows), :] = value[:, start : start + size]
-                    start += size
-
+            place = pl.multiple_of((2 * side + (1 - bit if arrived else bit)) * rows, rows)
+            start = 0
+            for n, (result, size) in enumerate(zip(results, widths, strict=True)):
+                copies.append(
+                    pltpu.make_async_copy(
+                        wide.at[side, :, pl.ds(start, size)],
+                        result.at[pl.ds(place, rows), :],
+                        semaphores.at[side, n],
+                    )
+                )
+                copies[-1].start()
+                start += size
+        for copy in copies:
+            copy.wait()
+
+    anywhere = pl.BlockSpec(memory_space=pl.ANY)
     return pl.pallas_call(
         kernel,
         in_specs=[pl.BlockSpec(memory_space=pltpu.SMEM)]
-        + [pl.BlockSpec(memory_space=pltpu.VMEM)] * 4,
-        out_specs=[pl.BlockSpec(memory_space=pltpu.VMEM)] * len(widths),
+        + [pl.BlockSpec(memory_space=pltpu.VMEM)] * 2
+        + [anywhere] * len(earlier),
+        out_specs=[anywhere] * len(widths),
         out_shape=[jax.ShapeDtypeStruct((4 * rows, size), jnp.float32) for size in widths],
+        scratch_shapes=[
+            pltpu.VMEM((2, rows, columns), jnp.float32),
+            pltpu.SemaphoreType.DMA((2, len(widths))),
+        ],
+        input_output_aliases={3 + n: n for n in range(len(earlier))},
         compiler_params=pltpu.CompilerParams(vmem_limit_bytes=VMEM_BYTES),
         cost_estimate=small_cost(),
         name="lay_out",
-    )(bits, *pieces)
+    )(bits, *halves, *earlier)
 
 
 def rotary_tables(tokens):
@@ -456,6 +473,42 @@
         ),
         name="attention_forward",
     )(core, *operands)
+
+
+def output_gradient(places, mixed, own, other):
+    half, width = own.shape
+    local = mixed.shape[1]
+    piece = local // 4
+
+    def kernel(places_ref, mixed_ref, own_ref, other_ref, *refs):
+        pieces, (whole_ref, result) = refs[:4], refs[4:]
+        core = places_ref[0]
+        whole_ref[pl.ds(pl.multiple_of(core * half, half), half), :] = own_ref[...]
+        whole_ref[pl.ds(pl.multiple_of((1 - core) * half, half), half), :] = other_ref[...]
+        result[...] = contract_rows(mixed_ref[...], whole_ref[...]).astype(jnp.bfloat16)
+        give_pieces(places_ref, result, pieces, piece)
+
+    low = jax.ShapeDtypeStruct((piece, width), jnp.bfloat16)
+    results = pl.pallas_call(
+        kernel,
+        in_specs=[pl.BlockSpec(memory_space=pltpu.SMEM)]
+        + [pl.BlockSpec(memory_space=pltpu.VMEM)] * 3,
+        out_specs=[pl.BlockSpec(memory_space=pltpu.VMEM)] * 5,
+        out_shape=[low] * 4 + [jax.ShapeDtypeStruct((2 * half, width), jnp.bfloat16)],
+        scratch_shapes=[pltpu.VMEM((local, width), jnp.bfloat16)],
+        compiler_params=pltpu.CompilerParams(vmem_limit_bytes=VMEM_BYTES),
+        cost_estimate=small_cost(),
+        name="output_gradient",
+    )(places, mixed, own, other)
+    return results[:4], results[4]
+
+
+def give_pieces(places_ref, result, pieces, rows):
+    for side in range(2):
+        bit = places_ref[1 + side]
+        for n, place in enumerate((bit, 1 - bit)):
+            start = pl.multiple_of((2 * side + place) * rows, rows)
+            pieces[2 * side + n][...] = result[pl.ds(start, rows), :]
 
 
 def attention_backward(grad_attn, w_output, queries, keys, values, cosine, sine):
@@ -684,7 +737,7 @@
     counts = [group[0][0].shape[0] // (2 * half) for group in groups]
     total = sum(counts)
     flat = [array for group in groups for part in group for array in part[:2]]
-    block = 256
+    block = 512
 
     def kernel(*refs):
         terms, refs = refs[: len(flat)], refs[len(flat) :]
@@ -728,8 +781,8 @@
     )(*flat, weights)
 
 
-def load_copies(sequence, half, sources, x_all, dy_all, semaphores):
-    for n in range(4):
+def load_copies(sequence, half, sources, x_all, dy_all, semaphores, which=range(4)):
+    for n in which:
         target = x_all if n < 2 else dy_all
         yield pltpu.make_async_copy(
             sources[2 * sequence + n % 2].at[pl.ds((n // 2) * half, half), :],
@@ -755,8 +808,9 @@
 
         def row_copies(of_gradients):
             for s in range(total):
-                copies = list(load_copies(s, half, sources, x_all, dy_all, semaphores))
-                yield from copies[2:] if of_gradients else copies[:2]
+                yield from load_copies(
+                    s, half, sources, x_all, dy_all, semaphores, (2, 3) if of_gradients else (0, 1)
+                )
 
         def term_copies(e, of_products):
             place = 0
@@ -976,14 +1030,13 @@
     )
     third = (third, swap(third))
     far_pieces = [(piece, None) for piece in far_weights]
-    all_third, far_second, weights = expert_terms(
+    all_third, far_second, far_early, weights = expert_terms(
         number,
-        [([third], 0), ([second], 3)],
+        [([third], 0), ([second], 3), ([own, first], 3)],
         [[(near_weights, 0)], [(near_weights, 1)], [(near_weights, 2)], far_pieces],
         0,
         True,
     )
-    (far_early,) = expert_terms(number, [([own, first], 0)], [[(weights, 3)]], 3, False)
     to_far = expert_weight_grads(
         [third, second, own, first], [(*all_third, 3), (*far_second, 0), (*far_early, 0)], 1, hidden
     )
@@ -1055,10 +1108,11 @@
         grad_unit_two - unit_two * jnp.mean(grad_unit_two * unit_two, axis=-1, keepdims=True)
     )
     grad_attn_half = grad_middle.astype(jnp.bfloat16)
-    grad_attn = ordered(grad_attn_half, swap(grad_attn_half), core)
-    grad_output = contract_rows(mixed, grad_attn).astype(jnp.bfloat16)
-    grad_attn, grad_output = together((grad_attn, grad_output))
-    output_parts = plane_scatter_first(grad_output, bit_x, bit_y)
+    places = jnp.stack([core, bit_x, bit_y])
+    output_pieces, grad_attn = output_gradient(places, mixed, grad_attn_half, swap(grad_attn_half))
+    output_pieces, grad_attn = together((output_pieces, grad_attn))
+    left, to_x_side, right, to_y_side = output_pieces
+    output_parts = add_low(left, flip(to_x_side, 1)), add_low(right, flip(to_y_side, 2))
     grad_all_pre = attention_backward(grad_attn, w_output, queries, keys, values, cosine, sine)
     grad_all_pre, output_parts = together((grad_all_pre, output_parts))
     grad_projections = contract_rows(normed, grad_all_pre).astype(jnp.bfloat16)
@@ -1084,11 +1138,11 @@
     gains = (gains + swap(gains)).reshape(-1, grad_projections.shape[1])
     gain_rows = gains.shape[0]
     gains = jnp.pad(gains, ((0, 16 - gain_rows), (0, 0))).astype(jnp.bfloat16)
-    grad_in = ordered(grad_in_half, swap(grad_in_half), core)
+    grad_in_other = swap(grad_in_half)
     output_both = jnp.concatenate(output_parts, axis=0)
     projection_both = jnp.concatenate([*projection_parts, gains], axis=0)
-    projection_both, output_both, grad_in, moe_result, with_x, with_y = together(
-        (projection_both, output_both, grad_in, moe_result, with_x, with_y)
+    projection_both, output_both, moe_result, with_x, with_y = together(
+        (projection_both, output_both, moe_result, with_x, with_y)
     )
     output_both, projection_both = lax.psum(
         (output_both, projection_both), "expert", axis_index_groups=columns
@@ -1102,24 +1156,30 @@
     gains, projection_both = projection_both[-16:].astype(jnp.float32), projection_both[:-16]
     output_halves = plane_gather_first(*jnp.split(output_both, 2), bit_x, bit_y)
     projection_halves = plane_gather_first(*jnp.split(projection_both, 2), bit_x, bit_y)
-    output_halves, projection_halves, gains, then_x, then_y = together(
-        (output_halves, projection_halves, gains, then_x, then_y)
+    output_halves, projection_halves, gains, then_x, then_y, grad_in_half, grad_in_other = together(
+        (output_halves, projection_halves, gains, then_x, then_y, grad_in_half, grad_in_other)
     )
     arrived = (*from_x, *from_y, then_y, then_x)
     expert_grads = own_weight_grads(
         [own, first, second, third], [near_early, near_second, all_third], arrived, hidden
     )
-    output_pieces = plane_gather_second(output_halves, bit_x, bit_y)
-    projection_pieces = plane_gather_second(projection_halves, bit_x, bit_y)
-    expert_grads, output_pieces, projection_pieces, gains = together(
-        (expert_grads, output_pieces, projection_pieces, gains)
-    )
+    grad_in = ordered(grad_in_half, grad_in_other, core)
+    bits = jnp.stack([bit_x, bit_y])
+    projection_widths = [w.shape[1] for w in (w_query, w_key, w_value)]
+    output_early = lay_out(bits, output_halves, (width,), False)
+    projections_early = lay_out(bits, projection_halves, projection_widths, False)
+    output_pieces = plane_gather_second(*output_halves)
+    projection_pieces = plane_gather_second(*projection_halves)
+    early_ones = (output_early, projections_early, grad_in)
+    expert_grads, output_pieces, projection_pieces, gains, early_ones = together(
+        (expert_grads, output_pieces, projection_pieces, gains, early_ones)
+    )
+    output_early, projections_early, grad_in = early_ones
     gains = (gains + flip(gains, 1)) + (flip(gains, 2) + flip(gains, 3))
     gains_sum = gains[:gain_rows].reshape(2, width)
     grad_gate, grad_up, grad_down = expert_grads
-    bits = jnp.stack([bit_x, bit_y])
-    (output_sum,) = lay_out(bits, output_pieces, (width,))
-    projections = lay_out(bits, projection_pieces, [w.shape[1] for w in (w_query, w_key, w_value)])
+    projections = lay_out(bits, projection_pieces, projection_widths, True, projections_early)
+    (output_sum,) = lay_out(bits, output_pieces, (width,), True, output_early)
     return (
         block_out,
         grad_in,

time: 588 us -> 577 us (0.981)
  waiting for transfers between devices: 193 us -> 180 us
  Pallas kernels: 196 us -> 202 us
    ppermute x37, waiting for transfers between devices: 53.4 us -> 44.2 us  [flip(): return lax.ppermute(value, 'expert', [(i, i ^ bit) for i in range(places)])]
    pallas_call x2 -> x4, Pallas kernels: 8.93 us -> 11.9 us  [lay_out(): pl.pallas_call(kernel, in_specs=[pl.BlockSpec(memory_space=pltpu.SMEM)] +...]
    pallas_call x3 -> x2, Pallas kernels: 53.1 us -> 51.4 us  [expert_terms(): pl.pallas_call(kernel, grid=(number,), in_specs=[pl.BlockSpec(memory_spac...]
  transfers between devices with their start and end apart: 67 -> 67, of which waited for: 32 -> 31; matrix products, arithmetic and copies ran while one was open for 11% -> 12% of each run, Pallas kernels for 26% -> 27%
where the time goes in v4:
time: 577 us; the launch traced here: 568 us
  Pallas kernels  202 us (35%)
  waiting for transfers between devices  180 us (31%)
  starting transfers between devices  84.5 us (15%)
  other arithmetic  61.9 us (11%)
  local copies, waits for them, and re-layouts  19.8 us (3%)
  between operations  15.4 us (3%)
    psum x1, waiting for transfers between devices, planes_of_four(): lax.psum((output_both, projection_both), 'expert', axis_index_groups=colu...  55.1 us
    pallas_call x2, Pallas kernels, expert_terms(): pl.pallas_call(kernel, grid=(number,), in_specs=[pl.BlockSpec(memory_spac...  51.4 us
    pallas_call x2, Pallas kernels, expert_sums(): pl.pallas_call(kernel, grid=(width // block,), in_specs=[whole(*a.shape)...  45.9 us
    pallas_call x2, Pallas kernels, expert_weight_grads(): pl.pallas_call(kernel, in_specs=[anywhere] * (len(flat) + 2 * len(terms))...  44.2 us
    ppermute x37, waiting for transfers between devices, flip(): return lax.ppermute(value, 'expert', [(i, i ^ bit) for i in range(places)])  44.2 us
    ppermute x37, starting transfers between devices, flip(): return lax.ppermute(value, 'expert', [(i, i ^ bit) for i in range(places)])  41.9 us
    ppermute x7, waiting for transfers between devices, climb(): lax.ppermute(value, 'expert', [(i, i + 4) for i in range(places - 4)])  40.3 us
    ppermute x7, starting transfers between devices, climb(): lax.ppermute(value, 'expert', [(i, i + 4) for i in range(places - 4)])  30.8 us
  transfers between devices with their start and end apart: 67, of which 31 were waited for; matrix products, arithmetic and copies ran while one was open for 12% of the time, Pallas kernels for 27%

profile of v4, /device:TPU:0, one launch (start us, length us, event | category | flops | bytes accessed | tf_op | source)
XLA Modules:
  0.0 567.5 jit_solution(1760278434839607449)
XLA Ops:
  18.4 4.4 collective-permute-start.2
  24.6 12.1 %attention_forward.1 = (bf16[512,1536]{1,0:T(8,128)(2,1)}, bf16[512,768]{1,0:T(8,128)(2,1)}, bf16[512,128]{1,0:T(8,128)(2,1)}, bf16[512,128]{1,0:T(8,128)(2,1)},...) custom-call(s32[1]{0:T(128)} %bitcast.core_ref, bf16[512,1536]{1,0:T(8,128)(2,1)} %hidden_ref.1, ...), custom_call_target="tpu_custom_call" | custom-call | flops 1000 | bytes 1000 | tf_op jit(solution)/shard_map/attention_forward/pallas_call | solution.py:463
  39.4 5.0 collective-permute-done.3
  59.5 7.4 %collective-permute-done.5.refs_8_ = bf16[384,1152]{1,0:T(8,128)(2,1)} collective-permute-done((bf16[384,1152]{1,0:T(8,128)(2,1)}, bf16[384,1152]{1,0:T(8,128)(2,1)}, u32[]{:S(2)}, u32[]{:S(2)}) %collective-permute-start.5) | collective-permute-done | bytes 884768 | tf_op jit(solution)/shard_map/ppermute | solution.py:294
  70.0 5.0 collective-permute-done.8
  75.0 3.8 pad_maximum_fusion.5
  80.2 3.8 collective-permute-start.11
  90.2 25.9 %collective-permute-done.11 = bf16[528,1536]{1,0:T(8,128)(2,1)} collective-permute-done((bf16[528,1536]{1,0:T(8,128)(2,1)}, bf16[528,1536]{1,0:T(8,128)(2,1)}, u32[]{:S(2)}, u32[]{:S(2)}) %collective-permute-start.11) | collective-permute-done | bytes 1622048 | tf_op jit(solution)/shard_map/ppermute | solution.py:299
  116.1 5.3 collective-permute-done.12
  132.1 26.5 %expert_terms.2 = (bf16[1024,1152]{1,0:T(8,128)(2,1)}, bf16[1024,2304]{1,0:T(8,128)(2,1)}, bf16[512,1152]{1,0:T(8,128)(2,1)}, bf16[512,2304]{1,0:T(8,128)(2,1)}, bf16[3,1536,1152]{2,1,0:T(8,128)(2,1)}) custom-call(s32[1]{0:T(128)} %bitcast.9.expert_ref, bf16[528,1536]{1,0:T(8,128)(2,1)} %copy-done, ...), custom_call_target="tpu_custom_call" | custom-call | flops 1000 | bytes 1000 | tf_op jit(solution)/shard_map/expert_terms/pallas_call | solution.py:713
  158.7 5.2 collective-permute-done.17
  163.9 5.3 collective-permute-done.18
  171.5 3.5 collective-permute-done.20.refs_1_.refs_7_
  176.2 24.8 %expert_terms.3 = (bf16[512,1536]{1,0:T(8,128)(2,1)}, bf16[512,3072]{1,0:T(8,128)(2,1)}, bf16[512,384]{1,0:T(8,128)(2,1)}, bf16[512,768]{1,0:T(8,128)(2,1)}, bf1...) custom-call(s32[1]{0:T(128)} %bitcast.9.expert_ref, ...), custom_call_target="tpu_custom_call" | custom-call | flops 1000 | bytes 1000 | tf_op jit(solution)/shard_map/expert_terms/pallas_call | solution.py:713
  201.0 18.0 %expert_weight_grads.2 = (bf16[384,1152]{1,0:T(8,128)(2,1)}, bf16[384,1152]{1,0:T(8,128)(2,1)}, bf16[384,1152]{1,0:T(8,128)(2,1)}, bf16[384,1152]{1,0:T(8,128)(2,1)}) custom-call(bf16[528,1536]{1,0:T(8,128)(2,1)} %copy-done.5, bf16[528,1536]{1,0:T(8,128)(2,1)} %copy-done.9, bf16[528,1536]{1,0:T(8,128)(2,1)} %copy-done.2, bf16[528,1536]{1,0:T(8,128)(2,1)} %copy-done.4, ...), custom_call_target="tpu_custom_call" | custom-call | flops 1000 | bytes 1000 | tf_op jit(solution)/shard_map/expert_weight_grads/pallas_call | solution.py:855
  220.7 23.0 %expert_sums.2 = (bf16[2,256,1536]{2,1,0:T(8,128)(2,1)}, bf16[2,256,1536]{2,1,0:T(8,128)(2,1)}, bf16[2,256,1536]{2,1,0:T(8,128)(2,1)}, bf16[2,256,1536]{2,1,0:T(8,128)(2,1)}) custom-call(bf16[512,1536]{1,0:T(8,128)(2,1)} %get-tuple-element.281.refs_8_.refs_0_.refs_12_, bf16[512,3072]{1,0:T(8,128)(2,1)} %get-tuple-element.282.refs_9_.refs_1_.refs_13_, ...), custom_call_target="tpu_custom_call" | custom-call | flops 1000 | bytes 1000 | tf_op jit(solution)/shard_map/expert_sums/pallas_call | solution.py:771
  251.4 5.9 %collective-permute-start.25 = (bf16[256,1536]{1,0:T(8,128)(2,1)}, bf16[256,1536]{1,0:T(8,128)(2,1)}, u32[]{:S(2)}, u32[]{:S(2)}) collective-permute-start(bf16[256,1536]{1,0:T(8,128)(2,1)} %slice_bitcast_fusion.2), channel_id=1, source_target_pairs={{0,8},{2,10},{4,12},{6,14},{8,16},{10,18},{12,20},{14,22},{16,24},... | collective-permute-start | bytes 2359304 | tf_op jit(solution)/shard_map/ppermute | solution.py:299
  257.4 26.1 %expert_weight_grads.3 = (bf16[384,1152]{1,0:T(8,128)(2,1)}, bf16[384,1152]{1,0:T(8,128)(2,1)}, bf16[384,1152]{1,0:T(8,128)(2,1)}, bf16[384,1152]{1,0:T(8,128)(2...) custom-call(bf16[528,1536]{1,0:T(8,128)(2,1)} %copy-done, ...), custom_call_target="tpu_custom_call" | custom-call | flops 1000 | bytes 1000 | tf_op jit(solution)/shard_map/expert_weight_grads/pallas_call | solution.py:855
  290.1 5.5 collective-permute-start.29
  295.6 22.9 %expert_sums.3 = (bf16[2,256,1536]{2,1,0:T(8,128)(2,1)}, bf16[2,256,1536]{2,1,0:T(8,128)(2,1)}, bf16[2,256,1536]{2,1,0:T(8,128)(2,1)}, bf16[2,256,1536]{2,1,0:T(8,128)(2,1)}) custom-call(bf16[1024,1152]{1,0:T(8,128)(2,1)} %get-tuple-element.279.refs_8_.refs_0_, bf16[1024,2304]{1,0:T(8,128)(2,1)} %get-tuple-element.280.refs_9_.refs_1_, ...), custom_call_target="tpu_custom_call" | custom-call | flops 1000 | bytes 1000 | tf_op jit(solution)/shard_map/expert_sums/pallas_call | solution.py:771
  332.6 5.3 collective-permute-start.34
  341.8 9.2 %collective-permute-done.33 = bf16[256,1536]{1,0:T(8,128)(2,1)} collective-permute-done((bf16[256,1536]{1,0:T(8,128)(2,1)}, bf16[256,1536]{1,0:T(8,128)(2,1)}, u32[]{:S(2)}, u32[]{:S(2)}) %collective-permute-start.33) | collective-permute-done | bytes 786464 | tf_op jit(solution)/shard_map/ppermute | solution.py:304
  351.0 3.5 collective-permute-done.34
  362.8 5.1 output_gradient.1
  371.1 12.5 %attention_backward.1 = bf16[512,1024]{1,0:T(8,128)(2,1)} custom-call(bf16[512,1536]{1,0:T(8,128)(2,1)} %get-tuple-element.345.ga_ref, bf16[768,1536]{1,0:T(8,128)(2,1)} %wo_ref.3, bf16[512,768]{1,0:T(8,128)(2,1)} %get-tuple-element.346.query_ref, bf16[512,128]{1,0:T(8,128)(2,1)} %get-tuple-element.347.key_ref, ...), custom_call_target="tpu_custom_call" | custom-call | flops 1000 | bytes 1000 | tf_op jit(solution)/shard_map/attention_backward/pallas_call | solution.py:559
  402.2 12.2 %collective-permute-done.44 = bf16[384,1024]{1,0:T(8,128)(2,1)S(1)} collective-permute-done((bf16[384,1024]{1,0:T(8,128)(2,1)S(1)}, bf16[384,1024]{1,0:T(8,128)(2,1)S(1)}, u32[]{:S(2)}, u32[]{:S(2)}) %collective-permute-start.44) | collective-permute-done | bytes 786464 | tf_op jit(solution)/shard_map/ppermute | solution.py:294
  419.4 8.8 %collective-permute-done.48 = bf16[192,1024]{1,0:T(8,128)(2,1)} collective-permute-done((bf16[192,1024]{1,0:T(8,128)(2,1)}, bf16[192,1024]{1,0:T(8,128)(2,1)}, u32[]{:S(2)}, u32[]{:S(2)}) %collective-permute-start.48) | collective-permute-done | bytes 393248 | tf_op jit(solution)/shard_map/ppermute | solution.py:294
  441.9 55.1 %all-reduce.5.cloned.1.call-done = (bf16[192,1536]{1,0:T(8,128)(2,1)}, bf16[400,1024]{1,0:T(8,128)(2,1)}) async-done(((bf16[192,1536]{1,0:T(8,128)(2,1)}, bf16[400,1024]{1,0:T(8,128)(2,1)}), (bf16[192,1536]{1,0:T(8,128)(2,1)}, bf16[400,1024]{1,0:T(8,128)(2,1)})) %all-reduce.5.cloned.1.call-update) | async-done | bytes 1409040 | tf_op jit(solution)/shard_map/psum | solution.py:1147
  502.4 5.7 %collective-permute-done.53 = bf16[96,1536]{1,0:T(8,128)(2,1)S(1)} collective-permute-done((bf16[96,1536]{1,0:T(8,128)(2,1)S(1)}, bf16[96,1536]{1,0:T(8,128)(2,1)S(1)}, u32[]{:S(2)}, u32[]{:S(2)}) %collective-permute-start.53) | collective-permute-done | bytes 294944 | tf_op jit(solution)/shard_map/ppermute | solution.py:294
  510.5 4.6 collective-permute-done.55
  527.3 18.9 %own_weight_grads.1 = (f32[1,1536,384]{2,1,0:T(8,128)}, f32[1,1536,384]{2,1,0:T(8,128)}, f32[1,384,1536]{2,1,0:T(8,128)}) custom-call(bf16[528,1536]{1,0:T(8,128)(2,1)} %copy-done, bf16[528,1536]{1,0:T(8,128)(2,1)} %collective-permute-done.13.refs_1_.refs_5_, bf16[528,1536]{1,0:T(8,128)(2,1)} %copy-done.1, bf16[528,1536]{1,0:T(8,128)(2,1)} %copy-done.3, ...), custom_call_target="tpu_custom_call" | custom-call | flops 1000 | bytes 1000 | tf_op jit(solution)/shard_map/own_weight_grads/pallas_call | solution.py:920
  546.3 4.0 maximum_select_fusion
  (301 shorter events, 167.7 us)
Async XLA Ops:
  7.2 423.6 %reduce-scatter.2.cloned.1.call-start = ((), (), s32[]{:S(2)}) async-start(), calls=%async_computation.1 | async-start | bytes 3932160 | tf_op jit(solution)/shard_map/reduce_scatter | solution.py:1098
  11.6 32.9 %collective-permute-start = (bf16[384,1152]{1,0:T(8,128)(2,1)S(1)}, bf16[384,1152]{1,0:T(8,128)(2,1)}, u32[]{:S(2)}, u32[]{:S(2)}) collective-permute-start(bf16[384,1152]{1,0:T(8,128)(2,1)S(1)} %get-tuple-element.426), channel_id=1, source_target_pairs={{0,2},{2,0},{4,6},{6,4},{8,10},{10,8},{12,14},{14,12},{16,18},{18,... | collective-permute-start | bytes 2654216 | tf_op jit(solution)/shard_map/ppermute | solution.py:294
  14.5 29.9 %collective-permute-start.1 = (bf16[384,1152]{1,0:T(8,128)(2,1)S(1)}, bf16[384,1152]{1,0:T(8,128)(2,1)S(1)}, u32[]{:S(2)}, u32[]{:S(2)}) collective-permute-start(bf16[384,1152]{1,0:T(8,128)(2,1)S(1)} %get-tuple-element.426), channel_id=1, source_target_pairs={{0,4},{2,6},{4,0},{6,2},{8,12},{10,14},{12,8},{14,10},{16,20},{18,... | collective-permute-start | bytes 2654216 | tf_op jit(solution)/shard_map/ppermute | solution.py:294
  44.5 22.4 %collective-permute-start.5 = (bf16[384,1152]{1,0:T(8,128)(2,1)}, bf16[384,1152]{1,0:T(8,128)(2,1)}, u32[]{:S(2)}, u32[]{:S(2)}) collective-permute-start(bf16[384,1152]{1,0:T(8,128)(2,1)} %get-tuple-element.216), channel_id=1, source_target_pairs={{0,2},{2,0},{4,6},{6,4},{8,10},{10,8},{12,14},{14,12},{16,18},{18,... | collective-permute-start | bytes 2654216 | tf_op jit(solution)/shard_map/ppermute | solution.py:294
  56.1 30.8 %collective-permute-start.13 = (bf16[528,1536]{1,0:T(8,128)(2,1)S(1)}, bf16[528,1536]{1,0:T(8,128)(2,1)}, u32[]{:S(2)}, u32[]{:S(2)}) collective-permute-start(bf16[528,1536]{1,0:T(8,128)(2,1)S(1)} %pad_maximum_fusion.7.refs_0_.refs_4_), channel_id=1, source_target_pairs={{0,1},{1,0},{2,3},{3,2},{4,5},{5,4},{6,7},{7,6},{8,9},{9,8},{10,11... | collective-permute-start | bytes 4866056 | tf_op jit(solution)/shard_map/ppermute | solution.py:289
  78.8 42.6 %collective-permute-start.9 = (bf16[768,1152]{1,0:T(8,128)(2,1)}, bf16[768,1152]{1,0:T(8,128)(2,1)}, u32[]{:S(2)}, u32[]{:S(2)}) collective-permute-start(bf16[768,1152]{1,0:T(8,128)(2,1)} %slice.65), channel_id=1, source_target_pairs={{0,2},{2,0},{4,6},{6,4},{8,10},{10,8},{12,14},{14,12},{16,18},{18,... | collective-permute-start | bytes 5308424 | tf_op jit(solution)/shard_map/ppermute | solution.py:294
  79.3 42.1 %collective-permute-start.10 = (bf16[768,1152]{1,0:T(8,128)(2,1)}, bf16[768,1152]{1,0:T(8,128)(2,1)}, u32[]{:S(2)}, u32[]{:S(2)}) collective-permute-start(bf16[768,1152]{1,0:T(8,128)(2,1)} %slice.65), channel_id=1, source_target_pairs={{0,4},{2,6},{4,0},{6,2},{8,12},{10,14},{12,8},{14,10},{16,20},{18,... | collective-permute-start | bytes 5308424 | tf_op jit(solution)/shard_map/ppermute | solution.py:294
  80.2 35.9 %collective-permute-start.11 = (bf16[528,1536]{1,0:T(8,128)(2,1)}, bf16[528,1536]{1,0:T(8,128)(2,1)}, u32[]{:S(2)}, u32[]{:S(2)}) collective-permute-start(bf16[528,1536]{1,0:T(8,128)(2,1)} %get-tuple-element.225), channel_id=1, source_target_pairs={{0,8},{2,10},{4,12},{6,14},{8,16},{10,18},{12,20},{14,22},{16,24},... | collective-permute-start | bytes 4866056 | tf_op jit(solution)/shard_map/ppermute | solution.py:299
  84.0 37.4 %collective-permute-start.12 = (bf16[528,1536]{1,0:T(8,128)(2,1)}, bf16[528,1536]{1,0:T(8,128)(2,1)}, u32[]{:S(2)}, u32[]{:S(2)}) collective-permute-start(bf16[528,1536]{1,0:T(8,128)(2,1)} %get-tuple-element.226), channel_id=1, source_target_pairs={{8,0},{10,2},{12,4},{14,6},{16,8},{18,10},{20,12},{22,14},{24,16},... | collective-permute-start | bytes 4866056 | tf_op jit(solution)/shard_map/ppermute | solution.py:304
  86.9 34.5 %collective-permute-start.14 = (bf16[528,1536]{1,0:T(8,128)(2,1)S(1)}, bf16[528,1536]{1,0:T(8,128)(2,1)S(1)}, u32[]{:S(2)}, u32[]{:S(2)}) collective-permute-start(bf16[528,1536]{1,0:T(8,128)(2,1)S(1)} %broadcast_select_fusion.refs_2_.refs_6_), channel_id=1, source_target_pairs={{0,1},{1,0},{2,3},{3,2},{4,5},{5,4},{6,7},{7,6},{8,9},{9,8},{10,11... | collective-permute-start | bytes 4866056 | tf_op jit(solution)/shard_map/ppermute | solution.py:289
  121.4 47.7 %collective-permute-start.15 = (bf16[768,1152]{1,0:T(8,128)(2,1)}, bf16[768,1152]{1,0:T(8,128)(2,1)}, u32[]{:S(2)}, u32[]{:S(2)}) collective-permute-start(bf16[768,1152]{1,0:T(8,128)(2,1)} %pad_maximum_fusion.2), channel_id=1, source_target_pairs={{0,2},{2,0},{4,6},{6,4},{8,10},{10,8},{12,14},{14,12},{16,18},{18,... | collective-permute-start | bytes 5308424 | tf_op jit(solution)/shard_map/ppermute | solution.py:294
  122.9 46.3 %collective-permute-start.16 = (bf16[768,1152]{1,0:T(8,128)(2,1)}, bf16[768,1152]{1,0:T(8,128)(2,1)}, u32[]{:S(2)}, u32[]{:S(2)}) collective-permute-start(bf16[768,1152]{1,0:T(8,128)(2,1)} %collective-permute-done.9.refs_9_), channel_id=1, source_target_pairs={{0,4},{2,6},{4,0},{6,2},{8,12},{10,14},{12,8},{14,10},{16,20},{18,... | collective-permute-start | bytes 5308424 | tf_op jit(solution)/shard_map/ppermute | solution.py:294
  126.6 37.2 %collective-permute-start.17 = (bf16[528,1536]{1,0:T(8,128)(2,1)}, bf16[528,1536]{1,0:T(8,128)(2,1)}, u32[]{:S(2)}, u32[]{:S(2)}) collective-permute-start(bf16[528,1536]{1,0:T(8,128)(2,1)} %collective-permute-done.11), channel_id=1, source_target_pairs={{0,8},{2,10},{4,12},{6,14},{8,16},{10,18},{12,20},{14,22},{16,24},... | collective-permute-start | bytes 4866056 | tf_op jit(solution)/shard_map/ppermute | solution.py:299
  129.1 40.0 %collective-permute-start.18 = (bf16[528,1536]{1,0:T(8,128)(2,1)}, bf16[528,1536]{1,0:T(8,128)(2,1)}, u32[]{:S(2)}, u32[]{:S(2)}) collective-permute-start(bf16[528,1536]{1,0:T(8,128)(2,1)} %collective-permute-done.12), channel_id=1, source_target_pairs={{8,0},{10,2},{12,4},{14,6},{16,8},{18,10},{20,12},{22,14},{24,16},... | collective-permute-start | bytes 4866056 | tf_op jit(solution)/shard_map/ppermute | solution.py:304
  219.0 24.7 %collective-permute-start.21 = (bf16[384,1152]{1,0:T(8,128)(2,1)}, bf16[384,1152]{1,0:T(8,128)(2,1)S(1)}, u32[]{:S(2)}, u32[]{:S(2)}) collective-permute-start(bf16[384,1152]{1,0:T(8,128)(2,1)} %get-tuple-element.257), channel_id=1, source_target_pairs={{0,2},{2,0},{4,6},{6,4},{8,10},{10,8},{12,14},{14,12},{16,18},{18,... | collective-permute-start | bytes 2654216 | tf_op jit(solution)/shard_map/ppermute | solution.py:294
  220.2 23.5 %collective-permute-start.22 = (bf16[384,1152]{1,0:T(8,128)(2,1)}, bf16[384,1152]{1,0:T(8,128)(2,1)S(1)}, u32[]{:S(2)}, u32[]{:S(2)}) collective-permute-start(bf16[384,1152]{1,0:T(8,128)(2,1)} %get-tuple-element.259), channel_id=1, source_target_pairs={{0,4},{2,6},{4,0},{6,2},{8,12},{10,14},{12,8},{14,10},{16,20},{18,... | collective-permute-start | bytes 2654216 | tf_op jit(solution)/shard_map/ppermute | solution.py:294
  243.8 39.7 %collective-permute-start.26 = (bf16[384,1152]{1,0:T(8,128)(2,1)}, bf16[384,1152]{1,0:T(8,128)(2,1)S(1)}, u32[]{:S(2)}, u32[]{:S(2)}) collective-permute-start(bf16[384,1152]{1,0:T(8,128)(2,1)} %get-tuple-element.292), channel_id=1, source_target_pairs={{0,2},{2,0},{4,6},{6,4},{8,10},{10,8},{12,14},{14,12},{16,18},{18,... | collective-permute-start | bytes 2654216 | tf_op jit(solution)/shard_map/ppermute | solution.py:294
  244.8 38.7 %collective-permute-start.27 = (bf16[384,1152]{1,0:T(8,128)(2,1)}, bf16[384,1152]{1,0:T(8,128)(2,1)}, u32[]{:S(2)}, u32[]{:S(2)}) collective-permute-start(bf16[384,1152]{1,0:T(8,128)(2,1)} %get-tuple-element.294), channel_id=1, source_target_pairs={{0,4},{2,6},{4,0},{6,2},{8,12},{10,14},{12,8},{14,10},{16,20},{18,... | collective-permute-start | bytes 2654216 | tf_op jit(solution)/shard_map/ppermute | solution.py:294
  250.2 33.4 %collective-permute-start.24 = (bf16[256,1536]{1,0:T(8,128)(2,1)}, bf16[256,1536]{1,0:T(8,128)(2,1)S(1)}, u32[]{:S(2)}, u32[]{:S(2)}) collective-permute-start(bf16[256,1536]{1,0:T(8,128)(2,1)} %slice_bitcast_fusion.2), channel_id=1, source_target_pairs={{8,0},{10,2},{12,4},{14,6},{16,8},{18,10},{20,12},{22,14},{24,16},... | collective-permute-start | bytes 2359304 | tf_op jit(solution)/shard_map/ppermute | solution.py:304
  251.4 32.1 %collective-permute-start.25 = (bf16[256,1536]{1,0:T(8,128)(2,1)}, bf16[256,1536]{1,0:T(8,128)(2,1)}, u32[]{:S(2)}, u32[]{:S(2)}) collective-permute-start(bf16[256,1536]{1,0:T(8,128)(2,1)} %slice_bitcast_fusion.2), channel_id=1, source_target_pairs={{0,8},{2,10},{4,12},{6,14},{8,16},{10,18},{12,20},{14,22},{16,24},... | collective-permute-start | bytes 2359304 | tf_op jit(solution)/shard_map/ppermute | solution.py:299
  283.5 35.0 %collective-permute-start.30 = (bf16[384,1152]{1,0:T(8,128)(2,1)}, bf16[384,1152]{1,0:T(8,128)(2,1)}, u32[]{:S(2)}, u32[]{:S(2)}) collective-permute-start(bf16[384,1152]{1,0:T(8,128)(2,1)} %get-tuple-element.307), channel_id=1, source_target_pairs={{0,2},{2,0},{4,6},{6,4},{8,10},{10,8},{12,14},{14,12},{16,18},{18,... | collective-permute-start | bytes 2654216 | tf_op jit(solution)/shard_map/ppermute | solution.py:294
  284.6 34.0 %collective-permute-start.31 = (bf16[384,1152]{1,0:T(8,128)(2,1)}, bf16[384,1152]{1,0:T(8,128)(2,1)}, u32[]{:S(2)}, u32[]{:S(2)}) collective-permute-start(bf16[384,1152]{1,0:T(8,128)(2,1)} %get-tuple-element.308), channel_id=1, source_target_pairs={{0,4},{2,6},{4,0},{6,2},{8,12},{10,14},{12,8},{14,10},{16,20},{18,... | collective-permute-start | bytes 2654216 | tf_op jit(solution)/shard_map/ppermute | solution.py:294
  288.8 29.7 %collective-permute-start.28 = (bf16[256,1536]{1,0:T(8,128)(2,1)}, bf16[256,1536]{1,0:T(8,128)(2,1)S(1)}, u32[]{:S(2)}, u32[]{:S(2)}) collective-permute-start(bf16[256,1536]{1,0:T(8,128)(2,1)} %get-tuple-element.299), channel_id=1, source_target_pairs={{8,0},{10,2},{12,4},{14,6},{16,8},{18,10},{20,12},{22,14},{24,16},... | collective-permute-start | bytes 2359304 | tf_op jit(solution)/shard_map/ppermute | solution.py:304
  290.1 28.4 %collective-permute-start.29 = (bf16[256,1536]{1,0:T(8,128)(2,1)}, bf16[256,1536]{1,0:T(8,128)(2,1)}, u32[]{:S(2)}, u32[]{:S(2)}) collective-permute-start(bf16[256,1536]{1,0:T(8,128)(2,1)} %get-tuple-element.300), channel_id=1, source_target_pairs={{0,8},{2,10},{4,12},{6,14},{8,16},{10,18},{12,20},{14,22},{16,24},... | collective-permute-start | bytes 2359304 | tf_op jit(solution)/shard_map/ppermute | solution.py:299
  370.6 126.3 %all-reduce.5.cloned.1.call-start = ((), (), s32[]{:S(2)}) async-start(), calls=%async_computation.2 | async-start | bytes 2818048 | tf_op jit(solution)/shard_map/psum | solution.py:1147
  430.8 66.2 %collective-permute-start.51 = (bf16[768,1152]{1,0:T(8,128)(2,1)}, bf16[768,1152]{1,0:T(8,128)(2,1)}, u32[]{:S(2)}, u32[]{:S(2)}) collective-permute-start(bf16[768,1152]{1,0:T(8,128)(2,1)} %pad_maximum_fusion.4), channel_id=1, source_target_pairs={{0,2},{2,0},{4,6},{6,4},{8,10},{10,8},{12,14},{14,12},{16,18},{18,... | collective-permute-start | bytes 5308424 | tf_op jit(solution)/shard_map/ppermute | solution.py:294
  431.7 65.2 %collective-permute-start.52 = (bf16[768,1152]{1,0:T(8,128)(2,1)}, bf16[768,1152]{1,0:T(8,128)(2,1)}, u32[]{:S(2)}, u32[]{:S(2)}) collective-permute-start(bf16[768,1152]{1,0:T(8,128)(2,1)} %pad_maximum_fusion.3), channel_id=1, source_target_pairs={{0,4},{2,6},{4,0},{6,2},{8,12},{10,14},{12,8},{14,10},{16,20},{18,... | collective-permute-start | bytes 5308424 | tf_op jit(solution)/shard_map/ppermute | solution.py:294
  435.4 81.3 %collective-permute-start.57 = (f32[256,1536]{1,0:T(8,128)S(1)}, f32[256,1536]{1,0:T(8,128)}, u32[]{:S(2)}, u32[]{:S(2)}) collective-permute-start(f32[256,1536]{1,0:T(8,128)S(1)} %copy-done.12), channel_id=1, source_target_pairs={{0,1},{1,0},{2,3},{3,2},{4,5},{5,4},{6,7},{7,6},{8,9},{9,8},{10,11... | collective-permute-start | bytes 4718600 | tf_op jit(solution)/shard_map/ppermute | solution.py:289
  516.7 33.6 %collective-permute-start.60 = (bf16[384,1024]{1,0:T(8,128)(2,1)S(1)}, bf16[384,1024]{1,0:T(8,128)(2,1)}, u32[]{:S(2)}, u32[]{:S(2)}) collective-permute-start(bf16[384,1024]{1,0:T(8,128)(2,1)S(1)} %maximum_select_fusion.2.refs_0_), channel_id=1, source_target_pairs={{0,2},{2,0},{4,6},{6,4},{8,10},{10,8},{12,14},{14,12},{16,18},{18,... | collective-permute-start | bytes 2359304 | tf_op jit(solution)/shard_map/ppermute | solution.py:294
  518.2 32.1 %collective-permute-start.61 = (bf16[384,1024]{1,0:T(8,128)(2,1)S(1)}, bf16[384,1024]{1,0:T(8,128)(2,1)}, u32[]{:S(2)}, u32[]{:S(2)}) collective-permute-start(bf16[384,1024]{1,0:T(8,128)(2,1)S(1)} %maximum_select_fusion.3.refs_1_), channel_id=1, source_target_pairs={{0,4},{2,6},{4,0},{6,2},{8,12},{10,14},{12,8},{14,10},{16,20},{18,... | collective-permute-start | bytes 2359304 | tf_op jit(solution)/shard_map/ppermute | solution.py:294
  518.8 31.4 %collective-permute-start.58 = (bf16[192,1536]{1,0:T(8,128)(2,1)}, bf16[192,1536]{1,0:T(8,128)(2,1)}, u32[]{:S(2)}, u32[]{:S(2)}) collective-permute-start(bf16[192,1536]{1,0:T(8,128)(2,1)} %maximum_select_fusion.4.refs_0_), channel_id=1, source_target_pairs={{0,2},{2,0},{4,6},{6,4},{8,10},{10,8},{12,14},{14,12},{16,18},{18,... | collective-permute-start | bytes 1769480 | tf_op jit(solution)/shard_map/ppermute | solution.py:294
  519.3 30.9 %collective-permute-start.59 = (bf16[192,1536]{1,0:T(8,128)(2,1)}, bf16[192,1536]{1,0:T(8,128)(2,1)}, u32[]{:S(2)}, u32[]{:S(2)}) collective-permute-start(bf16[192,1536]{1,0:T(8,128)(2,1)} %maximum_select_fusion.5.refs_1_), channel_id=1, source_target_pairs={{0,4},{2,6},{4,0},{6,2},{8,12},{10,14},{12,8},{14,10},{16,20},{18,... | collective-permute-start | bytes 1769480 | tf_op jit(solution)/shard_map/ppermute | solution.py:294
  (84 other events, 678.2 us)
Sparse Core Ops, SparseCore 0:
  370.8 59.0 reduce-scatter.1
  433.4 63.4 all-reduce.4

commit v5 on v4

--- a/solution.py
+++ b/solution.py
@@ -294,14 +294,13 @@
     return lax.ppermute(value, "expert", [(i, i ^ bit) for i in range(places)])
 
 
-def climb(value):
+def outer(value):
+    return flip(value, 4)
+
+
+def inner(value):
     places = lax.axis_size("expert")
-    return lax.ppermute(value, "expert", [(i, i + 4) for i in range(places - 4)])
-
-
-def descend(value):
-    places = lax.axis_size("expert")
-    return lax.ppermute(value, "expert", [(i + 4, i) for i in range(places - 4)])
+    return lax.ppermute(value, "expert", [(i, i ^ 12 if i // 4 in (1, 2) else i) for i in range(places)])
 
 
 def part(value, index, count):
@@ -978,39 +977,39 @@
     dy_own = jnp.concatenate([out_grad_half, extra], axis=0)
 
     x0, y0 = flip(pieces[0], 1), flip(pieces[0], 2)
-    dy_up_one, dy_down_one = climb(dy_own), descend(dy_own)
+    dy_out_one, dy_in_one = outer(dy_own), inner(dy_own)
     cosine, sine = (jnp.asarray(table) for table in rotary_tables(tokens))
     normed, queries, keys, values, mixed, keep, send = attention_forward(
         core.reshape(1), hidden_in, attn_gain[None], w_query, w_key, w_value, w_output, cosine, sine
     )
-    send, x0, y0, dy_up_one, dy_down_one, piece = together(
-        (send, x0, y0, dy_up_one, dy_down_one, pieces[1])
+    send, x0, y0, dy_out_one, dy_in_one, piece = together(
+        (send, x0, y0, dy_out_one, dy_in_one, pieces[1])
     )
     x1, y1 = flip(piece, 1), flip(piece, 2)
     middle = keep + swap(send).astype(jnp.float32)
     scale_two = lax.rsqrt(jnp.mean(middle * middle, axis=-1, keepdims=True) + epsilon)
     unit_two = middle * scale_two
     rows_in = (unit_two * moe_gain).astype(jnp.bfloat16)
-    up_one, down_one = climb(rows_in), descend(rows_in)
-    x1, y1, up_one, down_one, dy_up_one, dy_down_one, piece = together(
-        (x1, y1, up_one, down_one, dy_up_one, dy_down_one, pieces[2])
-    )
-    up_one = jnp.concatenate([up_one, dy_up_one], axis=0)
-    down_one = jnp.concatenate([down_one, dy_down_one], axis=0)
-    up_one, down_one, piece = together((up_one, down_one, piece))
+    out_one, in_one = outer(rows_in), inner(rows_in)
+    x1, y1, out_one, in_one, dy_out_one, dy_in_one, piece = together(
+        (x1, y1, out_one, in_one, dy_out_one, dy_in_one, pieces[2])
+    )
+    out_one = jnp.concatenate([out_one, dy_out_one], axis=0)
+    in_one = jnp.concatenate([in_one, dy_in_one], axis=0)
+    out_one, in_one, piece = together((out_one, in_one, piece))
     x2, y2 = flip(piece, 1), flip(piece, 2)
-    up_two, down_two = climb(up_one), descend(down_one)
+    out_two, in_two = outer(in_one), inner(out_one)
     own = jnp.concatenate([rows_in, dy_own], axis=0)
-    first = jnp.where(plane == 0, down_one, up_one)
-    own, first = (own, swap(own)), (first, swap(first))
+    own, first = (own, swap(own)), (out_one, swap(out_one))
     far_from_y = jnp.concatenate([y0, y1], axis=0)
-    x2, y2, up_two, down_two, own, first, far_from_y = together(
-        (x2, y2, up_two, down_two, own, first, far_from_y)
+    x2, y2, out_two, in_two, own, first, far_from_y = together(
+        (x2, y2, out_two, in_two, own, first, far_from_y)
     )
     far_weights = [flip(far_from_y, 1), flip(x2, 2)]
-    up_three, down_three = climb(up_two), descend(down_two)
+    out_three = outer(in_two)
+    at_end = (plane == 0) | (plane == 3)
     number = expert.reshape(1)
-    second = jnp.where(plane == 0, down_two, jnp.where(plane == 3, up_two, down_one))
+    second = jnp.where(at_end, out_two, in_one)
     second = (second, swap(second))
     near_pieces = [[own_weights], [x0, x1, x2], [y0, y1, y2]]
     near_early, near_second, near_weights = expert_terms(
@@ -1020,14 +1019,10 @@
         0,
         True,
     )
-    far_weights, up_three, down_three, near_early, near_second, second = together(
-        (far_weights, up_three, down_three, near_early, near_second, second)
-    )
-    third = jnp.where(
-        plane == 0,
-        down_three,
-        jnp.where(plane == 1, down_two, jnp.where(plane == 2, up_two, up_three)),
-    )
+    far_weights, out_three, near_early, near_second, second = together(
+        (far_weights, out_three, near_early, near_second, second)
+    )
+    third = jnp.where(at_end, out_three, in_two)
     third = (third, swap(third))
     far_pieces = [(piece, None) for piece in far_weights]
     all_third, far_second, far_early, weights = expert_terms(
@@ -1050,7 +1045,7 @@
     back_late, near_early, all_third = together((back_late, near_early, all_third))
     second_back, third_back = back_late[1], back_late[0]
 
-    falling, rising = descend(third_back), climb(third_back)
+    arrived_out = outer(third_back)
     over_x, over_y = over_x + [flip(to_far[1], 1)], over_y + [flip(to_far[3], 2)]
     beside = expert_weight_grads(
         [own, first, second, third],
@@ -1058,27 +1053,24 @@
         2,
         hidden,
     )
-    falling, rising, beside, over_x, over_y, far_early = together(
-        (falling, rising, beside, over_x, over_y, far_early)
+    arrived_out, beside, over_x, over_y, far_early = together(
+        (arrived_out, beside, over_x, over_y, far_early)
     )
     to_x, to_y = beside[:4], beside[4:]
-    falling = add_low(jnp.where(plane == 3, second_back, third_back), falling)
-    rising = add_low(jnp.where(plane == 0, second_back, third_back), rising)
-    falling, rising, far_early = together((falling, rising, far_early))
-    falling, rising = descend(falling), climb(rising)
+    arrived_in, arrived_out = inner(add_low(third_back, arrived_out)), outer(second_back)
     from_x, from_y = [flip(to_x[0], 1)], [flip(to_y[2], 2)]
     early_sums = expert_sums([[(*near_early, 0), (*far_early, 3)]], weights, half)
-    falling, rising, early_sums, from_x, from_y, to_x, to_y = together(
-        (falling, rising, early_sums, from_x, from_y, to_x, to_y)
+    arrived_in, arrived_out, early_sums, from_x, from_y, to_x, to_y = together(
+        (arrived_in, arrived_out, early_sums, from_x, from_y, to_x, to_y)
     )
     back_early = add_low(early_sums[0], swap(early_sums[1]))
     own_back, first_back = back_early[0], back_early[1]
-    falling = add_low(first_back, falling)
-    rising = add_low(jnp.where(plane == 0, first_back, second_back), rising)
-    falling, rising, early_sums, late_sums, over_x = together(
-        (falling, rising, early_sums, late_sums, over_x)
-    )
-    falling, rising = descend(falling), climb(rising)
+    going_out = jnp.where(at_end, first_back, add_low(first_back, arrived_in))
+    going_in = add_low(second_back, arrived_out)
+    going_out, going_in, early_sums, late_sums, over_x = together(
+        (going_out, going_in, early_sums, late_sums, over_x)
+    )
+    arrived_out, arrived_in = outer(going_out), inner(going_in)
     from_x, from_y = from_x + [flip(to_x[1], 1)], from_y + [flip(to_y[3], 2)]
     with_x = jnp.concatenate([add_low(to_y[n], over_x[n]) for n in range(2)], axis=0)
     with_y = jnp.concatenate([add_low(to_x[2 + n], over_y[n]) for n in range(2)], axis=0)
@@ -1087,20 +1079,19 @@
     own_out, first_out, second_out, third_out = out_early[0], out_early[1], out_late[1], out_late[0]
     by_plane = [
         jnp.where(plane == 0, own_out, jnp.where(plane == 1, first_out, third_out)),
-        jnp.where(plane == 1, own_out, jnp.where(plane == 3, second_out, first_out)),
-        jnp.where(plane == 2, own_out, jnp.where(plane == 3, first_out, second_out)),
-        jnp.where(plane == 3, own_out, jnp.where(plane == 2, second_out, third_out)),
+        jnp.where(plane == 0, first_out, jnp.where(plane == 1, own_out, second_out)),
+        jnp.where(plane == 3, first_out, jnp.where(plane == 2, own_out, second_out)),
+        jnp.where(plane == 3, own_out, jnp.where(plane == 2, first_out, third_out)),
     ]
     results = jnp.concatenate(by_plane, axis=0)
-    falling, rising, results, from_x, from_y, with_x, with_y = together(
-        (falling, rising, results, from_x, from_y, with_x, with_y)
+    arrived_out, arrived_in, results, from_x, from_y, with_x, with_y = together(
+        (arrived_out, arrived_in, results, from_x, from_y, with_x, with_y)
     )
     moe_result = lax.psum_scatter(
         results, "expert", axis_index_groups=columns, scatter_dimension=0, tiled=True
     )
-    grad_rows = (
-        own_back.astype(jnp.float32) + falling.astype(jnp.float32) + rising.astype(jnp.float32)
-    )
+    grad_rows = own_back.astype(jnp.float32) + arrived_out.astype(jnp.float32)
+    grad_rows = jnp.where(at_end, grad_rows, grad_rows + arrived_in.astype(jnp.float32))
     grad_out = out_grad_half.astype(jnp.float32)
     grad_unit_two = grad_rows * moe_gain
     grad_moe_gain = jnp.sum(grad_rows * unit_two, axis=0)

time: 577 us -> 557 us (0.965)
  waiting for transfers between devices: 180 us -> 172 us
  other arithmetic: 61.9 us -> 55.2 us
  starting transfers between devices: 84.5 us -> 78.3 us
    ppermute x14 -> x5, waiting for transfers between devices: 70.1 us -> 0.01 us  [inner(): lax.ppermute(value, 'expert', [(i, i ^ 12 if i // 4 in (1, 2) else i) for...]
    ppermute x37 -> x44, waiting for transfers between devices: 44.2 us -> 99.4 us  [flip(): return lax.ppermute(value, 'expert', [(i, i ^ bit) for i in range(places)])]
    ppermute x14 -> x5, starting transfers between devices: 40.4 us -> 19.7 us  [inner(): lax.ppermute(value, 'expert', [(i, i ^ 12 if i // 4 in (1, 2) else i) for...]
    ppermute x37 -> x44, starting transfers between devices: 41.9 us -> 56.7 us  [flip(): return lax.ppermute(value, 'expert', [(i, i ^ bit) for i in range(places)])]
  transfers between devices with their start and end apart: 67 -> 65, of which waited for: 31 -> 26; matrix products, arithmetic and copies ran while one was open for 12% -> 10% of each run, Pallas kernels for 27% -> 28%
where the time goes in v5:
time: 557 us; the launch traced here: 549 us
  Pallas kernels  202 us (36%)
  waiting for transfers between devices  172 us (31%)
  starting transfers between devices  78.3 us (14%)
  other arithmetic  55.2 us (10%)
  local copies, waits for them, and re-layouts  22.2 us (4%)
  between operations  15.3 us (3%)
    ppermute x44, waiting for transfers between devices, flip(): return lax.ppermute(value, 'expert', [(i, i ^ bit) for i in range(places)])  99.4 us
    ppermute x44, starting transfers between devices, flip(): return lax.ppermute(value, 'expert', [(i, i ^ bit) for i in range(places)])  56.7 us
    psum x1, waiting for transfers between devices, planes_of_four(): lax.psum((output_both, projection_both), 'expert', axis_index_groups=colu...  55.3 us
    pallas_call x2, Pallas kernels, expert_terms(): pl.pallas_call(kernel, grid=(number,), in_specs=[pl.BlockSpec(memory_spac...  51.4 us
    pallas_call x2, Pallas kernels, expert_sums(): pl.pallas_call(kernel, grid=(width // block,), in_specs=[whole(*a.shape)...  46.2 us
    pallas_call x2, Pallas kernels, expert_weight_grads(): pl.pallas_call(kernel, in_specs=[anywhere] * (len(flat) + 2 * len(terms))...  44.1 us
    ppermute x5, starting transfers between devices, inner(): lax.ppermute(value, 'expert', [(i, i ^ 12 if i // 4 in (1, 2) else i) for...  19.7 us
    pallas_call x1, Pallas kernels, own_weight_grads(): pl.pallas_call(kernel, grid=(1,), in_specs=[pl.BlockSpec(memory_space=pl....  18.9 us
  transfers between devices with their start and end apart: 65, of which 26 were waited for; matrix products, arithmetic and copies ran while one was open for 10% of the time, Pallas kernels for 28%

profile of v5, /device:TPU:0, one launch (start us, length us, event | category | flops | bytes accessed | tf_op | source)
XLA Modules:
  0.0 548.7 jit_solution(12615226874948317607)
XLA Ops:
  21.5 12.1 %attention_forward.1 = (bf16[512,1536]{1,0:T(8,128)(2,1)}, bf16[512,768]{1,0:T(8,128)(2,1)}, bf16[512,128]{1,0:T(8,128)(2,1)}, bf16[512,128]{1,0:T(8,128)(2,1)},...) custom-call(s32[1]{0:T(128)} %bitcast.core_ref, bf16[512,1536]{1,0:T(8,128)(2,1)} %hidden_ref.1, ...), custom_call_target="tpu_custom_call" | custom-call | flops 1000 | bytes 1000 | tf_op jit(solution)/shard_map/attention_forward/pallas_call | solution.py:462
  33.5 3.9 collective-permute-done.2
  45.9 4.8 collective-permute-start.7
  52.8 14.0 %collective-permute-done.5.refs_8_ = bf16[384,1152]{1,0:T(8,128)(2,1)S(1)} collective-permute-done((bf16[384,1152]{1,0:T(8,128)(2,1)S(1)}, bf16[384,1152]{1,0:T(8,128)(2,1)S(1)}, u32[]{:S(2)}, u32[]{:S(2)}) %collective-permute-start.5) | collective-permute-done | bytes 884768 | tf_op jit(solution)/shard_map/ppermute | solution.py:294
  72.4 3.6 collective-permute-start.11
  82.3 28.0 %collective-permute-done.11 = bf16[528,1536]{1,0:T(8,128)(2,1)} collective-permute-done((bf16[528,1536]{1,0:T(8,128)(2,1)}, bf16[528,1536]{1,0:T(8,128)(2,1)}, u32[]{:S(2)}, u32[]{:S(2)}) %collective-permute-start.11) | collective-permute-done | bytes 1622048 | tf_op jit(solution)/shard_map/ppermute | solution.py:294
  114.7 3.5 collective-permute-start.17
  119.4 26.6 %expert_terms.2 = (bf16[1024,1152]{1,0:T(8,128)(2,1)}, bf16[1024,2304]{1,0:T(8,128)(2,1)}, bf16[512,1152]{1,0:T(8,128)(2,1)}, bf16[512,2304]{1,0:T(8,128)(2,1)}, bf16[3,1536,1152]{2,1,0:T(8,128)(2,1)}) custom-call(s32[1]{0:T(128)} %bitcast.9.expert_ref, bf16[528,1536]{1,0:T(8,128)(2,1)} %copy-done, bf16[528,1536]{1,0:T(8,128)(2,1)} %copy-done.3, ...), custom_call_target="tpu_custom_call" | custom-call | flops 1000 | bytes 1000 | tf_op jit(solution)/shard_map/expert_terms/pallas_call | solution.py:712
  145.9 8.6 %collective-permute-done.17 = bf16[528,1536]{1,0:T(8,128)(2,1)} collective-permute-done((bf16[528,1536]{1,0:T(8,128)(2,1)}, bf16[528,1536]{1,0:T(8,128)(2,1)}, u32[]{:S(2)}, u32[]{:S(2)}) %collective-permute-start.17) | collective-permute-done | bytes 1622048 | tf_op jit(solution)/shard_map/ppermute | solution.py:294
  156.2 3.5 collective-permute-done.19.refs_1_.refs_7_
  160.9 24.8 %expert_terms.3 = (bf16[512,1536]{1,0:T(8,128)(2,1)}, bf16[512,3072]{1,0:T(8,128)(2,1)}, bf16[512,384]{1,0:T(8,128)(2,1)}, bf16[512,768]{1,0:T(8,128)(2,1)}, bf1...) custom-call(s32[1]{0:T(128)} %bitcast.9.expert_ref, ...), custom_call_target="tpu_custom_call" | custom-call | flops 1000 | bytes 1000 | tf_op jit(solution)/shard_map/expert_terms/pallas_call | solution.py:712
  185.7 18.0 %expert_weight_grads.2 = (bf16[384,1152]{1,0:T(8,128)(2,1)}, bf16[384,1152]{1,0:T(8,128)(2,1)}, bf16[384,1152]{1,0:T(8,128)(2,1)}, bf16[384,1152]{1,0:T(8,128)(2,1)}) custom-call(bf16[528,1536]{1,0:T(8,128)(2,1)} %copy-done.6, bf16[528,1536]{1,0:T(8,128)(2,1)} %copy-done.11, bf16[528,1536]{1,0:T(8,128)(2,1)} %copy-done.2, bf16[528,1536]{1,0:T(8,128)(2,1)} %copy-done.5, ...), custom_call_target="tpu_custom_call" | custom-call | flops 1000 | bytes 1000 | tf_op jit(solution)/shard_map/expert_weight_grads/pallas_call | solution.py:854
  206.4 23.3 %expert_sums.2 = (bf16[2,256,1536]{2,1,0:T(8,128)(2,1)}, bf16[2,256,1536]{2,1,0:T(8,128)(2,1)}, bf16[2,256,1536]{2,1,0:T(8,128)(2,1)}, bf16[2,256,1536]{2,1,0:T(8,128)(2,1)}) custom-call(bf16[512,1536]{1,0:T(8,128)(2,1)} %get-tuple-element.274.refs_8_.refs_0_.refs_12_, bf16[512,3072]{1,0:T(8,128)(2,1)} %get-tuple-element.275.refs_9_.refs_1_.refs_13_, ...), custom_call_target="tpu_custom_call" | custom-call | flops 1000 | bytes 1000 | tf_op jit(solution)/shard_map/expert_sums/pallas_call | solution.py:770
  238.5 26.1 %expert_weight_grads.3 = (bf16[384,1152]{1,0:T(8,128)(2,1)}, bf16[384,1152]{1,0:T(8,128)(2,1)}, bf16[384,1152]{1,0:T(8,128)(2,1)}, bf16[384,1152]{1,0:T(8,128)(2...) custom-call(bf16[528,1536]{1,0:T(8,128)(2,1)} %copy-done, ...), custom_call_target="tpu_custom_call" | custom-call | flops 1000 | bytes 1000 | tf_op jit(solution)/shard_map/expert_weight_grads/pallas_call | solution.py:854
  268.4 7.4 %collective-permute-start.26 = (bf16[256,1536]{1,0:T(8,128)(2,1)}, bf16[256,1536]{1,0:T(8,128)(2,1)}, u32[]{:S(2)}, u32[]{:S(2)}) collective-permute-start(bf16[256,1536]{1,0:T(8,128)(2,1)} %add_convert_fusion.13), channel_id=1, source_target_pairs={{0,0},{2,2},{4,4},{6,6},{8,16},{10,18},{12,20},{14,22},{16,8},{18,... | collective-permute-start | bytes 2359304 | tf_op jit(solution)/shard_map/ppermute | solution.py:303
  275.8 22.9 %expert_sums.3 = (bf16[2,256,1536]{2,1,0:T(8,128)(2,1)}, bf16[2,256,1536]{2,1,0:T(8,128)(2,1)}, bf16[2,256,1536]{2,1,0:T(8,128)(2,1)}, bf16[2,256,1536]{2,1,0:T(8,128)(2,1)}) custom-call(bf16[1024,1152]{1,0:T(8,128)(2,1)} %get-tuple-element.272.refs_8_.refs_0_, bf16[1024,2304]{1,0:T(8,128)(2,1)} %get-tuple-element.273.refs_9_.refs_1_, ...), custom_call_target="tpu_custom_call" | custom-call | flops 1000 | bytes 1000 | tf_op jit(solution)/shard_map/expert_sums/pallas_call | solution.py:770
  314.3 7.5 %collective-permute-start.32 = (bf16[256,1536]{1,0:T(8,128)(2,1)}, bf16[256,1536]{1,0:T(8,128)(2,1)}, u32[]{:S(2)}, u32[]{:S(2)}) collective-permute-start(bf16[256,1536]{1,0:T(8,128)(2,1)} %add_convert_fusion.11), channel_id=1, source_target_pairs={{0,0},{2,2},{4,4},{6,6},{8,16},{10,18},{12,20},{14,22},{16,8},{18,... | collective-permute-start | bytes 2359304 | tf_op jit(solution)/shard_map/ppermute | solution.py:303
  324.8 6.4 %collective-permute-done.31 = bf16[256,1536]{1,0:T(8,128)(2,1)} collective-permute-done((bf16[256,1536]{1,0:T(8,128)(2,1)}, bf16[256,1536]{1,0:T(8,128)(2,1)}, u32[]{:S(2)}, u32[]{:S(2)}) %collective-permute-start.31) | collective-permute-done | bytes 786464 | tf_op jit(solution)/shard_map/ppermute | solution.py:294
  333.3 3.5 fusion.28
  339.4 5.1 output_gradient.1
  346.8 12.5 %attention_backward.1 = bf16[512,1024]{1,0:T(8,128)(2,1)} custom-call(bf16[512,1536]{1,0:T(8,128)(2,1)} %get-tuple-element.333.ga_ref, bf16[768,1536]{1,0:T(8,128)(2,1)} %wo_ref.3, bf16[512,768]{1,0:T(8,128)(2,1)} %get-tuple-element.334.query_ref, bf16[512,128]{1,0:T(8,128)(2,1)} %get-tuple-element.335.key_ref, ...), custom_call_target="tpu_custom_call" | custom-call | flops 1000 | bytes 1000 | tf_op jit(solution)/shard_map/attention_backward/pallas_call | solution.py:558
  378.3 12.2 %collective-permute-done.42 = bf16[384,1024]{1,0:T(8,128)(2,1)S(1)} collective-permute-done((bf16[384,1024]{1,0:T(8,128)(2,1)S(1)}, bf16[384,1024]{1,0:T(8,128)(2,1)S(1)}, u32[]{:S(2)}, u32[]{:S(2)}) %collective-permute-start.42) | collective-permute-done | bytes 786464 | tf_op jit(solution)/shard_map/ppermute | solution.py:294
  395.4 9.2 %collective-permute-done.46 = bf16[192,1024]{1,0:T(8,128)(2,1)} collective-permute-done((bf16[192,1024]{1,0:T(8,128)(2,1)}, bf16[192,1024]{1,0:T(8,128)(2,1)}, u32[]{:S(2)}, u32[]{:S(2)}) %collective-permute-start.46) | collective-permute-done | bytes 393248 | tf_op jit(solution)/shard_map/ppermute | solution.py:294
  407.0 4.0 reduce-scatter.2.cloned.1.call-done
  416.8 3.0 collective-permute-done.48
  422.8 55.3 %all-reduce.5.cloned.1.call-done = (bf16[192,1536]{1,0:T(8,128)(2,1)}, bf16[400,1024]{1,0:T(8,128)(2,1)}) async-done(((bf16[192,1536]{1,0:T(8,128)(2,1)}, bf16[400,1024]{1,0:T(8,128)(2,1)}), (bf16[192,1536]{1,0:T(8,128)(2,1)}, bf16[400,1024]{1,0:T(8,128)(2,1)})) %all-reduce.5.cloned.1.call-update) | async-done | bytes 1409040 | tf_op jit(solution)/shard_map/psum | solution.py:1138
  483.6 5.7 %collective-permute-done.51 = bf16[96,1536]{1,0:T(8,128)(2,1)S(1)} collective-permute-done((bf16[96,1536]{1,0:T(8,128)(2,1)S(1)}, bf16[96,1536]{1,0:T(8,128)(2,1)S(1)}, u32[]{:S(2)}, u32[]{:S(2)}) %collective-permute-start.51) | collective-permute-done | bytes 294944 | tf_op jit(solution)/shard_map/ppermute | solution.py:294
  491.7 4.6 collective-permute-done.53
  505.3 3.2 lay_out.5
  508.5 18.9 %own_weight_grads.1 = (f32[1,1536,384]{2,1,0:T(8,128)}, f32[1,1536,384]{2,1,0:T(8,128)}, f32[1,384,1536]{2,1,0:T(8,128)}) custom-call(bf16[528,1536]{1,0:T(8,128)(2,1)} %copy-done, bf16[528,1536]{1,0:T(8,128)(2,1)} %copy-done.3, bf16[528,1536]{1,0:T(8,128)(2,1)} %copy-done.1, bf16[528,1536]{1,0:T(8,128)(2,1)} %copy-done.4, bf16[528,1536]{1,0:T(8,128)(2,1)} %copy-done.2, ...), custom_call_target="tpu_custom_call" | custom-call | flops 1000 | bytes 1000 | tf_op jit(solution)/shard_map/own_weight_grads/pallas_call | solution.py:919
  527.4 4.0 maximum_select_fusion
  537.7 3.2 lay_out.6
  (297 shorter events, 144.0 us)
Async XLA Ops:
  7.2 403.8 %reduce-scatter.2.cloned.1.call-start = ((), (), s32[]{:S(2)}) async-start(), calls=%async_computation.1 | async-start | bytes 3932160 | tf_op jit(solution)/shard_map/reduce_scatter | solution.py:1090
  11.9 25.6 %collective-permute-start = (bf16[384,1152]{1,0:T(8,128)(2,1)}, bf16[384,1152]{1,0:T(8,128)(2,1)}, u32[]{:S(2)}, u32[]{:S(2)}) collective-permute-start(bf16[384,1152]{1,0:T(8,128)(2,1)} %get-tuple-element.414), channel_id=1, source_target_pairs={{0,2},{2,0},{4,6},{6,4},{8,10},{10,8},{12,14},{14,12},{16,18},{18,... | collective-permute-start | bytes 2654216 | tf_op jit(solution)/shard_map/ppermute | solution.py:294
  14.8 22.7 %collective-permute-start.1 = (bf16[384,1152]{1,0:T(8,128)(2,1)}, bf16[384,1152]{1,0:T(8,128)(2,1)S(1)}, u32[]{:S(2)}, u32[]{:S(2)}) collective-permute-start(bf16[384,1152]{1,0:T(8,128)(2,1)} %get-tuple-element.414), channel_id=1, source_target_pairs={{0,4},{2,6},{4,0},{6,2},{8,12},{10,14},{12,8},{14,10},{16,20},{18,... | collective-permute-start | bytes 2654216 | tf_op jit(solution)/shard_map/ppermute | solution.py:294
  43.3 35.0 %collective-permute-start.13 = (bf16[528,1536]{1,0:T(8,128)(2,1)S(1)}, bf16[528,1536]{1,0:T(8,128)(2,1)S(1)}, u32[]{:S(2)}, u32[]{:S(2)}) collective-permute-start(bf16[528,1536]{1,0:T(8,128)(2,1)S(1)} %pad_maximum_fusion.7.refs_0_.refs_4_), channel_id=1, source_target_pairs={{0,1},{1,0},{2,3},{3,2},{4,5},{5,4},{6,7},{7,6},{8,9},{9,8},{10,11... | collective-permute-start | bytes 4866056 | tf_op jit(solution)/shard_map/ppermute | solution.py:289
  45.9 22.0 %collective-permute-start.7 = (bf16[256,1536]{1,0:T(8,128)(2,1)S(1)}, bf16[256,1536]{1,0:T(8,128)(2,1)S(1)}, u32[]{:S(2)}, u32[]{:S(2)}) collective-permute-start(bf16[256,1536]{1,0:T(8,128)(2,1)S(1)} %multiply_convert_fusion), channel_id=1, source_target_pairs={{0,8},{2,10},{4,12},{6,14},{8,0},{10,2},{12,4},{14,6},{16,24},{18,... | collective-permute-start | bytes 2359304 | tf_op jit(solution)/shard_map/ppermute | solution.py:294
  69.4 40.9 %collective-permute-start.9 = (bf16[768,1152]{1,0:T(8,128)(2,1)}, bf16[768,1152]{1,0:T(8,128)(2,1)}, u32[]{:S(2)}, u32[]{:S(2)}) collective-permute-start(bf16[768,1152]{1,0:T(8,128)(2,1)} %slice.65), channel_id=1, source_target_pairs={{0,2},{2,0},{4,6},{6,4},{8,10},{10,8},{12,14},{14,12},{16,18},{18,... | collective-permute-start | bytes 5308424 | tf_op jit(solution)/shard_map/ppermute | solution.py:294
  70.9 39.5 %collective-permute-start.10 = (bf16[768,1152]{1,0:T(8,128)(2,1)}, bf16[768,1152]{1,0:T(8,128)(2,1)}, u32[]{:S(2)}, u32[]{:S(2)}) collective-permute-start(bf16[768,1152]{1,0:T(8,128)(2,1)} %slice.65), channel_id=1, source_target_pairs={{0,4},{2,6},{4,0},{6,2},{8,12},{10,14},{12,8},{14,10},{16,20},{18,... | collective-permute-start | bytes 5308424 | tf_op jit(solution)/shard_map/ppermute | solution.py:294
  72.4 37.9 %collective-permute-start.11 = (bf16[528,1536]{1,0:T(8,128)(2,1)}, bf16[528,1536]{1,0:T(8,128)(2,1)}, u32[]{:S(2)}, u32[]{:S(2)}) collective-permute-start(bf16[528,1536]{1,0:T(8,128)(2,1)} %get-tuple-element.219), channel_id=1, source_target_pairs={{0,8},{2,10},{4,12},{6,14},{8,0},{10,2},{12,4},{14,6},{16,24},{18,... | collective-permute-start | bytes 4866056 | tf_op jit(solution)/shard_map/ppermute | solution.py:294
  76.0 34.3 %collective-permute-start.12 = (bf16[528,1536]{1,0:T(8,128)(2,1)S(1)}, bf16[528,1536]{1,0:T(8,128)(2,1)}, u32[]{:S(2)}, u32[]{:S(2)}) collective-permute-start(bf16[528,1536]{1,0:T(8,128)(2,1)S(1)} %get-tuple-element.228.refs_2_.refs_6_), channel_id=1, source_target_pairs={{0,0},{2,2},{4,4},{6,6},{8,16},{10,18},{12,20},{14,22},{16,8},{18,... | collective-permute-start | bytes 4866056 | tf_op jit(solution)/shard_map/ppermute | solution.py:303
  79.5 30.8 %collective-permute-start.14 = (bf16[528,1536]{1,0:T(8,128)(2,1)S(1)}, bf16[528,1536]{1,0:T(8,128)(2,1)S(1)}, u32[]{:S(2)}, u32[]{:S(2)}) collective-permute-start(bf16[528,1536]{1,0:T(8,128)(2,1)S(1)} %get-tuple-element.228.refs_2_.refs_6_), channel_id=1, source_target_pairs={{0,1},{1,0},{2,3},{3,2},{4,5},{5,4},{6,7},{7,6},{8,9},{9,8},{10,11... | collective-permute-start | bytes 4866056 | tf_op jit(solution)/shard_map/ppermute | solution.py:289
  110.4 44.1 %collective-permute-start.15 = (bf16[768,1152]{1,0:T(8,128)(2,1)}, bf16[768,1152]{1,0:T(8,128)(2,1)}, u32[]{:S(2)}, u32[]{:S(2)}) collective-permute-start(bf16[768,1152]{1,0:T(8,128)(2,1)} %pad_maximum_fusion.2), channel_id=1, source_target_pairs={{0,2},{2,0},{4,6},{6,4},{8,10},{10,8},{12,14},{14,12},{16,18},{18,... | collective-permute-start | bytes 5308424 | tf_op jit(solution)/shard_map/ppermute | solution.py:294
  111.5 43.1 %collective-permute-start.16 = (bf16[768,1152]{1,0:T(8,128)(2,1)}, bf16[768,1152]{1,0:T(8,128)(2,1)}, u32[]{:S(2)}, u32[]{:S(2)}) collective-permute-start(bf16[768,1152]{1,0:T(8,128)(2,1)} %collective-permute-done.9.refs_9_), channel_id=1, source_target_pairs={{0,4},{2,6},{4,0},{6,2},{8,12},{10,14},{12,8},{14,10},{16,20},{18,... | collective-permute-start | bytes 5308424 | tf_op jit(solution)/shard_map/ppermute | solution.py:294
  114.7 39.8 %collective-permute-start.17 = (bf16[528,1536]{1,0:T(8,128)(2,1)}, bf16[528,1536]{1,0:T(8,128)(2,1)}, u32[]{:S(2)}, u32[]{:S(2)}) collective-permute-start(bf16[528,1536]{1,0:T(8,128)(2,1)} %collective-permute-done.12), channel_id=1, source_target_pairs={{0,8},{2,10},{4,12},{6,14},{8,0},{10,2},{12,4},{14,6},{16,24},{18,... | collective-permute-start | bytes 4866056 | tf_op jit(solution)/shard_map/ppermute | solution.py:294
  203.7 26.0 %collective-permute-start.20 = (bf16[384,1152]{1,0:T(8,128)(2,1)}, bf16[384,1152]{1,0:T(8,128)(2,1)S(1)}, u32[]{:S(2)}, u32[]{:S(2)}) collective-permute-start(bf16[384,1152]{1,0:T(8,128)(2,1)} %get-tuple-element.250), channel_id=1, source_target_pairs={{0,2},{2,0},{4,6},{6,4},{8,10},{10,8},{12,14},{14,12},{16,18},{18,... | collective-permute-start | bytes 2654216 | tf_op jit(solution)/shard_map/ppermute | solution.py:294
  204.9 24.9 %collective-permute-start.21 = (bf16[384,1152]{1,0:T(8,128)(2,1)}, bf16[384,1152]{1,0:T(8,128)(2,1)S(1)}, u32[]{:S(2)}, u32[]{:S(2)}) collective-permute-start(bf16[384,1152]{1,0:T(8,128)(2,1)} %get-tuple-element.252), channel_id=1, source_target_pairs={{0,4},{2,6},{4,0},{6,2},{8,12},{10,14},{12,8},{14,10},{16,20},{18,... | collective-permute-start | bytes 2654216 | tf_op jit(solution)/shard_map/ppermute | solution.py:294
  229.8 34.8 %collective-permute-start.24 = (bf16[384,1152]{1,0:T(8,128)(2,1)}, bf16[384,1152]{1,0:T(8,128)(2,1)S(1)}, u32[]{:S(2)}, u32[]{:S(2)}) collective-permute-start(bf16[384,1152]{1,0:T(8,128)(2,1)} %get-tuple-element.285), channel_id=1, source_target_pairs={{0,2},{2,0},{4,6},{6,4},{8,10},{10,8},{12,14},{14,12},{16,18},{18,... | collective-permute-start | bytes 2654216 | tf_op jit(solution)/shard_map/ppermute | solution.py:294
  230.8 33.9 %collective-permute-start.25 = (bf16[384,1152]{1,0:T(8,128)(2,1)}, bf16[384,1152]{1,0:T(8,128)(2,1)}, u32[]{:S(2)}, u32[]{:S(2)}) collective-permute-start(bf16[384,1152]{1,0:T(8,128)(2,1)} %get-tuple-element.287), channel_id=1, source_target_pairs={{0,4},{2,6},{4,0},{6,2},{8,12},{10,14},{12,8},{14,10},{16,20},{18,... | collective-permute-start | bytes 2654216 | tf_op jit(solution)/shard_map/ppermute | solution.py:294
  236.5 28.2 %collective-permute-start.23 = (bf16[256,1536]{1,0:T(8,128)(2,1)}, bf16[256,1536]{1,0:T(8,128)(2,1)}, u32[]{:S(2)}, u32[]{:S(2)}) collective-permute-start(bf16[256,1536]{1,0:T(8,128)(2,1)} %get-tuple-element.422), channel_id=1, source_target_pairs={{0,8},{2,10},{4,12},{6,14},{8,0},{10,2},{12,4},{14,6},{16,24},{18,... | collective-permute-start | bytes 2359304 | tf_op jit(solution)/shard_map/ppermute | solution.py:294
  238.2 60.5 %collective-permute-start.27 = (bf16[256,1536]{1,0:T(8,128)(2,1)}, bf16[256,1536]{1,0:T(8,128)(2,1)}, u32[]{:S(2)}, u32[]{:S(2)}) collective-permute-start(bf16[256,1536]{1,0:T(8,128)(2,1)} %get-tuple-element.421), channel_id=1, source_target_pairs={{0,8},{2,10},{4,12},{6,14},{8,0},{10,2},{12,4},{14,6},{16,24},{18,... | collective-permute-start | bytes 2359304 | tf_op jit(solution)/shard_map/ppermute | solution.py:294
  264.7 34.1 %collective-permute-start.28 = (bf16[384,1152]{1,0:T(8,128)(2,1)}, bf16[384,1152]{1,0:T(8,128)(2,1)}, u32[]{:S(2)}, u32[]{:S(2)}) collective-permute-start(bf16[384,1152]{1,0:T(8,128)(2,1)} %get-tuple-element.295), channel_id=1, source_target_pairs={{0,2},{2,0},{4,6},{6,4},{8,10},{10,8},{12,14},{14,12},{16,18},{18,... | collective-permute-start | bytes 2654216 | tf_op jit(solution)/shard_map/ppermute | solution.py:294
  265.7 33.1 %collective-permute-start.29 = (bf16[384,1152]{1,0:T(8,128)(2,1)}, bf16[384,1152]{1,0:T(8,128)(2,1)}, u32[]{:S(2)}, u32[]{:S(2)}) collective-permute-start(bf16[384,1152]{1,0:T(8,128)(2,1)} %get-tuple-element.296), channel_id=1, source_target_pairs={{0,4},{2,6},{4,0},{6,2},{8,12},{10,14},{12,8},{14,10},{16,20},{18,... | collective-permute-start | bytes 2654216 | tf_op jit(solution)/shard_map/ppermute | solution.py:294
  268.4 30.3 %collective-permute-start.26 = (bf16[256,1536]{1,0:T(8,128)(2,1)}, bf16[256,1536]{1,0:T(8,128)(2,1)}, u32[]{:S(2)}, u32[]{:S(2)}) collective-permute-start(bf16[256,1536]{1,0:T(8,128)(2,1)} %add_convert_fusion.13), channel_id=1, source_target_pairs={{0,0},{2,2},{4,4},{6,6},{8,16},{10,18},{12,20},{14,22},{16,8},{18,... | collective-permute-start | bytes 2359304 | tf_op jit(solution)/shard_map/ppermute | solution.py:303
  298.8 25.9 %collective-permute-start.35 = (bf16[384,1152]{1,0:T(8,128)(2,1)}, bf16[384,1152]{1,0:T(8,128)(2,1)}, u32[]{:S(2)}, u32[]{:S(2)}) collective-permute-start(bf16[384,1152]{1,0:T(8,128)(2,1)} %get-tuple-element.320), channel_id=1, source_target_pairs={{0,2},{2,0},{4,6},{6,4},{8,10},{10,8},{12,14},{14,12},{16,18},{18,... | collective-permute-start | bytes 2654216 | tf_op jit(solution)/shard_map/ppermute | solution.py:294
  300.0 24.7 %collective-permute-start.36 = (bf16[384,1152]{1,0:T(8,128)(2,1)}, bf16[384,1152]{1,0:T(8,128)(2,1)}, u32[]{:S(2)}, u32[]{:S(2)}) collective-permute-start(bf16[384,1152]{1,0:T(8,128)(2,1)} %get-tuple-element.322), channel_id=1, source_target_pairs={{0,4},{2,6},{4,0},{6,2},{8,12},{10,14},{12,8},{14,10},{16,20},{18,... | collective-permute-start | bytes 2654216 | tf_op jit(solution)/shard_map/ppermute | solution.py:294
  346.3 131.8 %all-reduce.5.cloned.1.call-start = ((), (), s32[]{:S(2)}) async-start(), calls=%async_computation.2 | async-start | bytes 2818048 | tf_op jit(solution)/shard_map/psum | solution.py:1138
  411.0 67.1 %collective-permute-start.49 = (bf16[768,1152]{1,0:T(8,128)(2,1)}, bf16[768,1152]{1,0:T(8,128)(2,1)}, u32[]{:S(2)}, u32[]{:S(2)}) collective-permute-start(bf16[768,1152]{1,0:T(8,128)(2,1)} %pad_maximum_fusion.4), channel_id=1, source_target_pairs={{0,2},{2,0},{4,6},{6,4},{8,10},{10,8},{12,14},{14,12},{16,18},{18,... | collective-permute-start | bytes 5308424 | tf_op jit(solution)/shard_map/ppermute | solution.py:294
  412.5 65.6 %collective-permute-start.50 = (bf16[768,1152]{1,0:T(8,128)(2,1)}, bf16[768,1152]{1,0:T(8,128)(2,1)}, u32[]{:S(2)}, u32[]{:S(2)}) collective-permute-start(bf16[768,1152]{1,0:T(8,128)(2,1)} %pad_maximum_fusion.3), channel_id=1, source_target_pairs={{0,4},{2,6},{4,0},{6,2},{8,12},{10,14},{12,8},{14,10},{16,20},{18,... | collective-permute-start | bytes 5308424 | tf_op jit(solution)/shard_map/ppermute | solution.py:294
  416.3 81.5 %collective-permute-start.55 = (f32[256,1536]{1,0:T(8,128)S(1)}, f32[256,1536]{1,0:T(8,128)}, u32[]{:S(2)}, u32[]{:S(2)}) collective-permute-start(f32[256,1536]{1,0:T(8,128)S(1)} %copy-done.14), channel_id=1, source_target_pairs={{0,1},{1,0},{2,3},{3,2},{4,5},{5,4},{6,7},{7,6},{8,9},{9,8},{10,11... | collective-permute-start | bytes 4718600 | tf_op jit(solution)/shard_map/ppermute | solution.py:289
  497.8 33.6 %collective-permute-start.58 = (bf16[384,1024]{1,0:T(8,128)(2,1)S(1)}, bf16[384,1024]{1,0:T(8,128)(2,1)}, u32[]{:S(2)}, u32[]{:S(2)}) collective-permute-start(bf16[384,1024]{1,0:T(8,128)(2,1)S(1)} %maximum_select_fusion.2.refs_0_), channel_id=1, source_target_pairs={{0,2},{2,0},{4,6},{6,4},{8,10},{10,8},{12,14},{14,12},{16,18},{18,... | collective-permute-start | bytes 2359304 | tf_op jit(solution)/shard_map/ppermute | solution.py:294
  499.4 32.0 %collective-permute-start.59 = (bf16[384,1024]{1,0:T(8,128)(2,1)S(1)}, bf16[384,1024]{1,0:T(8,128)(2,1)}, u32[]{:S(2)}, u32[]{:S(2)}) collective-permute-start(bf16[384,1024]{1,0:T(8,128)(2,1)S(1)} %maximum_select_fusion.3.refs_1_), channel_id=1, source_target_pairs={{0,4},{2,6},{4,0},{6,2},{8,12},{10,14},{12,8},{14,10},{16,20},{18,... | collective-permute-start | bytes 2359304 | tf_op jit(solution)/shard_map/ppermute | solution.py:294
  500.0 31.4 %collective-permute-start.56 = (bf16[192,1536]{1,0:T(8,128)(2,1)}, bf16[192,1536]{1,0:T(8,128)(2,1)}, u32[]{:S(2)}, u32[]{:S(2)}) collective-permute-start(bf16[192,1536]{1,0:T(8,128)(2,1)} %maximum_select_fusion.4.refs_0_), channel_id=1, source_target_pairs={{0,2},{2,0},{4,6},{6,4},{8,10},{10,8},{12,14},{14,12},{16,18},{18,... | collective-permute-start | bytes 1769480 | tf_op jit(solution)/shard_map/ppermute | solution.py:294
  500.5 30.9 %collective-permute-start.57 = (bf16[192,1536]{1,0:T(8,128)(2,1)}, bf16[192,1536]{1,0:T(8,128)(2,1)}, u32[]{:S(2)}, u32[]{:S(2)}) collective-permute-start(bf16[192,1536]{1,0:T(8,128)(2,1)} %maximum_select_fusion.5.refs_1_), channel_id=1, source_target_pairs={{0,4},{2,6},{4,0},{6,2},{8,12},{10,14},{12,8},{14,10},{16,20},{18,... | collective-permute-start | bytes 1769480 | tf_op jit(solution)/shard_map/ppermute | solution.py:294
  (82 other events, 613.6 us)
Sparse Core Ops, SparseCore 0:
  346.4 64.5 reduce-scatter.1
  414.6 63.4 all-reduce.4

commit v6 on v5

--- a/solution.py
+++ b/solution.py
@@ -472,6 +472,61 @@
         ),
         name="attention_forward",
     )(core, *operands)
+
+
+def second_norm(keep, arrived, gain):
+    def kernel(keep_ref, arrived_ref, gain_ref, middle_ref, rows_ref):
+        middle = keep_ref[...] + arrived_ref[...].astype(jnp.float32)
+        middle_ref[...] = middle
+        scale = lax.rsqrt(jnp.mean(middle * middle, axis=-1, keepdims=True) + epsilon)
+        rows_ref[...] = (middle * scale * gain_ref[...]).astype(jnp.bfloat16)
+
+    vmem = pl.BlockSpec(memory_space=pltpu.VMEM)
+    return pl.pallas_call(
+        kernel,
+        in_specs=[vmem] * 3,
+        out_specs=[vmem] * 2,
+        out_shape=[
+            jax.ShapeDtypeStruct(keep.shape, jnp.float32),
+            jax.ShapeDtypeStruct(keep.shape, jnp.bfloat16),
+        ],
+        compiler_params=pltpu.CompilerParams(vmem_limit_bytes=VMEM_BYTES),
+        cost_estimate=small_cost(),
+        name="second_norm",
+    )(keep, arrived, gain)
+
+
+def second_norm_gradient(at_end, own, arrived_out, arrived_in, middle, out_grad, gain):
+    def kernel(
+        at_end_ref, own_ref, out_ref, in_ref, middle_ref, dy_ref, gain_ref, grad_ref, low_ref, gain_grad_ref
+    ):
+        rows = own_ref[...].astype(jnp.float32) + out_ref[...].astype(jnp.float32)
+        rows = jnp.where(at_end_ref[0] != 0, rows, rows + in_ref[...].astype(jnp.float32))
+        middle = middle_ref[...]
+        scale = lax.rsqrt(jnp.mean(middle * middle, axis=-1, keepdims=True) + epsilon)
+        unit = middle * scale
+        gain_grad_ref[...] = jnp.sum(rows * unit, axis=0, keepdims=True)
+        scaled = rows * gain_ref[...]
+        grad = dy_ref[...].astype(jnp.float32) + scale * (
+            scaled - unit * jnp.mean(scaled * unit, axis=-1, keepdims=True)
+        )
+        grad_ref[...] = grad
+        low_ref[...] = grad.astype(jnp.bfloat16)
+
+    vmem = pl.BlockSpec(memory_space=pltpu.VMEM)
+    return pl.pallas_call(
+        kernel,
+        in_specs=[pl.BlockSpec(memory_space=pltpu.SMEM)] + [vmem] * 6,
+        out_specs=[vmem] * 3,
+        out_shape=[
+            jax.ShapeDtypeStruct(middle.shape, jnp.float32),
+            jax.ShapeDtypeStruct(middle.shape, jnp.bfloat16),
+            jax.ShapeDtypeStruct((1, middle.shape[1]), jnp.float32),
+        ],
+        compiler_params=pltpu.CompilerParams(vmem_limit_bytes=VMEM_BYTES),
+        cost_estimate=small_cost(),
+        name="second_norm_gradient",
+    )(at_end, own, arrived_out, arrived_in, middle, out_grad, gain)
 
 
 def output_gradient(places, mixed, own, other):
@@ -986,10 +1041,7 @@
         (send, x0, y0, dy_out_one, dy_in_one, pieces[1])
     )
     x1, y1 = flip(piece, 1), flip(piece, 2)
-    middle = keep + swap(send).astype(jnp.float32)
-    scale_two = lax.rsqrt(jnp.mean(middle * middle, axis=-1, keepdims=True) + epsilon)
-    unit_two = middle * scale_two
-    rows_in = (unit_two * moe_gain).astype(jnp.bfloat16)
+    middle, rows_in = second_norm(keep, swap(send), moe_gain[None])
     out_one, in_one = outer(rows_in), inner(rows_in)
     x1, y1, out_one, in_one, dy_out_one, dy_in_one, piece = together(
         (x1, y1, out_one, in_one, dy_out_one, dy_in_one, pieces[2])
@@ -1090,15 +1142,15 @@
     moe_result = lax.psum_scatter(
         results, "expert", axis_index_groups=columns, scatter_dimension=0, tiled=True
     )
-    grad_rows = own_back.astype(jnp.float32) + arrived_out.astype(jnp.float32)
-    grad_rows = jnp.where(at_end, grad_rows, grad_rows + arrived_in.astype(jnp.float32))
-    grad_out = out_grad_half.astype(jnp.float32)
-    grad_unit_two = grad_rows * moe_gain
-    grad_moe_gain = jnp.sum(grad_rows * unit_two, axis=0)
-    grad_middle = grad_out + scale_two * (
-        grad_unit_two - unit_two * jnp.mean(grad_unit_two * unit_two, axis=-1, keepdims=True)
-    )
-    grad_attn_half = grad_middle.astype(jnp.bfloat16)
+    grad_middle, grad_attn_half, grad_moe_gain = second_norm_gradient(
+        at_end.astype(jnp.int32).reshape(1),
+        own_back,
+        arrived_out,
+        arrived_in,
+        middle,
+        out_grad_half,
+        moe_gain[None],
+    )
     places = jnp.stack([core, bit_x, bit_y])
     output_pieces, grad_attn = output_gradient(places, mixed, grad_attn_half, swap(grad_attn_half))
     output_pieces, grad_attn = together((output_pieces, grad_attn))
@@ -1123,7 +1175,7 @@
     grad_in_half = grad_middle + scale_half * (
         grad_unit_one - unit_half * jnp.mean(grad_unit_one * unit_half, axis=-1, keepdims=True)
     )
-    gains = jnp.stack([grad_attn_gain, grad_moe_gain])
+    gains = jnp.stack([grad_attn_gain, grad_moe_gain[0]])
     projection_parts, gains, grad_in_half = together((projection_parts, gains, grad_in_half))
     projection_parts = plane_scatter_second(projection_parts, bit_x, bit_y)
     gains = (gains + swap(gains)).reshape(-1, grad_projections.shape[1])

time: 557 us -> 561 us (level)
  Pallas kernels: 202 us -> 211 us
  waiting for transfers between devices: 172 us -> 180 us
  other arithmetic: 55.2 us -> 47.4 us
    ppermute x44, waiting for transfers between devices: 99.4 us -> 108 us  [flip(): return lax.ppermute(value, 'expert', [(i, i ^ bit) for i in range(places)])]
    pallas_call x0 -> x2, Pallas kernels: none -> 8.22 us  [the longest x1 4.95 us: second_norm_gradient(): pl.pallas_call(kernel, in_specs=[pl.BlockSpec(memory_space=pltpu.SMEM)] +...]
    unnamed x99 -> x101, local copies, waits for them, and re-layouts: 13.5 us -> 9.82 us
  transfers between devices with their start and end apart: 65 -> 65, of which waited for: 26 -> 28; matrix products, arithmetic and copies ran while one was open for 10% -> 10% of each run, Pallas kernels for 28% -> 28%
where the time goes in v6:
time: 561 us; the launch traced here: 552 us
  Pallas kernels  211 us (38%)
  waiting for transfers between devices  180 us (32%)
  starting transfers between devices  73.7 us (13%)
  other arithmetic  47.4 us (8%)
  local copies, waits for them, and re-layouts  21.5 us (4%)
  between operations  15.5 us (3%)
    ppermute x44, waiting for transfers between devices, flip(): return lax.ppermute(value, 'expert', [(i, i ^ bit) for i in range(places)])  108 us
    ppermute x44, starting transfers between devices, flip(): return lax.ppermute(value, 'expert', [(i, i ^ bit) for i in range(places)])  57.4 us
    psum x1, waiting for transfers between devices, planes_of_four(): lax.psum((output_both, projection_both), 'expert', axis_index_groups=colu...  55.4 us
    pallas_call x2, Pallas kernels, expert_terms(): pl.pallas_call(kernel, grid=(number,), in_specs=[pl.BlockSpec(memory_spac...  51.4 us
    pallas_call x2, Pallas kernels, expert_sums(): pl.pallas_call(kernel, grid=(width // block,), in_specs=[whole(*a.shape)...  46.3 us
    pallas_call x2, Pallas kernels, expert_weight_grads(): pl.pallas_call(kernel, in_specs=[anywhere] * (len(flat) + 2 * len(terms))...  44.4 us
    pallas_call x1, Pallas kernels, own_weight_grads(): pl.pallas_call(kernel, grid=(1,), in_specs=[pl.BlockSpec(memory_space=pl....  19 us
    ppermute x5, starting transfers between devices, inner(): lax.ppermute(value, 'expert', [(i, i ^ 12 if i // 4 in (1, 2) else i) for...  14.2 us
  transfers between devices with their start and end apart: 65, of which 28 were waited for; matrix products, arithmetic and copies ran while one was open for 10% of the time, Pallas kernels for 28%

profile of v6, /device:TPU:0, one launch (start us, length us, event | category | flops | bytes accessed | tf_op | source)
XLA Modules:
  0.0 552.5 jit_solution(16854877578809248872)
XLA Ops:
  23.7 12.1 %attention_forward.1 = (bf16[512,1536]{1,0:T(8,128)(2,1)}, bf16[512,768]{1,0:T(8,128)(2,1)}, bf16[512,128]{1,0:T(8,128)(2,1)}, bf16[512,128]{1,0:T(8,128)(2,1)},...) custom-call(s32[1]{0:T(128)} %bitcast.core_ref, bf16[512,1536]{1,0:T(8,128)(2,1)} %hidden_ref.1, ...), custom_call_target="tpu_custom_call" | custom-call | flops 1000 | bytes 1000 | tf_op jit(solution)/shard_map/attention_forward/pallas_call | solution.py:462
  35.8 3.9 collective-permute-done.2
  42.5 3.3 second_norm.1
  48.2 4.8 collective-permute-start.7
  56.5 12.8 %collective-permute-done.4.refs_8_ = bf16[384,1152]{1,0:T(8,128)(2,1)S(1)} collective-permute-done((bf16[384,1152]{1,0:T(8,128)(2,1)S(1)}, bf16[384,1152]{1,0:T(8,128)(2,1)S(1)}, u32[]{:S(2)}, u32[]{:S(2)}) %collective-permute-start.4) | collective-permute-done | bytes 884768 | tf_op jit(solution)/shard_map/ppermute | solution.py:294
  74.9 3.6 collective-permute-start.11
  84.9 28.0 %collective-permute-done.11 = bf16[528,1536]{1,0:T(8,128)(2,1)} collective-permute-done((bf16[528,1536]{1,0:T(8,128)(2,1)}, bf16[528,1536]{1,0:T(8,128)(2,1)}, u32[]{:S(2)}, u32[]{:S(2)}) %collective-permute-start.11) | collective-permute-done | bytes 1622048 | tf_op jit(solution)/shard_map/ppermute | solution.py:294
  117.0 3.7 collective-permute-start.17
  121.9 26.6 %expert_terms.2 = (bf16[1024,1152]{1,0:T(8,128)(2,1)}, bf16[1024,2304]{1,0:T(8,128)(2,1)}, bf16[512,1152]{1,0:T(8,128)(2,1)}, bf16[512,2304]{1,0:T(8,128)(2,1)}, bf16[3,1536,1152]{2,1,0:T(8,128)(2,1)}) custom-call(s32[1]{0:T(128)} %bitcast.4.expert_ref, bf16[528,1536]{1,0:T(8,128)(2,1)} %copy-done.2, bf16[528,1536]{1,0:T(8,128)(2,1)} %copy-done.5, ...), custom_call_target="tpu_custom_call" | custom-call | flops 1000 | bytes 1000 | tf_op jit(solution)/shard_map/expert_terms/pallas_call | solution.py:767
  148.5 8.6 %collective-permute-done.17 = bf16[528,1536]{1,0:T(8,128)(2,1)} collective-permute-done((bf16[528,1536]{1,0:T(8,128)(2,1)}, bf16[528,1536]{1,0:T(8,128)(2,1)}, u32[]{:S(2)}, u32[]{:S(2)}) %collective-permute-start.17) | collective-permute-done | bytes 1622048 | tf_op jit(solution)/shard_map/ppermute | solution.py:294
  158.8 3.5 collective-permute-done.19.refs_1_.refs_7_
  163.4 24.8 %expert_terms.3 = (bf16[512,1536]{1,0:T(8,128)(2,1)}, bf16[512,3072]{1,0:T(8,128)(2,1)}, bf16[512,384]{1,0:T(8,128)(2,1)}, bf16[512,768]{1,0:T(8,128)(2,1)}, bf1...) custom-call(s32[1]{0:T(128)} %bitcast.4.expert_ref, ...), custom_call_target="tpu_custom_call" | custom-call | flops 1000 | bytes 1000 | tf_op jit(solution)/shard_map/expert_terms/pallas_call | solution.py:767
  188.3 18.1 %expert_weight_grads.2 = (bf16[384,1152]{1,0:T(8,128)(2,1)}, bf16[384,1152]{1,0:T(8,128)(2,1)}, bf16[384,1152]{1,0:T(8,128)(2,1)}, bf16[384,1152]{1,0:T(8,128)(2,1)}) custom-call(bf16[528,1536]{1,0:T(8,128)(2,1)} %copy-done.8, bf16[528,1536]{1,0:T(8,128)(2,1)} %copy-done.10, bf16[528,1536]{1,0:T(8,128)(2,1)} %copy-done.4, bf16[528,1536]{1,0:T(8,128)(2,1)} %copy-done.7, ...), custom_call_target="tpu_custom_call" | custom-call | flops 1000 | bytes 1000 | tf_op jit(solution)/shard_map/expert_weight_grads/pallas_call | solution.py:909
  208.5 23.4 %expert_sums.2 = (bf16[2,256,1536]{2,1,0:T(8,128)(2,1)}, bf16[2,256,1536]{2,1,0:T(8,128)(2,1)}, bf16[2,256,1536]{2,1,0:T(8,128)(2,1)}, bf16[2,256,1536]{2,1,0:T(8,128)(2,1)}) custom-call(bf16[512,1536]{1,0:T(8,128)(2,1)} %get-tuple-element.280.refs_8_.refs_0_.refs_12_, bf16[512,3072]{1,0:T(8,128)(2,1)} %get-tuple-element.281.refs_9_.refs_1_.refs_13_, ...), custom_call_target="tpu_custom_call" | custom-call | flops 1000 | bytes 1000 | tf_op jit(solution)/shard_map/expert_sums/pallas_call | solution.py:825
  240.6 26.3 %expert_weight_grads.3 = (bf16[384,1152]{1,0:T(8,128)(2,1)}, bf16[384,1152]{1,0:T(8,128)(2,1)}, bf16[384,1152]{1,0:T(8,128)(2,1)}, bf16[384,1152]{1,0:T(8,128)(2...) custom-call(bf16[528,1536]{1,0:T(8,128)(2,1)} %copy-done.2, ...), custom_call_target="tpu_custom_call" | custom-call | flops 1000 | bytes 1000 | tf_op jit(solution)/shard_map/expert_weight_grads/pallas_call | solution.py:909
  271.3 7.4 %collective-permute-start.26 = (bf16[256,1536]{1,0:T(8,128)(2,1)}, bf16[256,1536]{1,0:T(8,128)(2,1)}, u32[]{:S(2)}, u32[]{:S(2)}) collective-permute-start(bf16[256,1536]{1,0:T(8,128)(2,1)} %add_convert_fusion.13), channel_id=1, source_target_pairs={{0,0},{2,2},{4,4},{6,6},{8,16},{10,18},{12,20},{14,22},{16,8},{18,... | collective-permute-start | bytes 2359304 | tf_op jit(solution)/shard_map/ppermute | solution.py:303
  278.7 22.9 %expert_sums.3 = (bf16[2,256,1536]{2,1,0:T(8,128)(2,1)}, bf16[2,256,1536]{2,1,0:T(8,128)(2,1)}, bf16[2,256,1536]{2,1,0:T(8,128)(2,1)}, bf16[2,256,1536]{2,1,0:T(8,128)(2,1)}) custom-call(bf16[1024,1152]{1,0:T(8,128)(2,1)} %get-tuple-element.278.refs_8_.refs_0_, bf16[1024,2304]{1,0:T(8,128)(2,1)} %get-tuple-element.279.refs_9_.refs_1_, ...), custom_call_target="tpu_custom_call" | custom-call | flops 1000 | bytes 1000 | tf_op jit(solution)/shard_map/expert_sums/pallas_call | solution.py:825
  325.3 7.4 %collective-permute-done.31.out_ref = bf16[256,1536]{1,0:T(8,128)(2,1)S(1)} collective-permute-done((bf16[256,1536]{1,0:T(8,128)(2,1)S(1)}, bf16[256,1536]{1,0:T(8,128)(2,1)S(1)}, u32[]{:S(2)}, u32[]{:S(2)}) %collective-permute-start.31) | collective-permute-done | bytes 786464 | tf_op jit(solution)/shard_map/ppermute | solution.py:294
  333.8 5.0 second_norm_gradient.1
  342.2 5.1 output_gradient.1
  350.2 12.5 %attention_backward.1 = bf16[512,1024]{1,0:T(8,128)(2,1)} custom-call(bf16[512,1536]{1,0:T(8,128)(2,1)} %get-tuple-element.341.ga_ref, bf16[768,1536]{1,0:T(8,128)(2,1)} %wo_ref.3, bf16[512,768]{1,0:T(8,128)(2,1)} %get-tuple-element.342.query_ref, bf16[512,128]{1,0:T(8,128)(2,1)} %get-tuple-element.343.key_ref, ...), custom_call_target="tpu_custom_call" | custom-call | flops 1000 | bytes 1000 | tf_op jit(solution)/shard_map/attention_backward/pallas_call | solution.py:613
  378.5 13.7 %collective-permute-done.43 = bf16[384,1024]{1,0:T(8,128)(2,1)S(1)} collective-permute-done((bf16[384,1024]{1,0:T(8,128)(2,1)S(1)}, bf16[384,1024]{1,0:T(8,128)(2,1)S(1)}, u32[]{:S(2)}, u32[]{:S(2)}) %collective-permute-start.43) | collective-permute-done | bytes 786464 | tf_op jit(solution)/shard_map/ppermute | solution.py:294
  396.8 5.8 %collective-permute-done.45 = bf16[192,1024]{1,0:T(8,128)(2,1)S(1)} collective-permute-done((bf16[192,1024]{1,0:T(8,128)(2,1)}, bf16[192,1024]{1,0:T(8,128)(2,1)S(1)}, u32[]{:S(2)}, u32[]{:S(2)}) %collective-permute-start.45) | collective-permute-done | bytes 393248 | tf_op jit(solution)/shard_map/ppermute | solution.py:294
  402.7 5.3 collective-permute-done.46
  410.1 4.3 reduce-scatter.2.cloned.1.call-done
  426.2 55.4 %all-reduce.5.cloned.1.call-done = (bf16[192,1536]{1,0:T(8,128)(2,1)}, bf16[400,1024]{1,0:T(8,128)(2,1)}) async-done(((bf16[192,1536]{1,0:T(8,128)(2,1)}, bf16[400,1024]{1,0:T(8,128)(2,1)}), (bf16[192,1536]{1,0:T(8,128)(2,1)}, bf16[400,1024]{1,0:T(8,128)(2,1)})) %all-reduce.5.cloned.1.call-update) | async-done | bytes 1409040 | tf_op jit(solution)/shard_map/psum | solution.py:1190
  487.0 5.7 %collective-permute-done.52 = bf16[96,1536]{1,0:T(8,128)(2,1)S(1)} collective-permute-done((bf16[96,1536]{1,0:T(8,128)(2,1)S(1)}, bf16[96,1536]{1,0:T(8,128)(2,1)S(1)}, u32[]{:S(2)}, u32[]{:S(2)}) %collective-permute-start.52) | collective-permute-done | bytes 294944 | tf_op jit(solution)/shard_map/ppermute | solution.py:294
  495.3 4.5 collective-permute-done.54
  506.1 3.2 lay_out.5
  512.0 19.0 %own_weight_grads.1 = (f32[1,1536,384]{2,1,0:T(8,128)}, f32[1,1536,384]{2,1,0:T(8,128)}, f32[1,384,1536]{2,1,0:T(8,128)}) custom-call(bf16[528,1536]{1,0:T(8,128)(2,1)} %copy-done.2, bf16[528,1536]{1,0:T(8,128)(2,1)} %copy-done.5, bf16[528,1536]{1,0:T(8,128)(2,1)} %copy-done.3, bf16[528,1536]{1,0:T(8,128)(2,1)} %copy-done.6, bf16[528,1536]{1,0:T(8,128)(2,1)} %copy-done.4, ...), custom_call_target="tpu_custom_call" | custom-call | flops 1000 | bytes 1000 | tf_op jit(solution)/shard_map/own_weight_grads/pallas_call | solution.py:974
  531.1 4.0 maximum_select_fusion
  541.4 3.3 lay_out.6
  (296 shorter events, 149.0 us)
Async XLA Ops:
  7.2 407.3 %reduce-scatter.2.cloned.1.call-start = ((), (), s32[]{:S(2)}) async-start(), calls=%async_computation.1 | async-start | bytes 3932160 | tf_op jit(solution)/shard_map/reduce_scatter | solution.py:1142
  14.0 25.7 %collective-permute-start = (bf16[384,1152]{1,0:T(8,128)(2,1)}, bf16[384,1152]{1,0:T(8,128)(2,1)}, u32[]{:S(2)}, u32[]{:S(2)}) collective-permute-start(bf16[384,1152]{1,0:T(8,128)(2,1)} %get-tuple-element.418), channel_id=1, source_target_pairs={{0,2},{2,0},{4,6},{6,4},{8,10},{10,8},{12,14},{14,12},{16,18},{18,... | collective-permute-start | bytes 2654216 | tf_op jit(solution)/shard_map/ppermute | solution.py:294
  16.9 22.8 %collective-permute-start.1 = (bf16[384,1152]{1,0:T(8,128)(2,1)}, bf16[384,1152]{1,0:T(8,128)(2,1)S(1)}, u32[]{:S(2)}, u32[]{:S(2)}) collective-permute-start(bf16[384,1152]{1,0:T(8,128)(2,1)} %get-tuple-element.418), channel_id=1, source_target_pairs={{0,4},{2,6},{4,0},{6,2},{8,12},{10,14},{12,8},{14,10},{16,20},{18,... | collective-permute-start | bytes 2654216 | tf_op jit(solution)/shard_map/ppermute | solution.py:294
  47.1 33.7 %collective-permute-start.13 = (bf16[528,1536]{1,0:T(8,128)(2,1)S(1)}, bf16[528,1536]{1,0:T(8,128)(2,1)S(1)}, u32[]{:S(2)}, u32[]{:S(2)}) collective-permute-start(bf16[528,1536]{1,0:T(8,128)(2,1)S(1)} %pad_maximum_fusion.7.refs_0_.refs_4_), channel_id=1, source_target_pairs={{0,1},{1,0},{2,3},{3,2},{4,5},{5,4},{6,7},{7,6},{8,9},{9,8},{10,11... | collective-permute-start | bytes 4866056 | tf_op jit(solution)/shard_map/ppermute | solution.py:289
  48.2 22.3 %collective-permute-start.7 = (bf16[256,1536]{1,0:T(8,128)(2,1)S(1)}, bf16[256,1536]{1,0:T(8,128)(2,1)S(1)}, u32[]{:S(2)}, u32[]{:S(2)}) collective-permute-start(bf16[256,1536]{1,0:T(8,128)(2,1)S(1)} %copy-done.35), channel_id=1, source_target_pairs={{0,8},{2,10},{4,12},{6,14},{8,0},{10,2},{12,4},{14,6},{16,24},{18,... | collective-permute-start | bytes 2359304 | tf_op jit(solution)/shard_map/ppermute | solution.py:294
  71.9 41.0 %collective-permute-start.10 = (bf16[768,1152]{1,0:T(8,128)(2,1)}, bf16[768,1152]{1,0:T(8,128)(2,1)}, u32[]{:S(2)}, u32[]{:S(2)}) collective-permute-start(bf16[768,1152]{1,0:T(8,128)(2,1)} %slice.65), channel_id=1, source_target_pairs={{0,4},{2,6},{4,0},{6,2},{8,12},{10,14},{12,8},{14,10},{16,20},{18,... | collective-permute-start | bytes 5308424 | tf_op jit(solution)/shard_map/ppermute | solution.py:294
  73.4 39.8 %collective-permute-start.9 = (bf16[768,1152]{1,0:T(8,128)(2,1)}, bf16[768,1152]{1,0:T(8,128)(2,1)}, u32[]{:S(2)}, u32[]{:S(2)}) collective-permute-start(bf16[768,1152]{1,0:T(8,128)(2,1)} %slice.65), channel_id=1, source_target_pairs={{0,2},{2,0},{4,6},{6,4},{8,10},{10,8},{12,14},{14,12},{16,18},{18,... | collective-permute-start | bytes 5308424 | tf_op jit(solution)/shard_map/ppermute | solution.py:294
  74.9 38.0 %collective-permute-start.11 = (bf16[528,1536]{1,0:T(8,128)(2,1)}, bf16[528,1536]{1,0:T(8,128)(2,1)}, u32[]{:S(2)}, u32[]{:S(2)}) collective-permute-start(bf16[528,1536]{1,0:T(8,128)(2,1)} %get-tuple-element.225), channel_id=1, source_target_pairs={{0,8},{2,10},{4,12},{6,14},{8,0},{10,2},{12,4},{14,6},{16,24},{18,... | collective-permute-start | bytes 4866056 | tf_op jit(solution)/shard_map/ppermute | solution.py:294
  78.5 34.4 %collective-permute-start.12 = (bf16[528,1536]{1,0:T(8,128)(2,1)S(1)}, bf16[528,1536]{1,0:T(8,128)(2,1)}, u32[]{:S(2)}, u32[]{:S(2)}) collective-permute-start(bf16[528,1536]{1,0:T(8,128)(2,1)S(1)} %get-tuple-element.234.refs_2_.refs_6_), channel_id=1, source_target_pairs={{0,0},{2,2},{4,4},{6,6},{8,16},{10,18},{12,20},{14,22},{16,8},{18,... | collective-permute-start | bytes 4866056 | tf_op jit(solution)/shard_map/ppermute | solution.py:303
  82.1 30.8 %collective-permute-start.14 = (bf16[528,1536]{1,0:T(8,128)(2,1)S(1)}, bf16[528,1536]{1,0:T(8,128)(2,1)S(1)}, u32[]{:S(2)}, u32[]{:S(2)}) collective-permute-start(bf16[528,1536]{1,0:T(8,128)(2,1)S(1)} %get-tuple-element.234.refs_2_.refs_6_), channel_id=1, source_target_pairs={{0,1},{1,0},{2,3},{3,2},{4,5},{5,4},{6,7},{7,6},{8,9},{9,8},{10,11... | collective-permute-start | bytes 4866056 | tf_op jit(solution)/shard_map/ppermute | solution.py:289
  113.2 43.9 %collective-permute-start.15 = (bf16[768,1152]{1,0:T(8,128)(2,1)}, bf16[768,1152]{1,0:T(8,128)(2,1)}, u32[]{:S(2)}, u32[]{:S(2)}) collective-permute-start(bf16[768,1152]{1,0:T(8,128)(2,1)} %pad_maximum_fusion.2), channel_id=1, source_target_pairs={{0,2},{2,0},{4,6},{6,4},{8,10},{10,8},{12,14},{14,12},{16,18},{18,... | collective-permute-start | bytes 5308424 | tf_op jit(solution)/shard_map/ppermute | solution.py:294
  114.7 42.4 %collective-permute-start.16 = (bf16[768,1152]{1,0:T(8,128)(2,1)}, bf16[768,1152]{1,0:T(8,128)(2,1)}, u32[]{:S(2)}, u32[]{:S(2)}) collective-permute-start(bf16[768,1152]{1,0:T(8,128)(2,1)} %collective-permute-done.9.refs_9_), channel_id=1, source_target_pairs={{0,4},{2,6},{4,0},{6,2},{8,12},{10,14},{12,8},{14,10},{16,20},{18,... | collective-permute-start | bytes 5308424 | tf_op jit(solution)/shard_map/ppermute | solution.py:294
  117.0 40.0 %collective-permute-start.17 = (bf16[528,1536]{1,0:T(8,128)(2,1)}, bf16[528,1536]{1,0:T(8,128)(2,1)}, u32[]{:S(2)}, u32[]{:S(2)}) collective-permute-start(bf16[528,1536]{1,0:T(8,128)(2,1)} %collective-permute-done.12), channel_id=1, source_target_pairs={{0,8},{2,10},{4,12},{6,14},{8,0},{10,2},{12,4},{14,6},{16,24},{18,... | collective-permute-start | bytes 4866056 | tf_op jit(solution)/shard_map/ppermute | solution.py:294
  206.4 25.5 %collective-permute-start.20 = (bf16[384,1152]{1,0:T(8,128)(2,1)}, bf16[384,1152]{1,0:T(8,128)(2,1)S(1)}, u32[]{:S(2)}, u32[]{:S(2)}) collective-permute-start(bf16[384,1152]{1,0:T(8,128)(2,1)} %get-tuple-element.256), channel_id=1, source_target_pairs={{0,2},{2,0},{4,6},{6,4},{8,10},{10,8},{12,14},{14,12},{16,18},{18,... | collective-permute-start | bytes 2654216 | tf_op jit(solution)/shard_map/ppermute | solution.py:294
  208.0 23.9 %collective-permute-start.21 = (bf16[384,1152]{1,0:T(8,128)(2,1)}, bf16[384,1152]{1,0:T(8,128)(2,1)S(1)}, u32[]{:S(2)}, u32[]{:S(2)}) collective-permute-start(bf16[384,1152]{1,0:T(8,128)(2,1)} %get-tuple-element.258), channel_id=1, source_target_pairs={{0,4},{2,6},{4,0},{6,2},{8,12},{10,14},{12,8},{14,10},{16,20},{18,... | collective-permute-start | bytes 2654216 | tf_op jit(solution)/shard_map/ppermute | solution.py:294
  232.0 35.0 %collective-permute-start.24 = (bf16[384,1152]{1,0:T(8,128)(2,1)}, bf16[384,1152]{1,0:T(8,128)(2,1)S(1)}, u32[]{:S(2)}, u32[]{:S(2)}) collective-permute-start(bf16[384,1152]{1,0:T(8,128)(2,1)} %get-tuple-element.291), channel_id=1, source_target_pairs={{0,2},{2,0},{4,6},{6,4},{8,10},{10,8},{12,14},{14,12},{16,18},{18,... | collective-permute-start | bytes 2654216 | tf_op jit(solution)/shard_map/ppermute | solution.py:294
  233.3 33.7 %collective-permute-start.25 = (bf16[384,1152]{1,0:T(8,128)(2,1)}, bf16[384,1152]{1,0:T(8,128)(2,1)}, u32[]{:S(2)}, u32[]{:S(2)}) collective-permute-start(bf16[384,1152]{1,0:T(8,128)(2,1)} %get-tuple-element.293), channel_id=1, source_target_pairs={{0,4},{2,6},{4,0},{6,2},{8,12},{10,14},{12,8},{14,10},{16,20},{18,... | collective-permute-start | bytes 2654216 | tf_op jit(solution)/shard_map/ppermute | solution.py:294
  238.6 28.4 %collective-permute-start.23 = (bf16[256,1536]{1,0:T(8,128)(2,1)}, bf16[256,1536]{1,0:T(8,128)(2,1)}, u32[]{:S(2)}, u32[]{:S(2)}) collective-permute-start(bf16[256,1536]{1,0:T(8,128)(2,1)} %get-tuple-element.426), channel_id=1, source_target_pairs={{0,8},{2,10},{4,12},{6,14},{8,0},{10,2},{12,4},{14,6},{16,24},{18,... | collective-permute-start | bytes 2359304 | tf_op jit(solution)/shard_map/ppermute | solution.py:294
  240.4 61.2 %collective-permute-start.27 = (bf16[256,1536]{1,0:T(8,128)(2,1)}, bf16[256,1536]{1,0:T(8,128)(2,1)}, u32[]{:S(2)}, u32[]{:S(2)}) collective-permute-start(bf16[256,1536]{1,0:T(8,128)(2,1)} %get-tuple-element.425), channel_id=1, source_target_pairs={{0,8},{2,10},{4,12},{6,14},{8,0},{10,2},{12,4},{14,6},{16,24},{18,... | collective-permute-start | bytes 2359304 | tf_op jit(solution)/shard_map/ppermute | solution.py:294
  267.0 34.7 %collective-permute-start.28 = (bf16[384,1152]{1,0:T(8,128)(2,1)}, bf16[384,1152]{1,0:T(8,128)(2,1)}, u32[]{:S(2)}, u32[]{:S(2)}) collective-permute-start(bf16[384,1152]{1,0:T(8,128)(2,1)} %get-tuple-element.301), channel_id=1, source_target_pairs={{0,2},{2,0},{4,6},{6,4},{8,10},{10,8},{12,14},{14,12},{16,18},{18,... | collective-permute-start | bytes 2654216 | tf_op jit(solution)/shard_map/ppermute | solution.py:294
  268.3 33.4 %collective-permute-start.29 = (bf16[384,1152]{1,0:T(8,128)(2,1)}, bf16[384,1152]{1,0:T(8,128)(2,1)}, u32[]{:S(2)}, u32[]{:S(2)}) collective-permute-start(bf16[384,1152]{1,0:T(8,128)(2,1)} %get-tuple-element.302), channel_id=1, source_target_pairs={{0,4},{2,6},{4,0},{6,2},{8,12},{10,14},{12,8},{14,10},{16,20},{18,... | collective-permute-start | bytes 2654216 | tf_op jit(solution)/shard_map/ppermute | solution.py:294
  271.3 30.3 %collective-permute-start.26 = (bf16[256,1536]{1,0:T(8,128)(2,1)}, bf16[256,1536]{1,0:T(8,128)(2,1)}, u32[]{:S(2)}, u32[]{:S(2)}) collective-permute-start(bf16[256,1536]{1,0:T(8,128)(2,1)} %add_convert_fusion.13), channel_id=1, source_target_pairs={{0,0},{2,2},{4,4},{6,6},{8,16},{10,18},{12,20},{14,22},{16,8},{18,... | collective-permute-start | bytes 2359304 | tf_op jit(solution)/shard_map/ppermute | solution.py:303
  301.7 22.4 %collective-permute-start.35 = (bf16[384,1152]{1,0:T(8,128)(2,1)}, bf16[384,1152]{1,0:T(8,128)(2,1)}, u32[]{:S(2)}, u32[]{:S(2)}) collective-permute-start(bf16[384,1152]{1,0:T(8,128)(2,1)} %get-tuple-element.326), channel_id=1, source_target_pairs={{0,2},{2,0},{4,6},{6,4},{8,10},{10,8},{12,14},{14,12},{16,18},{18,... | collective-permute-start | bytes 2654216 | tf_op jit(solution)/shard_map/ppermute | solution.py:294
  303.3 22.0 %collective-permute-start.36 = (bf16[384,1152]{1,0:T(8,128)(2,1)}, bf16[384,1152]{1,0:T(8,128)(2,1)}, u32[]{:S(2)}, u32[]{:S(2)}) collective-permute-start(bf16[384,1152]{1,0:T(8,128)(2,1)} %get-tuple-element.328), channel_id=1, source_target_pairs={{0,4},{2,6},{4,0},{6,2},{8,12},{10,14},{12,8},{14,10},{16,20},{18,... | collective-permute-start | bytes 2654216 | tf_op jit(solution)/shard_map/ppermute | solution.py:294
  349.7 131.9 %all-reduce.5.cloned.1.call-start = ((), (), s32[]{:S(2)}) async-start(), calls=%async_computation.2 | async-start | bytes 2818048 | tf_op jit(solution)/shard_map/psum | solution.py:1190
  414.4 67.1 %collective-permute-start.49 = (bf16[768,1152]{1,0:T(8,128)(2,1)}, bf16[768,1152]{1,0:T(8,128)(2,1)}, u32[]{:S(2)}, u32[]{:S(2)}) collective-permute-start(bf16[768,1152]{1,0:T(8,128)(2,1)} %pad_maximum_fusion.4), channel_id=1, source_target_pairs={{0,2},{2,0},{4,6},{6,4},{8,10},{10,8},{12,14},{14,12},{16,18},{18,... | collective-permute-start | bytes 5308424 | tf_op jit(solution)/shard_map/ppermute | solution.py:294
  415.9 65.6 %collective-permute-start.50 = (bf16[768,1152]{1,0:T(8,128)(2,1)}, bf16[768,1152]{1,0:T(8,128)(2,1)}, u32[]{:S(2)}, u32[]{:S(2)}) collective-permute-start(bf16[768,1152]{1,0:T(8,128)(2,1)} %pad_maximum_fusion.3), channel_id=1, source_target_pairs={{0,4},{2,6},{4,0},{6,2},{8,12},{10,14},{12,8},{14,10},{16,20},{18,... | collective-permute-start | bytes 5308424 | tf_op jit(solution)/shard_map/ppermute | solution.py:294
  419.6 81.7 %collective-permute-start.55 = (f32[256,1536]{1,0:T(8,128)S(1)}, f32[256,1536]{1,0:T(8,128)}, u32[]{:S(2)}, u32[]{:S(2)}) collective-permute-start(f32[256,1536]{1,0:T(8,128)S(1)} %fusion.17), channel_id=1, source_target_pairs={{0,1},{1,0},{2,3},{3,2},{4,5},{5,4},{6,7},{7,6},{8,9},{9,8},{10,11... | collective-permute-start | bytes 4718600 | tf_op jit(solution)/shard_map/ppermute | solution.py:289
  501.4 33.7 %collective-permute-start.58 = (bf16[384,1024]{1,0:T(8,128)(2,1)S(1)}, bf16[384,1024]{1,0:T(8,128)(2,1)}, u32[]{:S(2)}, u32[]{:S(2)}) collective-permute-start(bf16[384,1024]{1,0:T(8,128)(2,1)S(1)} %maximum_select_fusion.2.refs_0_), channel_id=1, source_target_pairs={{0,2},{2,0},{4,6},{6,4},{8,10},{10,8},{12,14},{14,12},{16,18},{18,... | collective-permute-start | bytes 2359304 | tf_op jit(solution)/shard_map/ppermute | solution.py:294
  502.0 33.1 %collective-permute-start.59 = (bf16[384,1024]{1,0:T(8,128)(2,1)S(1)}, bf16[384,1024]{1,0:T(8,128)(2,1)}, u32[]{:S(2)}, u32[]{:S(2)}) collective-permute-start(bf16[384,1024]{1,0:T(8,128)(2,1)S(1)} %maximum_select_fusion.3.refs_1_), channel_id=1, source_target_pairs={{0,4},{2,6},{4,0},{6,2},{8,12},{10,14},{12,8},{14,10},{16,20},{18,... | collective-permute-start | bytes 2359304 | tf_op jit(solution)/shard_map/ppermute | solution.py:294
  503.5 31.6 %collective-permute-start.56 = (bf16[192,1536]{1,0:T(8,128)(2,1)}, bf16[192,1536]{1,0:T(8,128)(2,1)}, u32[]{:S(2)}, u32[]{:S(2)}) collective-permute-start(bf16[192,1536]{1,0:T(8,128)(2,1)} %maximum_select_fusion.4.refs_0_), channel_id=1, source_target_pairs={{0,2},{2,0},{4,6},{6,4},{8,10},{10,8},{12,14},{14,12},{16,18},{18,... | collective-permute-start | bytes 1769480 | tf_op jit(solution)/shard_map/ppermute | solution.py:294
  504.9 30.1 %collective-permute-start.57 = (bf16[192,1536]{1,0:T(8,128)(2,1)}, bf16[192,1536]{1,0:T(8,128)(2,1)}, u32[]{:S(2)}, u32[]{:S(2)}) collective-permute-start(bf16[192,1536]{1,0:T(8,128)(2,1)} %maximum_select_fusion.5.refs_1_), channel_id=1, source_target_pairs={{0,4},{2,6},{4,0},{6,2},{8,12},{10,14},{12,8},{14,10},{16,20},{18,... | collective-permute-start | bytes 1769480 | tf_op jit(solution)/shard_map/ppermute | solution.py:294
  (83 other events, 674.7 us)
Sparse Core Ops, SparseCore 0:
  349.8 64.5 reduce-scatter.1
  418.0 63.4 all-reduce.4
